TPU v7x, 128 devices: a whole 4x4x4 slice. The times are simulated.
128 devices in a mesh: gx: 4 (over y), gy: 8 (over x_hi, z), gz: 4 (over x_lo, core).
Axes of the slice: x: 4 (x_hi: 2, x_lo: 2; x = x_hi * 2 + x_lo), y: 4, z: 4, core: 2. Of those that a mesh axis runs over, the one named last changes fastest.
Arguments:
- volume: bfloat16 [16, 32, 128, 256], P(None, 'gx', 'gy', 'gz'), may hold values from -6 to 6
- w_fine: bfloat16 [27, 16, 16], replicated, may hold values from -0.3125 to 0.3125
- w_down: bfloat16 [27, 16, 32], replicated, may hold values from -0.875 to 0.875
- w_lift: bfloat16 [32, 256], replicated, may hold values from -2 to 2
- w_coarse: bfloat16 [27, 256, 256], replicated, may hold values from -0.078125 to 0.078125
- w_proj: bfloat16 [256, 32], replicated, may hold values from -0.75 to 0.75
- w_up: bfloat16 [27, 32, 16], replicated, may hold values from -0.21875 to 0.21875
- cotangent: bfloat16 [16, 32, 128, 256], P(None, 'gx', 'gy', 'gz'), may hold values from -6 to 6
Outputs:
- decoded: bfloat16 [16, 32, 128, 256], P(None, 'gx', 'gy', 'gz')
- grad_w_fine: float32 [27, 16, 16], replicated
- grad_w_down: float32 [27, 16, 32], replicated
- grad_w_lift: float32 [32, 256], replicated
- grad_w_coarse: float32 [27, 256, 256], replicated
- grad_w_proj: float32 [256, 32], replicated
- grad_w_up: float32 [27, 32, 16], replicated
All inputs are finite; a program needn't handle non-finite values.
Results may differ from a plain program's by a relative error of at most 0.035.
Values may be sent and summed in bfloat16 or wider, within the bound.
A program may use at most 128 MiB of HBM per device.

v0:
```python
import math

import jax
import jax.numpy as jnp
from jax import lax
from jax.sharding import PartitionSpec as P


def padded_2(cells, sides, width):
    for axis, dim in sides:
        count = lax.axis_size(axis)
        ends = count - 1
        head = lax.slice_in_dim(cells, 0, width, axis=dim)
        tail = lax.slice_in_dim(cells, cells.shape[dim] - width, cells.shape[dim], axis=dim)
        cells = jnp.concatenate(
            [
                lax.ppermute(tail, axis, [(i, (i + 1) % count) for i in range(ends)]),
                cells,
                lax.ppermute(head, axis, [((i + 1) % count, i) for i in range(ends)]),
            ],
            axis=dim,
        )
    return cells


def silu_grad(values):
    sig = jax.nn.sigmoid(values)
    return sig * (1.0 + values * (1.0 - sig))


def shifted(padded, row_tap, col_tap, depth_tap, extent, channels_last):
    if channels_last:
        return padded[
            row_tap : row_tap + extent[0],
            col_tap : col_tap + extent[1],
            depth_tap : depth_tap + extent[2],
            :,
        ]
    return padded[
        :,
        row_tap : row_tap + extent[0],
        col_tap : col_tap + extent[1],
        depth_tap : depth_tap + extent[2],
    ]


def apply_taps(padded, weight, extent, channels_last):
    result = None
    for row_tap in range(3):
        for col_tap in range(3):
            stacked = jnp.stack(
                [
                    shifted(padded, row_tap, col_tap, depth_tap, extent, channels_last)
                    for depth_tap in range(3)
                ]
            )
            first = 9 * row_tap + 3 * col_tap
            tap_weights = weight[first : first + 3]
            if channels_last:
                product = jnp.einsum(
                    "kxyzc,kco->xyzo", stacked, tap_weights, preferred_element_type=jnp.float32
                )
            else:
                product = jnp.einsum(
                    "kcxyz,kco->oxyz", stacked, tap_weights, preferred_element_type=jnp.float32
                )
            result = product if result is None else result + product
    return result


def gather_taps(padded, grad, extent, channels_last):
    pieces = []
    for row_tap in range(3):
        for col_tap in range(3):
            stacked = jnp.stack(
                [
                    shifted(padded, row_tap, col_tap, depth_tap, extent, channels_last)
                    for depth_tap in range(3)
                ]
            )
            if channels_last:
                pieces.append(
                    jnp.einsum("kxyzc,xyzo->kco", stacked, grad, preferred_element_type=jnp.float32)
                )
            else:
                pieces.append(
                    jnp.einsum("kcxyz,oxyz->kco", stacked, grad, preferred_element_type=jnp.float32)
                )
    return jnp.concatenate(pieces, axis=0)


def flipped(weight):
    return jnp.transpose(jnp.flip(weight, 0), (0, 2, 1))


def pool_sum(values, factor):
    chans, depth, height, width = values.shape
    shaped = values.astype(jnp.float32).reshape(
        chans, depth // factor, factor, height // factor, factor, width // factor, factor
    )
    return jnp.sum(shaped, axis=(2, 4, 6))


def pool_mean(values, factor):
    return pool_sum(values, factor) / float(factor**3)


def upsample(values, factor):
    return jnp.repeat(
        jnp.repeat(jnp.repeat(values, factor, axis=1), factor, axis=2), factor, axis=3
    )


def fine_border(values):
    return padded_2(values, (("gx", 1), ("gy", 2), ("gz", 3)), 1)


def mid_border(values):
    return padded_2(values, (("gx", 1), ("gy", 2), ("gz", 3)), 1)


def back_border(values):
    return padded_2(values, (("gx", 1), ("gy", 2), ("gz", 3)), 1)


def column_border(values):
    column = lax.all_gather(values, "gy", axis=1, tiled=True)
    edged = padded_2(column, (("gx", 0), ("gz", 2)), 1)
    return jnp.pad(edged, ((0, 0), (1, 1), (0, 0), (0, 0)))


def shards(volume, w_fine, w_down, w_lift, w_coarse, w_proj, w_up, cotangent):
    fine_extent = volume.shape[1:]
    total_cells = (
        fine_extent[0]
        * fine_extent[1]
        * fine_extent[2]
        * lax.axis_size("gx")
        * lax.axis_size("gy")
        * lax.axis_size("gz")
    )
    padded_fine = fine_border(volume)
    pre_fine = apply_taps(padded_fine, w_fine, fine_extent, False)
    act_fine = jax.nn.silu(pre_fine).astype(jnp.bfloat16)
    pool_mid = pool_mean(act_fine, 2).astype(jnp.bfloat16)
    mid_extent = pool_mid.shape[1:]
    padded_pool = mid_border(pool_mid)
    pre_mid = apply_taps(padded_pool, w_down, mid_extent, False)
    act_mid = jax.nn.silu(pre_mid).astype(jnp.bfloat16)
    pool_coarse = pool_mean(act_mid, 4).astype(jnp.bfloat16)
    pre_lift = jnp.einsum("cxyz,cd->xyzd", pool_coarse, w_lift, preferred_element_type=jnp.float32)
    act_lift = jax.nn.silu(pre_lift).astype(jnp.bfloat16)
    coarse_extent = act_lift.shape[:3]
    own_height = coarse_extent[1]
    column_extent = (coarse_extent[0], own_height * lax.axis_size("gy"), coarse_extent[2])
    row_start = lax.axis_index("gy") * own_height
    padded_lift = column_border(act_lift)
    pre_coarse = lax.dynamic_slice_in_dim(
        apply_taps(padded_lift, w_coarse, column_extent, True), row_start, own_height, 1
    )
    act_coarse = jax.nn.silu(pre_coarse).astype(jnp.bfloat16)
    coarse_out = jnp.einsum("xyzd,dc->cxyz", act_coarse, w_proj, preferred_element_type=jnp.float32)
    joined = (act_mid.astype(jnp.float32) + upsample(coarse_out, 4)).astype(jnp.bfloat16)
    padded_joined = mid_border(joined)
    pre_up = apply_taps(padded_joined, w_up, mid_extent, False)
    decoded = (act_fine.astype(jnp.float32) + upsample(jax.nn.silu(pre_up), 2)).astype(jnp.bfloat16)
    grad_out = cotangent.astype(jnp.float32) * jnp.float32(1.0 / math.sqrt(total_cells))
    grad_pre_up = (pool_sum(grad_out, 2) * silu_grad(pre_up)).astype(jnp.bfloat16)
    grad_w_up = gather_taps(padded_joined, grad_pre_up, mid_extent, False)
    grad_joined = apply_taps(back_border(grad_pre_up), flipped(w_up), mid_extent, False)
    grad_coarse_out = pool_sum(grad_joined, 4).astype(jnp.bfloat16)
    grad_w_proj = jnp.einsum(
        "xyzd,cxyz->dc", act_coarse, grad_coarse_out, preferred_element_type=jnp.float32
    )
    grad_act_coarse = jnp.einsum(
        "cxyz,dc->xyzd", grad_coarse_out, w_proj, preferred_element_type=jnp.float32
    )
    grad_pre_coarse = (grad_act_coarse * silu_grad(pre_coarse)).astype(jnp.bfloat16)
    padded_grad = column_border(grad_pre_coarse)
    inner_grad = padded_grad[1:-1, 1:-1, 1:-1, :]
    grad_w_coarse = lax.psum(
        gather_taps(padded_lift, inner_grad, column_extent, True).astype(jnp.bfloat16), ("gx", "gz")
    ).astype(jnp.float32)
    grad_act_lift = lax.dynamic_slice_in_dim(
        apply_taps(padded_grad, flipped(w_coarse), column_extent, True), row_start, own_height, 1
    )
    grad_pre_lift = (grad_act_lift * silu_grad(pre_lift)).astype(jnp.bfloat16)
    grad_w_lift = jnp.einsum(
        "cxyz,xyzd->cd", pool_coarse, grad_pre_lift, preferred_element_type=jnp.float32
    )
    grad_pool_coarse = jnp.einsum(
        "xyzd,cd->cxyz", grad_pre_lift, w_lift, preferred_element_type=jnp.float32
    )
    grad_pre_mid = (
        (grad_joined + upsample(grad_pool_coarse, 4) / 64.0) * silu_grad(pre_mid)
    ).astype(jnp.bfloat16)
    grad_w_down = gather_taps(padded_pool, grad_pre_mid, mid_extent, False)
    grad_pool_mid = apply_taps(back_border(grad_pre_mid), flipped(w_down), mid_extent, False)
    grad_pre_fine = ((grad_out + upsample(grad_pool_mid, 2) / 8.0) * silu_grad(pre_fine)).astype(
        jnp.bfloat16
    )
    grad_w_fine = gather_taps(padded_fine, grad_pre_fine, fine_extent, False)
    summed = lax.psum(
        (grad_w_fine, grad_w_down, grad_w_up, grad_w_lift, grad_w_proj), ("gx", "gy", "gz")
    )
    return (decoded, summed[0], summed[1], summed[3], grad_w_coarse, summed[4], summed[2])


def solution(mesh):
    placed = (P(None, "gx", "gy", "gz"), P(), P(), P(), P(), P(), P(), P(None, "gx", "gy", "gz"))
    return jax.shard_map(
        shards,
        mesh=mesh,
        in_specs=placed,
        out_specs=(P(None, "gx", "gy", "gz"), P(), P(), P(), P(), P(), P()),
        check_vma=False,
    )
```

profile of v0, /device:TPU:1, one launch (start us, length us, event | category | flops | bytes accessed | tf_op | source)
XLA Modules:
  0.0 684.5 jit_solution(5909702981705691976)
XLA Ops:
  10.7 5.3 collective-permute-start
  18.4 4.4 copy.442
  37.5 3.7 collective-permute-start.2
  48.8 4.4 collective-permute-start.5
  77.4 4.8 reduce_sum.39
  86.5 4.1 collective-permute-done.7
  90.6 3.5 collective-permute-start.8
  99.0 5.5 collective-permute-start.10
  107.6 4.4 collective-permute-done.11
  118.2 28.5 %all-gather = bf16[16,8,256]{2,1,0:T(8,128)(2,1)S(1)} all-gather(bf16[2,8,256]{2,1,0:T(8,128)(2,1)S(1)} %get-tuple-element.295), channel_id=2, replica_groups=mesh['gx'=4,'gy'=8,'gz'=4] {'gy'}, dimensions={0}, use_global_device_ids=true | all-gather | bytes 73728 | tf_op jit(solution)/shard_map/all_gather | solution.py:127
  147.9 4.2 collective-permute-start.12
  153.6 8.7 %collective-permute-start.14 = (bf16[3,16,1,256]{3,2,1,0:T(2,128)(2,1)S(1)}, bf16[3,16,1,256]{3,2,1,0:T(2,128)(2,1)S(1)}, u32[]{:S(2)}, u32[]{:S(2)}) collective-permute-start(bf16[3,16,1,256]{3,2,1,0:T(2,128)(2,1)S(1)} %get-tuple-element.269), channel_id=1, source_target_pairs={{0,1},{1,2},{2,3},{4,5},{5,6},{6,7},{8,9},{9,10},{10,11},{12,13},{... | collective-permute-start | bytes 73736 | tf_op jit(solution)/shard_map/ppermute | solution.py:17
  167.6 4.8 reduce_sum.54
  178.2 4.0 collective-permute-start.16
  183.6 3.9 collective-permute-done.17
  187.5 5.2 collective-permute-start.18
  197.7 6.2 collective-permute-start.20
  227.0 3.6 collective-permute-start.22
  236.5 3.7 copy.436
  240.3 5.3 collective-permute-start.24
  246.9 3.5 collective-permute-done.25
  257.1 4.4 collective-permute-done.27
  266.9 28.1 %all-gather.1 = bf16[16,8,256]{2,1,0:T(8,128)(2,1)S(1)} all-gather(bf16[2,8,256]{2,1,0:T(8,128)(2,1)S(1)} %fusion.83), channel_id=3, replica_groups=mesh['gx'=4,'gy'=8,'gz'=4] {'gy'}, dimensions={0}, use_global_device_ids=true | all-gather | bytes 73728 | tf_op jit(solution)/shard_map/all_gather | solution.py:127
  296.4 4.9 collective-permute-start.28
  308.3 8.1 %collective-permute-start.30 = (bf16[3,16,1,256]{3,2,1,0:T(2,128)(2,1)S(1)}, bf16[3,16,1,256]{3,2,1,0:T(2,128)(2,1)S(1)}, u32[]{:S(2)}, u32[]{:S(2)}) collective-permute-start(bf16[3,16,1,256]{3,2,1,0:T(2,128)(2,1)S(1)} %get-tuple-element.263), channel_id=1, source_target_pairs={{0,1},{1,2},{2,3},{4,5},{5,6},{6,7},{8,9},{9,10},{10,11},{12,13},{... | collective-permute-start | bytes 73736 | tf_op jit(solution)/shard_map/ppermute | solution.py:17
  329.6 3.6 collective-permute-start.32
  338.3 5.2 collective-permute-start.34
  344.9 4.0 collective-permute-done.35
  349.0 4.1 collective-permute-start.36
  390.6 146.6 %all-reduce.8.cloned.1.call-done = (f32[27,16,16]{2,1,0:T(8,128)}, f32[27,16,32]{2,1,0:T(8,128)}, f32[32,256]{1,0:T(8,128)}, f32[256,32]{0,1:T(8,128)}, f32[27,32,16]{1,2,0:T(8,128)}) async-done(((f32[27,16,16]{2,1,0:T(8,128)}, f32[27,16,32]{2,1,0:T(8,128)}, f32[32,256]{1,0:T(8,128)}, f32[256,32]{0,1:T(8,128)}, f32[27,32,16]{1,2,0:T(8,128)}), (f32[27,16,16]{2,1,0:T(8,128)}, f32[27,16,32]{2,1,0:T(8,128)}, ...) | async-done | bytes 203792 | tf_op jit(solution)/shard_map/psum | solution.py:203
  538.9 129.8 %all-reduce.6.cloned.1.call-done = bf16[27,256,256]{2,1,0:T(8,128)(2,1)} async-done(((bf16[27,256,256]{2,1,0:T(8,128)(2,1)}), bf16[27,256,256]{2,1,0:T(8,128)(2,1)}) %all-reduce.6.cloned.1.call-update) | async-done | bytes 3538960 | tf_op jit(solution)/shard_map/psum | solution.py:181
  668.7 5.8 convert_element_type.114
  (647 shorter events, 200.2 us)
Async XLA Ops:
  7.2 530.0 %all-reduce.8.cloned.1.call-start = ((), (), s32[]{:S(2)}) async-start(), calls=%async_computation.1 | async-start | bytes 1458176 | tf_op jit(solution)/shard_map/psum | solution.py:203
  9.4 27.1 %collective-permute-start.1 = (bf16[16,1,16,64]{3,0,2,1:T(8,128)(2,1)}, bf16[16,1,16,64]{3,0,2,1:T(8,128)(2,1)}, u32[]{:S(2)}, u32[]{:S(2)}) collective-permute-start(bf16[16,1,16,64]{3,0,2,1:T(8,128)(2,1)} %get-tuple-element.121), channel_id=1, source_target_pairs={{32,0},{64,32},{96,64},{33,1},{65,33},{97,65},{34,2},{66,34},{98,6... | collective-permute-start | bytes 98312 | tf_op jit(solution)/shard_map/ppermute | solution.py:19
  10.7 23.5 %collective-permute-start = (bf16[16,1,16,64]{3,0,2,1:T(8,128)(2,1)}, bf16[16,1,16,64]{3,0,2,1:T(8,128)(2,1)}, u32[]{:S(2)}, u32[]{:S(2)}) collective-permute-start(bf16[16,1,16,64]{3,0,2,1:T(8,128)(2,1)} %get-tuple-element.122), channel_id=1, source_target_pairs={{0,32},{32,64},{64,96},{1,33},{33,65},{65,97},{2,34},{34,66},{66,9... | collective-permute-start | bytes 98312 | tf_op jit(solution)/shard_map/ppermute | solution.py:17
  37.5 6.9 %collective-permute-start.2 = (bf16[16,10,1,64]{3,0,2,1:T(8,128)(2,1)S(1)}, bf16[16,10,1,64]{3,0,2,1:T(8,128)(2,1)S(1)}, u32[]{:S(2)}, u32[]{:S(2)}) collective-permute-start(bf16[16,10,1,64]{3,0,2,1:T(8,128)(2,1)S(1)} %get-tuple-element.79), channel_id=1, source_target_pairs={{0,4},{4,8},{8,12},{12,16},{16,20},{20,24},{24,28},{1,5},{5,9},{9,... | collective-permute-start | bytes 61448 | tf_op jit(solution)/shard_map/ppermute | solution.py:17
  48.8 10.6 %collective-permute-start.5 = (bf16[16,10,18,1]{2,0,3,1:T(8,128)(2,1)S(1)}, bf16[16,10,18,1]{2,0,3,1:T(8,128)(2,1)S(1)}, u32[]{:S(2)}, u32[]{:S(2)}) collective-permute-start(bf16[16,10,18,1]{2,0,3,1:T(8,128)(2,1)S(1)} %copy.403), channel_id=1, source_target_pairs={{1,0},{2,1},{3,2},{5,4},{6,5},{7,6},{9,8},{10,9},{11,10},{13,12},{... | collective-permute-start | bytes 17288 | tf_op jit(solution)/shard_map/ppermute | solution.py:19
  85.1 5.5 collective-permute-start.7
  90.6 5.3 collective-permute-start.8
  99.0 8.6 %collective-permute-start.10 = (bf16[16,6,10,1]{3,0,2,1:T(8,128)(2,1)S(1)}, bf16[16,6,10,1]{3,0,2,1:T(8,128)(2,1)S(1)}, u32[]{:S(2)}, u32[]{:S(2)}) collective-permute-start(bf16[16,6,10,1]{3,0,2,1:T(8,128)(2,1)S(1)} %get-tuple-element.249), channel_id=1, source_target_pairs={{0,1},{1,2},{2,3},{4,5},{5,6},{6,7},{8,9},{9,10},{10,11},{12,13},{... | collective-permute-start | bytes 5768 | tf_op jit(solution)/shard_map/ppermute | solution.py:17
  104.4 7.5 %collective-permute-start.11 = (bf16[16,6,10,1]{3,0,2,1:T(8,128)(2,1)S(1)}, bf16[16,6,10,1]{3,0,2,1:T(8,128)(2,1)S(1)}, u32[]{:S(2)}, u32[]{:S(2)}) collective-permute-start(bf16[16,6,10,1]{3,0,2,1:T(8,128)(2,1)S(1)} %get-tuple-element.250), channel_id=1, source_target_pairs={{1,0},{2,1},{3,2},{5,4},{6,5},{7,6},{9,8},{10,9},{11,10},{13,12},{... | collective-permute-start | bytes 5768 | tf_op jit(solution)/shard_map/ppermute | solution.py:19
  146.7 6.2 collective-permute-start.13
  147.9 5.5 collective-permute-start.12
  153.6 19.0 %collective-permute-start.14 = (bf16[3,16,1,256]{3,2,1,0:T(2,128)(2,1)S(1)}, bf16[3,16,1,256]{3,2,1,0:T(2,128)(2,1)S(1)}, u32[]{:S(2)}, u32[]{:S(2)}) collective-permute-start(bf16[3,16,1,256]{3,2,1,0:T(2,128)(2,1)S(1)} %get-tuple-element.269), channel_id=1, source_target_pairs={{0,1},{1,2},{2,3},{4,5},{5,6},{6,7},{8,9},{9,10},{10,11},{12,13},{... | collective-permute-start | bytes 73736 | tf_op jit(solution)/shard_map/ppermute | solution.py:17
  162.2 10.4 %collective-permute-start.15 = (bf16[3,16,1,256]{3,2,1,0:T(2,128)(2,1)S(1)}, bf16[3,16,1,256]{3,2,1,0:T(2,128)(2,1)S(1)}, u32[]{:S(2)}, u32[]{:S(2)}) collective-permute-start(bf16[3,16,1,256]{3,2,1,0:T(2,128)(2,1)S(1)} %get-tuple-element.270), channel_id=1, source_target_pairs={{1,0},{2,1},{3,2},{5,4},{6,5},{7,6},{9,8},{10,9},{11,10},{13,12},{... | collective-permute-start | bytes 73736 | tf_op jit(solution)/shard_map/ppermute | solution.py:19
  178.2 5.4 collective-permute-start.16
  182.2 5.3 collective-permute-start.17
  187.5 6.7 collective-permute-start.18
  197.7 8.7 %collective-permute-start.20 = (bf16[32,6,10,1]{0,3,2,1:T(2,128)(2,1)S(1)}, bf16[32,6,10,1]{0,3,2,1:T(2,128)(2,1)S(1)}, u32[]{:S(2)}, u32[]{:S(2)}) collective-permute-start(bf16[32,6,10,1]{0,3,2,1:T(2,128)(2,1)S(1)} %get-tuple-element.129), channel_id=1, source_target_pairs={{0,1},{1,2},{2,3},{4,5},{5,6},{6,7},{8,9},{9,10},{10,11},{12,13},{... | collective-permute-start | bytes 11528 | tf_op jit(solution)/shard_map/ppermute | solution.py:17
  203.9 5.2 collective-permute-start.21
  227.0 13.2 %collective-permute-start.22 = (bf16[16,1,8,32]{3,0,2,1:T(8,128)(2,1)}, bf16[16,1,8,32]{3,0,2,1:T(8,128)(2,1)S(1)}, u32[]{:S(2)}, u32[]{:S(2)}) collective-permute-start(bf16[16,1,8,32]{3,0,2,1:T(8,128)(2,1)} %get-tuple-element.277), channel_id=1, source_target_pairs={{0,32},{32,64},{64,96},{1,33},{33,65},{65,97},{2,34},{34,66},{66,9... | collective-permute-start | bytes 24584 | tf_op jit(solution)/shard_map/ppermute | solution.py:17
  230.6 9.6 %collective-permute-start.23 = (bf16[16,1,8,32]{3,0,2,1:T(8,128)(2,1)}, bf16[16,1,8,32]{3,0,2,1:T(8,128)(2,1)S(1)}, u32[]{:S(2)}, u32[]{:S(2)}) collective-permute-start(bf16[16,1,8,32]{3,0,2,1:T(8,128)(2,1)} %get-tuple-element.278), channel_id=1, source_target_pairs={{32,0},{64,32},{96,64},{33,1},{65,33},{97,65},{34,2},{66,34},{98,6... | collective-permute-start | bytes 24584 | tf_op jit(solution)/shard_map/ppermute | solution.py:19
  240.3 6.6 collective-permute-start.24
  250.6 6.5 collective-permute-start.26
  254.0 7.5 %collective-permute-start.27 = (bf16[16,6,10,1]{3,0,2,1:T(8,128)(2,1)S(1)}, bf16[16,6,10,1]{3,0,2,1:T(8,128)(2,1)S(1)}, u32[]{:S(2)}, u32[]{:S(2)}) collective-permute-start(bf16[16,6,10,1]{3,0,2,1:T(8,128)(2,1)S(1)} %get-tuple-element.222), channel_id=1, source_target_pairs={{1,0},{2,1},{3,2},{5,4},{6,5},{7,6},{9,8},{10,9},{11,10},{13,12},{... | collective-permute-start | bytes 5768 | tf_op jit(solution)/shard_map/ppermute | solution.py:19
  295.0 13.2 %collective-permute-start.29 = (bf16[1,16,8,256]{3,2,1,0:T(8,128)(2,1)S(1)}, bf16[1,16,8,256]{3,2,1,0:T(8,128)(2,1)S(1)}, u32[]{:S(2)}, u32[]{:S(2)}) collective-permute-start(bf16[1,16,8,256]{3,2,1,0:T(8,128)(2,1)S(1)} %bitcast.1500), channel_id=1, source_target_pairs={{32,0},{64,32},{96,64},{33,1},{65,33},{97,65},{34,2},{66,34},{98,6... | collective-permute-start | bytes 196616 | tf_op jit(solution)/shard_map/ppermute | solution.py:19
  296.4 11.8 %collective-permute-start.28 = (bf16[1,16,8,256]{3,2,1,0:T(8,128)(2,1)S(1)}, bf16[1,16,8,256]{3,2,1,0:T(8,128)(2,1)S(1)}, u32[]{:S(2)}, u32[]{:S(2)}) collective-permute-start(bf16[1,16,8,256]{3,2,1,0:T(8,128)(2,1)S(1)} %bitcast.1501), channel_id=1, source_target_pairs={{0,32},{32,64},{64,96},{1,33},{33,65},{65,97},{2,34},{34,66},{66,9... | collective-permute-start | bytes 196616 | tf_op jit(solution)/shard_map/ppermute | solution.py:17
  308.3 10.9 %collective-permute-start.30 = (bf16[3,16,1,256]{3,2,1,0:T(2,128)(2,1)S(1)}, bf16[3,16,1,256]{3,2,1,0:T(2,128)(2,1)S(1)}, u32[]{:S(2)}, u32[]{:S(2)}) collective-permute-start(bf16[3,16,1,256]{3,2,1,0:T(2,128)(2,1)S(1)} %get-tuple-element.263), channel_id=1, source_target_pairs={{0,1},{1,2},{2,3},{4,5},{5,6},{6,7},{8,9},{9,10},{10,11},{12,13},{... | collective-permute-start | bytes 73736 | tf_op jit(solution)/shard_map/ppermute | solution.py:17
  316.4 5.4 collective-permute-start.31
  329.6 5.8 collective-permute-start.32
  338.3 6.7 collective-permute-start.34
  343.5 5.4 collective-permute-start.35
  349.0 6.7 collective-permute-start.36
  388.5 280.2 %all-reduce.6.cloned.1.call-start = ((), (), s32[]{:S(2)}) async-start(), calls=%async_computation | async-start | bytes 7077888 | tf_op jit(solution)/shard_map/psum | solution.py:181
  (190 other events, 1465.8 us)
Sparse Core Ops, SparseCore 0:
  388.6 148.5 all-reduce.7
  539.7 128.9 all-reduce.5
where the time goes:
time: 693 us; the launch traced here: 684 us
  waiting for transfers between devices  322 us (46%)
  starting transfers between devices  123 us (18%)
  local copies, waits for them, and re-layouts  80.3 us (12%)
  blocking collectives  56.6 us (8%)
  matrix products  56.4 us (8%)
  other arithmetic  28.5 us (4%)
  between operations  17.7 us (3%)
    psum x1, waiting for transfers between devices, shards(): lax.psum((grad_w_fine, grad_w_down, grad_w_up, grad_w_lift, grad_w_proj),...  147 us
    psum x1, waiting for transfers between devices, shards(): lax.psum(gather_taps(padded_lift, inner_grad, column_extent, True).astype...  130 us
    ppermute x19, starting transfers between devices, padded_2(): lax.ppermute(tail, axis, [(i, (i + 1) % count) for i in range(ends)])  90.5 us
    all_gather x2, blocking collectives, column_border(): column = lax.all_gather(values, 'gy', axis=1, tiled=True)  56.6 us
    ppermute x19, waiting for transfers between devices, padded_2(): lax.ppermute(head, axis, [((i + 1) % count, i) for i in range(ends)])  43.2 us
    unnamed x382, local copies, waits for them, and re-layouts  41 us
    ppermute x19, starting transfers between devices, padded_2(): lax.ppermute(head, axis, [((i + 1) % count, i) for i in range(ends)])  32.5 us
    dot_general x45, matrix products, apply_taps(): jnp.einsum('kcxyz,kco->oxyz', stacked, tap_weights, preferred_element_typ...  26.1 us
  transfers between devices with their start and end apart: 40, of which 18 were waited for; matrix products, arithmetic and copies ran while one was open for 8% of the time, Pallas kernels for 0%

commit v1 on v0

v1 whole, which is shorter than its diff:
```python
import functools
import math

import jax
import jax.numpy as jnp
from jax import lax
from jax.experimental import pallas as pl
from jax.experimental.pallas import tpu as pltpu
from jax.sharding import PartitionSpec as P

BF = jnp.bfloat16
F32 = jnp.float32
MESH = pl.DeviceIdType.MESH
LANES = 128


def dot(left, right):
    return jnp.dot(left, right, preferred_element_type=F32)


def dot_nt(left, right):
    return lax.dot_general(left, right, (((1,), (1,)), ((), ())), preferred_element_type=F32)


def dot_tn(left, right):
    return lax.dot_general(left, right, (((0,), (0,)), ((), ())), preferred_element_type=F32)


def sigmoid(values):
    return 0.5 * jnp.tanh(0.5 * values) + 0.5


def slope(values, sig):
    return sig * (1.0 + values * (1.0 - sig))


def lane_of(rows):
    return lax.broadcasted_iota(jnp.int32, (rows, LANES), 1)


def turn(row, by):
    if isinstance(by, int):
        by = by % LANES
        return row if by == 0 else pltpu.roll(row, by, 1)
    return pltpu.roll(row, lax.rem(by + 4 * LANES, LANES), 1)


def store_taps(ref, at, row, rows):
    ref[at + (pl.ds(0, rows),)] = turn(row, 1).astype(BF)
    ref[at + (pl.ds(rows, rows),)] = row.astype(BF)
    ref[at + (pl.ds(2 * rows, rows),)] = turn(row, -1).astype(BF)


def around(ref, x, y):
    block = ref[pl.ds(x, 3), pl.ds(y, 3)]
    return block.reshape(9 * block.shape[2], LANES)


def conv_pair(weight, ref, x, y):
    both = jnp.concatenate([around(ref, x, y), around(ref, x, y + 1)], axis=1)
    out = dot(weight, both)
    return out[:, :LANES], out[:, LANES:]


def pool_matrix():
    row = lax.broadcasted_iota(jnp.int32, (8 * LANES, LANES), 0)
    col = lax.broadcasted_iota(jnp.int32, (8 * LANES, LANES), 1)
    hit = (row // 256 == col // 32) & (row % 64 // 2 == col % 32)
    return jnp.where(hit, 1.0, 0.0).astype(BF)


def grow_matrix():
    row = lax.broadcasted_iota(jnp.int32, (LANES, 4 * LANES), 0)
    col = lax.broadcasted_iota(jnp.int32, (LANES, 4 * LANES), 1)
    hit = (row // 32 == col // LANES) & (row % 32 == col % 64 // 2)
    return jnp.where(hit, 1.0, 0.0).astype(BF)


def coarse_sum_matrix(tiles):
    row = lax.broadcasted_iota(jnp.int32, (8, tiles * LANES), 0)
    col = lax.broadcasted_iota(jnp.int32, (8, tiles * LANES), 1) % LANES
    return jnp.where((col < 32) & (col // 4 == row), 1.0, 0.0).astype(BF)


def coarse_grow_matrix(cells, gz):
    row = lax.broadcasted_iota(jnp.int32, (cells, LANES), 0)
    col = lax.broadcasted_iota(jnp.int32, (cells, LANES), 1)
    cell = jnp.where(col < 64, col, col - LANES)
    near = (cell >= -3) & (cell < 35)
    mid = cell + gz * 32
    hit = near & (mid >= 0) & (row == (mid + 4) // 4 - 1)
    return jnp.where(hit, 1.0, 0.0).astype(BF)


def pack_four(rows):
    lane = lane_of(rows[0].shape[0])
    total = None
    for q, row in enumerate(rows):
        part = turn(jnp.where(lane < 32, row, 0.0), 32 * q)
        total = part if total is None else total + part
    return total


def plane_rows(block):
    rows = jnp.swapaxes(block, 0, 1)
    return [jnp.concatenate([rows[2 * t], rows[2 * t + 1]], axis=1) for t in range(8)]


def arrange_kernel(vol_ref, v_ref, e_ref):
    lane = lane_of(16)

    def plane(x, edges):
        low, high = edges
        for t, tile in enumerate(plane_rows(vol_ref[:, x])):
            v_ref[x, t] = tile
            wide = tile.astype(F32)
            for b in range(2):
                at = x * 16 + 2 * t + b
                low = jnp.where(lane == at, turn(wide, at - 64 * b), low)
                high = jnp.where(lane == at, turn(wide, at - 64 * b - 63), high)
        return low, high

    zero = jnp.zeros((16, LANES), F32)
    low, high = lax.fori_loop(0, 8, plane, (zero, zero))
    e_ref[0] = low.astype(BF)
    e_ref[1] = high.astype(BF)


def halo_kernel(sizes, hx, ht, a_ref, e_ref, p_ref, er_ref, el_ref, send_sem, recv_sem):
    me = [lax.axis_index(name) for name in ("gx", "gy", "gz")]
    planes, tiles = a_ref.shape[:2]

    def there(at, step):
        if step == 0:
            return None
        return at[0] > 0 if step < 0 else at[0] < at[1] - 1

    def valid(steps):
        found = None
        for axis, step in enumerate(steps):
            test = there((me[axis], sizes[axis]), step)
            if test is not None:
                found = test if found is None else found & test
        return found

    def part(step, halo, count):
        if step == 0:
            return pl.ds(0, count), pl.ds(halo, count)
        if step > 0:
            return pl.ds(count - halo, halo), pl.ds(0, halo)
        return pl.ds(0, halo), pl.ds(count + halo, halo)

    steps_all = [
        (dx, dy, dz)
        for dz in (-1, 1, 0)
        for dx in (-1, 0, 1)
        for dy in (-1, 0, 1)
        if (dx, dy, dz) != (0, 0, 0)
    ]

    def copy_of(k, steps):
        dx, dy, dz = steps
        if dz == 0:
            fx, tx = part(dx, hx, planes)
            fy, ty = part(dy, ht, tiles)
            src, dst = a_ref.at[fx, fy], p_ref.at[tx, ty]
        elif dz > 0:
            src, dst = e_ref.at[1], el_ref.at[1 - dx, 1 - dy]
        else:
            src, dst = e_ref.at[0], er_ref.at[1 - dx, 1 - dy]
        return pltpu.make_async_remote_copy(
            src_ref=src,
            dst_ref=dst,
            send_sem=send_sem.at[k],
            recv_sem=recv_sem.at[k],
            device_id=(me[0] + dx, me[1] + dy, me[2] + dz),
            device_id_type=MESH,
        )

    barrier = pltpu.get_barrier_semaphore()
    total = 1
    for axis in range(3):
        low = jnp.where(me[axis] > 0, 1, 0)
        high = jnp.where(me[axis] < sizes[axis] - 1, 1, 0)
        total = total * (1 + low + high)
    for steps in steps_all:

        @pl.when(valid(steps))
        def _():
            pl.semaphore_signal(
                barrier,
                inc=1,
                device_id=tuple(me[axis] + steps[axis] for axis in range(3)),
                device_id_type=MESH,
            )

    pl.semaphore_wait(barrier, total - 1)

    for k, steps in enumerate(steps_all):

        @pl.when(valid(steps))
        def _():
            copy_of(k, steps).start()

    p_ref[pl.ds(hx, planes), pl.ds(ht, tiles)] = a_ref[...]
    for k, steps in enumerate(steps_all):
        back = tuple(-step for step in steps)
        dx, dy, dz = steps

        @pl.when(jnp.logical_not(valid(back)))
        def _():
            if dz == 0:
                _, tx = part(dx, hx, planes)
                _, ty = part(dy, ht, tiles)
                into = p_ref.at[tx, ty]
            elif dz > 0:
                into = el_ref.at[1 - dx, 1 - dy]
            else:
                into = er_ref.at[1 - dx, 1 - dy]
            into[...] = jnp.zeros(into.shape, into.dtype)

    for k, steps in enumerate(steps_all):
        back = tuple(-step for step in steps)

        @pl.when(valid(back))
        def _():
            copy_of(k, steps).wait_recv()

    for k, steps in enumerate(steps_all):

        @pl.when(valid(steps))
        def _():
            copy_of(k, steps).wait_send()


def plane_peers(nx, nz):
    return [(ox, oz) for ox in range(nx) for oz in range(nz) if (ox, oz) != (0, 0)]


def greet(peers):
    barrier = pltpu.get_barrier_semaphore()
    for peer in peers:
        pl.semaphore_signal(barrier, inc=1, device_id=peer, device_id_type=MESH)
    pl.semaphore_wait(barrier, len(peers))


def gather_kernel(sizes, g_ref, all_ref, stage, send_a, recv_a, send_b, recv_b):
    nx, ny, nz = sizes
    gx, gy, gz = [lax.axis_index(name) for name in ("gx", "gy", "gz")]
    plane = plane_peers(nx, nz)
    greet(
        [(lax.rem(gx + ox, nx), gy, lax.rem(gz + oz, nz)) for ox, oz in plane]
        + [(gx, lax.rem(gy + oy, ny), gz) for oy in range(1, ny)]
    )

    def first(k, x, z, peer):
        return pltpu.make_async_remote_copy(
            src_ref=g_ref,
            dst_ref=stage.at[x, pl.ds(pl.multiple_of(z * 8, 8), 8)],
            send_sem=send_a.at[k],
            recv_sem=recv_a.at[k],
            device_id=peer,
            device_id_type=MESH,
        )

    def second(oy, y):
        return pltpu.make_async_remote_copy(
            src_ref=all_ref.at[gy],
            dst_ref=all_ref.at[y],
            send_sem=send_b.at[oy],
            recv_sem=recv_b.at[oy],
            device_id=(gx, lax.rem(gy + oy, ny), gz),
            device_id_type=MESH,
        )

    for k, (ox, oz) in enumerate(plane):
        first(k, gx, gz, (lax.rem(gx + ox, nx), gy, lax.rem(gz + oz, nz))).start()
    stage[gx, pl.ds(pl.multiple_of(gz * 8, 8), 8)] = g_ref[...]
    for k, (ox, oz) in enumerate(plane):
        peer = (lax.rem(gx + ox, nx), gy, lax.rem(gz + oz, nz))
        first(k, lax.rem(gx + nx - ox, nx), lax.rem(gz + nz - oz, nz), peer).wait_recv()
    all_ref[gy] = stage[...].astype(BF)
    for oy in range(1, ny):
        second(oy, gy).start()
    for k, (ox, oz) in enumerate(plane):
        first(k, gx, gz, (lax.rem(gx + ox, nx), gy, lax.rem(gz + oz, nz))).wait_send()
    for oy in range(1, ny):
        second(oy, lax.rem(gy + ny - oy, ny)).wait_recv()
    for oy in range(1, ny):
        second(oy, gy).wait_send()


def reduce_kernel(sizes, pay_ref, out_ref, ra, rb, send_a, recv_a, send_b, recv_b, send_c, recv_c):
    nx, ny, nz = sizes
    gx, gy, gz = [lax.axis_index(name) for name in ("gx", "gy", "gz")]
    mine = gx * nz + gz
    plane = plane_peers(nx, nz)
    greet(
        [(lax.rem(gx + ox, nx), gy, lax.rem(gz + oz, nz)) for ox, oz in plane]
        + [(gx, lax.rem(gy + oy, ny), gz) for oy in range(1, ny)]
    )

    def ahead(ox, oz):
        return lax.rem(gx + ox, nx), lax.rem(gz + oz, nz)

    def behind(ox, oz):
        return lax.rem(gx + nx - ox, nx), lax.rem(gz + nz - oz, nz)

    def scatter(k, ox, oz, slot):
        x, z = ahead(ox, oz)
        return pltpu.make_async_remote_copy(
            src_ref=pay_ref.at[x * nz + z],
            dst_ref=ra.at[slot],
            send_sem=send_a.at[k],
            recv_sem=recv_a.at[k],
            device_id=(x, gy, z),
            device_id_type=MESH,
        )

    def across(oy, slot):
        return pltpu.make_async_remote_copy(
            src_ref=rb.at[gy],
            dst_ref=rb.at[slot],
            send_sem=send_b.at[oy],
            recv_sem=recv_b.at[oy],
            device_id=(gx, lax.rem(gy + oy, ny), gz),
            device_id_type=MESH,
        )

    def spread(k, ox, oz, slot):
        x, z = ahead(ox, oz)
        return pltpu.make_async_remote_copy(
            src_ref=out_ref.at[mine],
            dst_ref=out_ref.at[slot],
            send_sem=send_c.at[k],
            recv_sem=recv_c.at[k],
            device_id=(x, gy, z),
            device_id_type=MESH,
        )

    for k, (ox, oz) in enumerate(plane):
        scatter(k, ox, oz, mine).start()
    ra[mine] = pay_ref[mine]
    for k, (ox, oz) in enumerate(plane):
        x, z = behind(ox, oz)
        scatter(k, ox, oz, x * nz + z).wait_recv()
    rb[gy] = jnp.sum(ra[...], axis=0)
    for oy in range(1, ny):
        across(oy, gy).start()
    for k, (ox, oz) in enumerate(plane):
        scatter(k, ox, oz, mine).wait_send()
    for oy in range(1, ny):
        across(oy, lax.rem(gy + ny - oy, ny)).wait_recv()
    out_ref[mine] = jnp.sum(rb[...], axis=0)
    for k, (ox, oz) in enumerate(plane):
        spread(k, ox, oz, mine).start()
    for oy in range(1, ny):
        across(oy, gy).wait_send()
    for k, (ox, oz) in enumerate(plane):
        x, z = behind(ox, oz)
        spread(k, ox, oz, x * nz + z).wait_recv()
    for k, (ox, oz) in enumerate(plane):
        spread(k, ox, oz, mine).wait_send()


def fine_kernel(
    p_ref, er_ref, el_ref, cot_ref, wf_ref, pre_ref, act_ref, mg_ref, e_ref, v3_ref, ct_ref, sums
):
    lane = lane_of(16)

    def rows(x, _):
        dx, sx = (x + 7) // 8, lax.rem(x + 7, 8)
        for y in range(18):
            dy, sy = (y + 15) // 16, (y + 15) % 16
            base = turn(p_ref[x, (y + 1) // 2].astype(F32), 64 * ((y + 1) % 2))
            at = sx * 16 + sy
            right = turn(er_ref[dx, dy].astype(F32), 64 - at)
            left = turn(el_ref[dx, dy].astype(F32), 127 - at)
            edge = jnp.where(lane == 64, right, jnp.where(lane == 127, left, 0.0))
            store_taps(v3_ref, (x, y), jnp.where(lane < 64, base, edge), 16)
        return 0

    lax.fori_loop(0, 10, rows, 0)
    sums[...] = pool_matrix()
    weight = wf_ref[...]

    def conv(x, _):
        for t, tile in enumerate(plane_rows(cot_ref[:, x])):
            ct_ref[x, t] = tile
        for t in range(8):
            one, two = conv_pair(weight, v3_ref, x, 2 * t)
            pre = jnp.where(lane < 64, one, turn(two, 64))
            pre_ref[x, t] = pre
            act_ref[x, t] = (pre * sigmoid(pre)).astype(BF)
        return 0

    lax.fori_loop(0, 8, conv, 0)

    lane = lane_of(32)

    def pools(x, edges):
        low, high = edges
        for half in range(2):
            parts = []
            for ref, factor in ((act_ref, 0.125), (ct_ref, 1.0)):
                cells = jnp.concatenate(
                    [ref[2 * x + a, 4 * half + q] for q in range(4) for a in range(2)], axis=1
                )
                parts.append((dot(cells, sums[...]) * factor).astype(BF))
            tile = jnp.concatenate(parts, axis=0)
            mg_ref[x, half] = tile
            wide = tile.astype(F32)
            for q in range(4):
                at = (x * 8 + half * 4 + q) * 4
                here = (lane >= at) & (lane < at + 4)
                low = jnp.where(here, turn(wide, at - 32 * q), low)
                high = jnp.where(here, turn(wide, at - 32 * q - 28), high)
        return low, high

    zero = jnp.zeros((32, LANES), F32)
    low, high = lax.fori_loop(0, 4, pools, (zero, zero))
    e_ref[0] = low.astype(BF)
    e_ref[1] = high.astype(BF)


def mid_kernel(
    sizes, p_ref, er_ref, el_ref, wd_ref, am_ref, dsm_ref, pm3n_ref, pgr_ref, pc_ref, pm3, pgf, dsf
):
    gx, gy, gz = [lax.axis_index(name) for name in ("gx", "gy", "gz")]
    nx, ny, nz = sizes
    lane = lane_of(32)

    def rows(x, _):
        dx, sx = x // 4, lax.rem(x, 4)
        for y in range(16):
            dy, sy = (y + 4) // 8, (y + 4) % 8
            base = turn(p_ref[x, y // 4].astype(F32), -32 * (y % 4))
            at = (sx * 8 + sy) * 4
            right = turn(er_ref[dx, dy].astype(F32), 32 - at)
            left = turn(el_ref[dx, dy].astype(F32), 124 - at)
            edge = jnp.where(lane < 36, right, jnp.where(lane >= 124, left, 0.0))
            row = jnp.where(lane < 32, base, edge)
            store_taps(pm3, (x, y), row[:16], 16)
            pgf[x, y] = row[16:].astype(BF)
        return 0

    lax.fori_loop(0, 12, rows, 0)
    weight = wd_ref[...]
    cell = jnp.where(lane < 64, lane, lane - LANES)
    mid = cell + gz * 32
    inside = (cell >= -3) & (cell < 35) & (mid >= 0) & (mid < 32 * nz)

    def conv(x, _):
        at_x = gx * 4 + x - 3
        for y in range(0, 14, 2):
            for b, pre in enumerate(conv_pair(weight, pm3, x, y)):
                at_y = gy * 8 + y + b - 3
                there = (at_x >= 0) & (at_x < 4 * nx) & (at_y >= 0) & (at_y < 8 * ny)
                keep = inside & there
                sig = sigmoid(pre)
                am_ref[x, y + b] = jnp.where(keep, pre * sig, 0.0).astype(BF)
                dsf[x, y + b] = jnp.where(keep, slope(pre, sig), 0.0).astype(BF)
        return 0

    lax.fori_loop(0, 10, conv, 0)
    dsm_ref[...] = dsf[2:8, 2:12]
    pm3n_ref[...] = pm3[3:9, 3:13]
    pgr_ref[...] = pgf[2:10, 2:14]
    halves = [
        jnp.concatenate([am_ref[3 + a, 3 + 4 * h + b] for a in range(4) for b in range(4)], axis=1)
        for h in range(2)
    ]
    cells = jnp.concatenate(halves + [jnp.zeros((64, 16 * LANES), BF)], axis=0)
    pooled = dot_nt(coarse_sum_matrix(16), cells) * (1.0 / 64.0)
    pc_ref[...] = pooled.astype(BF).astype(F32)


def place_weight(ref, weight):
    for y2 in range(2):
        ref[y2] = jnp.zeros((LANES, 256), BF)
        ref[y2, pl.ds(32 * y2, 32)] = weight


def store_coarse_taps(ref, at, cells):
    count = cells.shape[0]
    row = lax.broadcasted_iota(jnp.int32, cells.shape, 0)
    before = jnp.where(row > 0, pltpu.roll(cells, 1, 0), 0.0)
    after = jnp.where(row < count - 1, pltpu.roll(cells, count - 1, 0), 0.0)
    ref[at + (slice(None), pl.ds(0, 256))] = before.astype(BF)
    ref[at + (slice(None), pl.ds(256, 256))] = cells.astype(BF)
    ref[at + (slice(None), pl.ds(512, 256))] = after.astype(BF)


def zero_rim(ref, rim):
    planes, rows = ref.shape[:2]

    def clear(x, _):
        for y in list(range(rim)) + list(range(rows - rim, rows)):
            ref[x, y] = jnp.zeros(ref.shape[2:], ref.dtype)
        return 0

    lax.fori_loop(0, planes, clear, 0)

    def clear_plane(y, _):
        for x in list(range(rim)) + list(range(planes - rim, planes)):
            ref[x, y] = jnp.zeros(ref.shape[2:], ref.dtype)
        return 0

    lax.fori_loop(0, rows, clear_plane, 0)


def clamp(at, count):
    return jnp.minimum(jnp.maximum(at, 0), count - 1)


def near_cells(sizes):
    nx, ny, _ = sizes
    gx, gy = lax.axis_index("gx"), lax.axis_index("gy")
    found = []
    for dx in range(3):
        for dy in range(4):
            x, y = gx - 1 + dx, gy + (dy + 1) // 2 - 1
            there = (x >= 0) & (x < nx) & (y >= 0) & (y < ny)
            keep = jnp.where(there, 1.0, 0.0)
            found.append((dx, dy, clamp(x, nx), clamp(y, ny), (dy + 1) % 2, keep))
    return found


def up_kernel(
    sizes,
    scale,
    pcg_ref,
    am_ref,
    act_ref,
    pgr_ref,
    wl_ref,
    wc_ref,
    wp_ref,
    wu_ref,
    wut_ref,
    dec_ref,
    gj_ref,
    gwu_ref,
    gc_ref,
    dsc_ref,
    actc_ref,
    alc_ref,
    wide_lift,
    al3,
    acc,
    cos,
    j3,
    gu3,
    su,
    plane,
):
    nx, ny, nz = sizes
    gz = lax.axis_index("gz")
    cells = 8 * nz
    place_weight(wide_lift, wl_ref[...])
    zero_rim(al3, 1)

    def lift(y, _):
        for x in range(nx):
            for y2 in range(2):
                pre = dot(pcg_ref[y, x], wide_lift[y2])
                act = (pre * sigmoid(pre)).astype(BF)
                alc_ref[x, y, y2] = act
                store_coarse_taps(al3, (x + 1, 2 * y + y2 + 1), act.astype(F32))
        return 0

    lax.fori_loop(0, ny, lift, 0)

    def coarse(x, _):
        for i in range(3):
            for j in range(3):
                block = al3[x + i, pl.ds(j, 2 * ny)].reshape(2 * ny * cells, 768)
                part = dot(block, wc_ref[3 * i + j])
                if i + j == 0:
                    acc[...] = part
                else:
                    acc[...] += part
        pre = acc[...]
        sig = sigmoid(pre)
        shape = (ny, 2, cells, 256)
        actc_ref[x] = (pre * sig).astype(BF).reshape(shape)
        dsc_ref[x] = slope(pre, sig).astype(BF).reshape(shape)
        return 0

    lax.fori_loop(0, nx, coarse, 0)

    spread = coarse_grow_matrix(cells, gz)
    for dx, dy, x, y, y2, keep in near_cells(sizes):
        out = dot_nt(wp_ref[...], actc_ref[x, y, y2]).astype(BF)
        cos[dx, dy] = dot(out, spread) * keep

    def join(x, _):
        for y in range(14):
            row = am_ref[x, y].astype(F32) + cos[(x + 1) // 4, (y + 1) // 4]
            store_taps(j3, (x, y), row.astype(BF).astype(F32), 32)
        return 0

    lax.fori_loop(0, 10, join, 0)

    lane = lane_of(16)
    near = (lane < 34) | (lane >= 126)
    weight = wu_ref[...]

    def up(x, _):
        for y in range(0, 12, 2):
            for b, pre in enumerate(conv_pair(weight, j3, x, y)):
                sig = sigmoid(pre)
                su[x, y + b] = (pre * sig).astype(BF)
                pooled = pgr_ref[x, y + b].astype(F32) * scale
                grad = jnp.where(near, pooled * slope(pre, sig), 0.0)
                store_taps(gu3, (x, y + b), grad.astype(BF).astype(F32), 16)
        return 0

    lax.fori_loop(0, 8, up, 0)

    weight_t = wut_ref[...]

    def back(x, _):
        for y in range(0, 10, 2):
            for b, grad in enumerate(conv_pair(weight_t, gu3, x, y)):
                gj_ref[x, y + b] = grad
        return 0

    lax.fori_loop(0, 6, back, 0)

    sums = coarse_sum_matrix(1)
    halves = []
    for h in range(2):
        total = None
        for a in range(4):
            for b in range(4):
                row = gj_ref[1 + a, 1 + 4 * h + b]
                total = row if total is None else total + row
        halves.append(total)
    total = jnp.concatenate(halves + [jnp.zeros((64, LANES), F32)], axis=0)
    head = total.astype(BF)
    tail = (total - head.astype(F32)).astype(BF)
    gc_ref[...] = (dot_nt(sums, head) + dot_nt(sums, tail)).astype(BF).astype(F32)

    gwu_ref[...] = jnp.zeros(gwu_ref.shape, F32)

    def taps(x, _):
        grads, cells_near = [], []
        for y in range(8):
            grads.append(jnp.where(lane < 32, gu3[x + 2, y + 2, pl.ds(16, 16)].astype(F32), 0.0))
            cells_near.append(around(j3, x + 2, y + 2))
        grad = jnp.concatenate(grads, axis=1).astype(BF)
        gwu_ref[:, pl.ds(0, 864)] += dot_nt(grad, jnp.concatenate(cells_near, axis=1))
        return 0

    lax.fori_loop(0, 4, taps, 0)

    grow = grow_matrix()

    def decode(x, _):
        for a in range(2):
            for half in range(2):
                rows = [su[x + 2, 4 * half + q + 2].astype(F32) for q in range(4)]
                grown = dot(pack_four(rows).astype(BF), grow)
                for q in range(4):
                    t = 4 * half + q
                    tile = act_ref[2 * x + a, t].astype(F32) + grown[:, q * LANES : (q + 1) * LANES]
                    plane[2 * t] = tile.astype(BF)
                    plane[2 * t + 1] = turn(tile, 64).astype(BF)
            dec_ref[:, 2 * x + a] = jnp.swapaxes(plane[...], 0, 1)[:, :, :64]
        return 0

    lax.fori_loop(0, 4, decode, 0)


def back_kernel(
    sizes,
    scale,
    gcg_ref,
    pcg_ref,
    dsc_ref,
    actc_ref,
    gj_ref,
    dsm_ref,
    pm3n_ref,
    ct_ref,
    pre_ref,
    v3_ref,
    gwu_ref,
    wl_ref,
    wc_ref,
    wp_ref,
    wdt_ref,
    pay_ref,
    gpc_ref,
    gwp_ref,
    wide_lift,
    wide_proj,
    gp3,
    acc,
    gps,
    gm3,
    gpm,
    gf,
    accf,
    accd,
    sums,
):
    nx, ny, nz = sizes
    gx, gy, gz = [lax.axis_index(name) for name in ("gx", "gy", "gz")]
    cells = 8 * nz
    place_weight(wide_lift, wl_ref[...])
    place_weight(wide_proj, wp_ref[...])
    zero_rim(gp3, 2)

    def coarse(y, _):
        for x in range(nx):
            for y2 in range(2):
                grad = dot(gcg_ref[y, x], wide_proj[y2]) * dsc_ref[x, y, y2].astype(F32)
                grad = grad.astype(BF)
                gpc_ref[x, y, y2] = grad
                store_coarse_taps(gp3, (x + 2, 2 * y + y2 + 2), grad.astype(F32))
        return 0

    lax.fori_loop(0, ny, coarse, 0)

    sums[...] = jnp.zeros(sums.shape, F32)

    def proj_grad(x, _):
        for y2 in range(2):
            grads = gcg_ref[:, x].reshape(ny * cells, LANES)
            sums[y2] += dot_tn(grads, actc_ref[x, :, y2].reshape(ny * cells, 256))
        return 0

    lax.fori_loop(0, nx, proj_grad, 0)
    gwp_ref[...] = sums[0, :32] + sums[1, 32:64]

    acc[...] = jnp.zeros(acc.shape, F32)

    def coarse_back(i, _):
        for j in range(3):
            block = gp3[pl.ds(gx + i, 3), pl.ds(2 * gy + j, 4)].reshape(12 * cells, 768)
            for k in range(3):
                weight = wc_ref[8 - 3 * i - j, pl.ds(256 * (2 - k), 256)]
                acc[...] += dot_nt(block[:, 256 * k : 256 * (k + 1)], weight)
        return 0

    lax.fori_loop(0, 3, coarse_back, 0)

    spread = coarse_grow_matrix(cells, gz)
    own = lax.broadcasted_iota(jnp.int32, (cells, 256), 0) // 8 == gz
    for at, (dx, dy, x, y, y2, keep) in enumerate(near_cells(sizes)):
        pre = dot(pcg_ref[y, x], wide_lift[y2])
        grad = (acc[pl.ds(at * cells, cells)] * slope(pre, sigmoid(pre))).astype(BF)
        out = dot_nt(wl_ref[...], grad).astype(BF)
        gps[dx, dy] = dot(out, spread) * (keep * (1.0 / 64.0))
        if dx == 1 and dy in (1, 2):
            masked = jnp.where(own, grad.astype(F32), 0.0).astype(BF)
            sums[y2] = dot_tn(pcg_ref[y, x], masked)

    def join(x, _):
        for y in range(10):
            row = gj_ref[x, y] + gps[(x + 3) // 4, (y + 3) // 4]
            row = row * dsm_ref[x, y].astype(F32)
            store_taps(gm3, (x, y), row.astype(BF).astype(F32), 32)
        return 0

    lax.fori_loop(0, 6, join, 0)

    weight_t = wdt_ref[...]

    def back(x, _):
        rows = []
        for y in range(0, 8, 2):
            rows.extend(conv_pair(weight_t, gm3, x, y))
        for half in range(2):
            gpm[x, half] = pack_four(rows[4 * half : 4 * half + 4]).astype(BF)
        return 0

    lax.fori_loop(0, 4, back, 0)

    grow = grow_matrix()

    def fine(x, _):
        for half in range(2):
            grown = dot(gpm[x, half], grow) * 0.125
            for a in range(2):
                for q in range(4):
                    t = 4 * half + q
                    pre = pre_ref[2 * x + a, t]
                    grad = ct_ref[2 * x + a, t].astype(F32) * scale
                    grad = grad + grown[:, q * LANES : (q + 1) * LANES]
                    gf[2 * x + a, t] = (grad * slope(pre, sigmoid(pre))).astype(BF)
        return 0

    lax.fori_loop(0, 4, fine, 0)

    accd[...] = jnp.zeros(accd.shape, F32)
    lane = lane_of(32)

    def taps_down(x, _):
        grads, cells_near = [], []
        for y in range(8):
            grads.append(jnp.where(lane < 32, gm3[x + 1, y + 1, pl.ds(32, 32)].astype(F32), 0.0))
            cells_near.append(around(pm3n_ref, x, y))
        grad = jnp.concatenate(grads, axis=1).astype(BF)
        accd[:, pl.ds(0, 432)] += dot_nt(grad, jnp.concatenate(cells_near, axis=1))
        return 0

    lax.fori_loop(0, 4, taps_down, 0)

    accf[...] = jnp.zeros(accf.shape, F32)
    lane16 = lane_of(16)

    def taps_fine(x, _):
        for half in range(2):
            grads, cells_near = [], []
            for t in range(4 * half, 4 * half + 4):
                tile = gf[x, t].astype(F32)
                for b in range(2):
                    grads.append(jnp.where(lane16 < 64, turn(tile, 64 * b), 0.0))
                    cells_near.append(around(v3_ref, x, 2 * t + b))
            grad = jnp.concatenate(grads, axis=1).astype(BF)
            accf[:, pl.ds(0, 432)] += dot_nt(grad, jnp.concatenate(cells_near, axis=1))
        return 0

    lax.fori_loop(0, 8, taps_fine, 0)

    for b in range(4):
        pay_ref[pl.ds(16 * b, 16)] = accf[:, b * LANES : (b + 1) * LANES]
    for b in range(7):
        pay_ref[pl.ds(64 + 16 * b, 16)] = gwu_ref[:, b * LANES : (b + 1) * LANES]
    for b in range(4):
        pay_ref[pl.ds(176 + 32 * b, 32)] = accd[:, b * LANES : (b + 1) * LANES]
    lifts = sums[0, :32] + sums[1, 32:64]
    for b in range(2):
        pay_ref[pl.ds(304 + 32 * b, 32)] = lifts[:, b * LANES : (b + 1) * LANES]
    pay_ref[pl.ds(368, 16)] = jnp.zeros((16, LANES), F32)


def last_kernel(
    sizes,
    gpc_ref,
    alc_ref,
    red_ref,
    gwp_ref,
    wc_out,
    wf_out,
    wd_out,
    wl_out,
    wp_out,
    wu_out,
    cells_t,
    gs,
):
    nx, ny, nz = sizes
    cells = 8 * nz
    count = nx * ny * 2 * cells
    step = pl.program_id(0)

    @pl.when(step == 0)
    def _():
        def columns(start, blocks, rows):
            return jnp.concatenate(
                [red_ref[pl.ds(start + rows * b, rows)] for b in range(blocks)], axis=1
            )

        wf_out[...] = columns(0, 4, 16)[:, :432].T.reshape(27, 16, 16)
        wu_out[...] = columns(64, 7, 16)[:, :864].T.reshape(27, 32, 16)
        wd_out[...] = columns(176, 4, 32)[:, :432].T.reshape(27, 16, 32)
        wl_out[...] = columns(304, 2, 32)
        wp_out[...] = gwp_ref[...].T
        cells_t[...] = alc_ref[...].reshape(count, 256).T
        for k in range(3):
            zero_rim(gs.at[k], 1)

        def shift(y, _):
            row = lax.broadcasted_iota(jnp.int32, (cells, 256), 0)
            for x in range(nx):
                for y2 in range(2):
                    at = (x + 1, 2 * y + y2 + 1)
                    grad = gpc_ref[x, y, y2].astype(F32)
                    after = jnp.where(row < cells - 1, pltpu.roll(grad, cells - 1, 0), 0.0)
                    before = jnp.where(row > 0, pltpu.roll(grad, 1, 0), 0.0)
                    gs[(0,) + at] = after.astype(BF)
                    gs[(1,) + at] = grad.astype(BF)
                    gs[(2,) + at] = before.astype(BF)
            return 0

        lax.fori_loop(0, ny, shift, 0)

    i, j, k = step // 9, lax.rem(step // 3, 3), lax.rem(step, 3)
    block = gs[k, pl.ds(2 - i, nx), pl.ds(2 - j, 2 * ny)].reshape(count, 256)
    wc_out[0] = dot(cells_t[...], block)


VMEM = pl.BlockSpec(memory_space=pltpu.VMEM)


def call(kernel, outs, args, scratch=(), collective=None):
    params = dict(vmem_limit_bytes=56 * 1024 * 1024)
    if collective is not None:
        params.update(collective_id=collective, has_side_effects=True)
    return pl.pallas_call(
        kernel,
        out_shape=[jax.ShapeDtypeStruct(shape, kind) for shape, kind in outs],
        in_specs=[VMEM] * len(args),
        out_specs=[VMEM] * len(outs),
        scratch_shapes=list(scratch),
        compiler_params=pltpu.CompilerParams(**params),
    )(*args)


def dma(count):
    return pltpu.SemaphoreType.DMA((count,))


def exchange(sizes, cells, edges, hx, ht, collective):
    planes, tiles, chans, _ = cells.shape
    return call(
        functools.partial(halo_kernel, sizes, hx, ht),
        [
            ((planes + 2 * hx, tiles + 2 * ht, chans, LANES), BF),
            ((3, 3, chans, LANES), BF),
            ((3, 3, chans, LANES), BF),
        ],
        [cells, edges],
        [dma(26), dma(26)],
        collective,
    )


def gather(sizes, cells, collective):
    nx, ny, nz = sizes
    return call(
        functools.partial(gather_kernel, sizes),
        [((ny, nx, 8 * nz, LANES), BF)],
        [cells],
        [pltpu.VMEM((nx, 8 * nz, LANES), F32), dma(nx * nz), dma(nx * nz), dma(ny), dma(ny)],
        collective,
    )[0]


def reduce_all(sizes, pay, collective):
    nx, ny, nz = sizes
    parts = nx * nz
    rows = pay.shape[0] // parts
    out = call(
        functools.partial(reduce_kernel, sizes),
        [((parts, rows, LANES), F32)],
        [pay.reshape(parts, rows, LANES)],
        [
            pltpu.VMEM((parts, rows, LANES), F32),
            pltpu.VMEM((ny, rows, LANES), F32),
            dma(parts),
            dma(parts),
            dma(ny),
            dma(ny),
            dma(parts),
            dma(parts),
        ],
        collective,
    )[0]
    return out.reshape(pay.shape)


def shards(sizes, volume, w_fine, w_down, w_lift, w_coarse, w_proj, w_up, cotangent):
    nx, ny, nz = sizes
    total = 8 * nx * 16 * ny * 64 * nz
    scale = 1.0 / math.sqrt(total)
    cells = 8 * nz
    wf = jnp.transpose(w_fine, (2, 0, 1)).reshape(16, 432)
    wd = jnp.transpose(w_down, (2, 0, 1)).reshape(32, 432)
    wu = jnp.transpose(w_up, (2, 0, 1)).reshape(16, 864)
    wdt = jnp.transpose(jnp.flip(w_down, 0), (1, 0, 2)).reshape(16, 864)
    wut = jnp.transpose(jnp.flip(w_up, 0), (1, 0, 2)).reshape(32, 432)
    wp = jnp.transpose(w_proj)
    wc = w_coarse.reshape(9, 768, 256)

    rows, edges = call(arrange_kernel, [((8, 8, 16, LANES), BF), ((2, 16, LANES), BF)], [volume])
    padded, right, left = exchange(sizes, rows, edges, 1, 1, 1)
    pre, act, mg, edges, v3, ct = call(
        fine_kernel,
        [
            ((8, 8, 16, LANES), F32),
            ((8, 8, 16, LANES), BF),
            ((4, 2, 32, LANES), BF),
            ((2, 32, LANES), BF),
            ((10, 18, 48, LANES), BF),
            ((8, 8, 16, LANES), BF),
        ],
        [padded, right, left, cotangent, wf],
        [pltpu.VMEM((8 * LANES, LANES), BF)],
    )
    padded, right, left = exchange(sizes, mg, edges, 4, 1, 2)
    am, dsm, pm3n, pgr, pc = call(
        functools.partial(mid_kernel, sizes),
        [
            ((10, 14, 32, LANES), BF),
            ((6, 10, 32, LANES), BF),
            ((6, 10, 48, LANES), BF),
            ((8, 12, 16, LANES), BF),
            ((8, LANES), F32),
        ],
        [padded, right, left, wd],
        [
            pltpu.VMEM((12, 16, 48, LANES), BF),
            pltpu.VMEM((12, 16, 16, LANES), BF),
            pltpu.VMEM((10, 14, 32, LANES), BF),
        ],
    )
    pcg = gather(sizes, pc, 3)
    grid = (nx, ny, 2, cells, 256)
    dec, gj, gwu, gc, dsc, actc, alc = call(
        functools.partial(up_kernel, sizes, scale),
        [
            ((16, 8, 16, 64), BF),
            ((6, 10, 32, LANES), F32),
            ((16, 896), F32),
            ((8, LANES), F32),
            (grid, BF),
            (grid, BF),
            (grid, BF),
        ],
        [pcg, am, act, pgr, w_lift, wc, wp, wu, wut],
        [
            pltpu.VMEM((2, LANES, 256), BF),
            pltpu.VMEM((nx + 2, 2 * ny + 2, cells, 768), BF),
            pltpu.VMEM((2 * ny * cells, 256), F32),
            pltpu.VMEM((3, 4, 32, LANES), F32),
            pltpu.VMEM((10, 14, 96, LANES), BF),
            pltpu.VMEM((8, 12, 48, LANES), BF),
            pltpu.VMEM((8, 12, 16, LANES), BF),
            pltpu.VMEM((16, 16, LANES), BF),
        ],
    )
    gcg = gather(sizes, gc, 4)
    pay, gpc, gwp = call(
        functools.partial(back_kernel, sizes, scale),
        [((384, LANES), F32), (grid, BF), ((32, 256), F32)],
        [gcg, pcg, dsc, actc, gj, dsm, pm3n, ct, pre, v3, gwu, w_lift, wc, wp, wdt],
        [
            pltpu.VMEM((2, LANES, 256), BF),
            pltpu.VMEM((2, LANES, 256), BF),
            pltpu.VMEM((nx + 4, 2 * ny + 4, cells, 768), BF),
            pltpu.VMEM((12 * cells, 256), F32),
            pltpu.VMEM((3, 4, 32, LANES), F32),
            pltpu.VMEM((6, 10, 96, LANES), BF),
            pltpu.VMEM((4, 2, 16, LANES), BF),
            pltpu.VMEM((8, 8, 16, LANES), BF),
            pltpu.VMEM((16, 512), F32),
            pltpu.VMEM((32, 512), F32),
            pltpu.VMEM((2, LANES, 256), F32),
        ],
    )
    red = reduce_all(sizes, pay, 5)
    shapes = [
        (27, 256, 256),
        (27, 16, 16),
        (27, 16, 32),
        (32, 256),
        (256, 32),
        (27, 32, 16),
    ]
    specs = [pl.BlockSpec((1, 256, 256), lambda t: (t, 0, 0))] + [
        pl.BlockSpec(shape, functools.partial(lambda n, t: (0,) * n, len(shape)))
        for shape in shapes[1:]
    ]
    ins = [gpc, alc, red, gwp]
    gwc, gwf, gwd, gwl, gwp, gwu = pl.pallas_call(
        functools.partial(last_kernel, sizes),
        grid=(27,),
        out_shape=[jax.ShapeDtypeStruct(shape, F32) for shape in shapes],
        in_specs=[
            pl.BlockSpec(arg.shape, functools.partial(lambda n, t: (0,) * n, arg.ndim)) for arg in ins
        ],
        out_specs=specs,
        scratch_shapes=[
            pltpu.VMEM((256, nx * ny * 2 * cells), BF),
            pltpu.VMEM((3, nx + 2, 2 * ny + 2, cells, 256), BF),
        ],
        compiler_params=pltpu.CompilerParams(
            vmem_limit_bytes=56 * 1024 * 1024, dimension_semantics=("arbitrary",)
        ),
    )(*ins)
    return dec, gwf, gwd, gwl, gwc, gwp, gwu


def solution(mesh):
    sizes = tuple(mesh.shape[name] for name in ("gx", "gy", "gz"))
    block = P(None, "gx", "gy", "gz")
    return jax.shard_map(
        functools.partial(shards, sizes),
        mesh=mesh,
        in_specs=(block, P(), P(), P(), P(), P(), P(), block),
        out_specs=(block, P(), P(), P(), P(), P(), P()),
        check_vma=False,
    )
```

time: 693 us -> 184 us (0.27); the launches traced: 684 us -> 184 us
  waiting for transfers between devices: 322 us -> 0 us
  Pallas kernels: 0 us -> 171 us
  starting transfers between devices: 123 us -> 0 us
  local copies, waits for them, and re-layouts: 80.3 us -> 11.9 us
  blocking collectives: 56.6 us -> 0 us
  matrix products: 56.4 us -> 0 us
  other arithmetic: 28.5 us -> 0 us
  between operations: 17.7 us -> 0.72 us
    psum x2 -> x0, waiting for transfers between devices: 276 us -> none  [the longest x1 147 us: shards(): lax.psum((grad_w_fine, grad_w_down, grad_w_up, grad_w_lift, grad_w_proj),...]
    pallas_call x0 -> x11, Pallas kernels: none -> 171 us  [the longest x10 152 us: call(): pl.pallas_call(kernel, out_shape=[jax.ShapeDtypeStruct(shape, kind) for s...]
    ppermute x38 -> x0, starting transfers between devices: 123 us -> none  [the longest x19 90.5 us: padded_2(): lax.ppermute(tail, axis, [(i, (i + 1) % count) for i in range(ends)])]
    all_gather x2 -> x0, blocking collectives: 56.6 us -> none  [column_border(): column = lax.all_gather(values, 'gy', axis=1, tiled=True)]
    dot_general x105 -> x0, matrix products: 56.4 us -> none  [the longest x45 26.1 us: apply_taps(): jnp.einsum('kcxyz,kco->oxyz', stacked, tap_weights, preferred_element_typ...]
    ppermute x38 -> x0, waiting for transfers between devices: 45.6 us -> none  [the longest x19 43.2 us: padded_2(): lax.ppermute(head, axis, [((i + 1) % count, i) for i in range(ends)])]
    unnamed x382 -> x7, local copies, waits for them, and re-layouts: 41 us -> 5.23 us
    reduce_sum x5 -> x0, other arithmetic: 10.3 us -> none  [pool_sum(): return jnp.sum(shaped, axis=(2, 4, 6))]
  transfers between devices with their start and end apart: 40 -> 0, of which waited for: 18 -> 0; matrix products, arithmetic and copies ran while one was open for 8% -> 0% of each run, Pallas kernels for 0% -> 0%
where the time goes in v1:
time: 184 us
  Pallas kernels  171 us (93%)
  local copies, waits for them, and re-layouts  11.9 us (6%)
    pallas_call x10, Pallas kernels, call(): pl.pallas_call(kernel, out_shape=[jax.ShapeDtypeStruct(shape, kind) for s...  152 us
    pallas_call x1, Pallas kernels, shards(): pl.pallas_call(functools.partial(last_kernel, sizes), grid=(27,), out_sha...  19.2 us
    unnamed x7, local copies, waits for them, and re-layouts  5.23 us

profile of v1, /device:TPU:1, one launch (start us, length us, event | category | flops | bytes accessed | tf_op | source)
XLA Modules:
  0.0 183.8 jit_solution(803281035118894772)
XLA Ops:
  0.6 0.0 copy-start.1
  0.6 3.2 %shard_map.135 = (bf16[8,8,16,128]{3,2,1,0:T(8,128)(2,1)}, bf16[2,16,128]{2,1,0:T(8,128)(2,1)}) custom-call(bf16[16,8,16,64]{3,2,1,0:T(8,128)(2,1)} %vol_ref.1), custom_call_target="tpu_custom_call" | custom-call | tf_op jit(solution)/shard_map/pallas_call | solution.py:904
  3.8 11.6 %shard_map.136 = (bf16[10,10,16,128]{3,2,1,0:T(8,128)(2,1)}, bf16[3,3,16,128]{3,2,1,0:T(8,128)(2,1)}, bf16[3,3,16,128]{3,2,1,0:T(8,128)(2,1)}) custom-call(bf16[8,8,16,128]{3,2,1,0:T(8,128)(2,1)} %get-tuple-element.42.a_ref, bf16[2,16,128]{2,1,0:T(8,128)(2,1)} %get-tuple-element.43.e_ref), custom_call_target="tpu_custom_call" | custom-call | tf_op jit(solution)/shard_map/pallas_call | solution.py:904
  15.4 1.0 copy.23
  16.4 0.8 reshape.38.wf_ref
  17.2 10.1 %shard_map.137 = (f32[8,8,16,128]{3,2,1,0:T(8,128)}, bf16[8,8,16,128]{3,2,1,0:T(8,128)(2,1)}, bf16[4,2,32,128]{3,2,1,0:T(8,128)(2,1)}, bf16[2,32,128]{2,1,0:T(8,...) custom-call(bf16[10,10,16,128]{3,2,1,0:T(8,128)(2,1)} %get-tuple-element.44.p_ref, ...), custom_call_target="tpu_custom_call" | custom-call | tf_op jit(solution)/shard_map/pallas_call | solution.py:904
  27.3 8.9 %shard_map.138 = (bf16[12,4,32,128]{3,2,1,0:T(8,128)(2,1)}, bf16[3,3,32,128]{3,2,1,0:T(8,128)(2,1)}, bf16[3,3,32,128]{3,2,1,0:T(8,128)(2,1)}) custom-call(bf16[4,2,32,128]{3,2,1,0:T(8,128)(2,1)} %get-tuple-element.47.a_ref, bf16[2,32,128]{2,1,0:T(8,128)(2,1)} %get-tuple-element.48.e_ref), custom_call_target="tpu_custom_call" | custom-call | tf_op jit(solution)/shard_map/pallas_call | solution.py:904
  36.2 1.6 copy.24.wd_ref
  37.8 10.7 %shard_map.139 = (bf16[10,14,32,128]{3,2,1,0:T(8,128)(2,1)}, bf16[6,10,32,128]{3,2,1,0:T(8,128)(2,1)}, bf16[6,10,48,128]{3,2,1,0:T(8,128)(2,1)}, bf16[8,12,16,128]{3,2,1,0:T(8,128)(2,1)}, f32[8,128]{1,0:T(8,128)}) custom-call(bf16[12,4,32,128]{3,2,1,0:T(8,128)(2,1)} %get-tuple-element.49.p_ref, bf16[3,3,32,128]{3,2,1,0:T(8,128)(2,1)} %get-tuple-element.50.er_ref, ...), custom_call_target="tpu_custom_call" | custom-call | tf_op jit(solution)/shard_map/pallas_call | solution.py:904
  48.5 0.0 copy-start
  48.5 22.1 %shard_map.140.pcg_ref = bf16[8,4,32,128]{3,2,1,0:T(8,128)(2,1)} custom-call(f32[8,128]{1,0:T(8,128)} %get-tuple-element.52.g_ref), custom_call_target="tpu_custom_call" | custom-call | tf_op jit(solution)/shard_map/pallas_call | solution.py:904
  70.6 0.9 copy.25
  71.6 0.8 reshape.41.wu_ref
  72.4 0.0 copy-done.1
  72.4 0.7 copy.26.wut_ref
  73.1 27.4 %shard_map.141 = (bf16[16,8,16,64]{3,2,1,0:T(8,128)(2,1)}, f32[6,10,32,128]{3,2,1,0:T(8,128)}, f32[16,896]{1,0:T(8,128)}, f32[8,128]{1,0:T(8,128)}, bf16[4,8,2,3...) custom-call(bf16[8,4,32,128]{3,2,1,0:T(8,128)(2,1)} %shard_map.140.pcg_ref, ...), custom_call_target="tpu_custom_call" | custom-call | tf_op jit(solution)/shard_map/pallas_call | solution.py:904
  100.5 16.4 %shard_map.142.gcg_ref = bf16[8,4,32,128]{3,2,1,0:T(8,128)(2,1)} custom-call(f32[8,128]{1,0:T(8,128)} %get-tuple-element.57.g_ref), custom_call_target="tpu_custom_call" | custom-call | tf_op jit(solution)/shard_map/pallas_call | solution.py:904
  116.9 0.0 copy-done
  117.0 0.8 reshape.43.wdt_ref
  117.8 21.4 %shard_map.143 = (f32[384,128]{1,0:T(8,128)}, bf16[4,8,2,32,256]{4,3,2,1,0:T(8,128)(2,1)}, f32[32,256]{1,0:T(8,128)}) custom-call(bf16[8,4,32,128]{3,2,1,0:T(8,128)(2,1)} %shard_map.142.gcg_ref, bf16[8,4,32,128]{3,2,1,0:T(8,128)(2,1)} %shard_map.140.pcg_ref, bf16[4,8,2,32,256]{4,3,2,1,0:T(8,128)(2,1)} %get-tuple-element.58.dsc_ref, ...), custom_call_target="tpu_custom_call" | custom-call | tf_op jit(solution)/shard_map/pallas_call | solution.py:904
  139.2 20.2 %shard_map.144 = f32[16,24,128]{2,1,0:T(8,128)} custom-call(f32[16,24,128]{2,1,0:T(8,128)} %bitcast.20), custom_call_target="tpu_custom_call" | custom-call | tf_op jit(solution)/shard_map/pallas_call | solution.py:904
  159.4 19.2 %shard_map.145 = (f32[27,256,256]{2,1,0:T(8,128)}, f32[27,16,16]{2,1,0:T(8,128)}, f32[27,16,32]{2,1,0:T(8,128)}, f32[32,256]{1,0:T(8,128)}, f32[256,32]{1,0:T(8,128)}, /*index=5*/f32[27,32,16]{2,1,0:T(8,128)}) custom-call(bf16[4,8,2,32,256]{4,3,2,1,0:T(8,128)(2,1)} %get-tuple-element.67.gpc_ref, bf16[4,8,2,32,256]{4,3,2,1,0:T(8,128)(2,1)} %get-tuple-element.68.alc_ref, ...), custom_call_target="tpu_custom_call" | custom-call | tf_op jit(solution)/shard_map/pallas_call | solution.py:1070
  178.6 1.9 %copy.30 = f32[27,32,16]{1,2,0:T(8,128)} copy(f32[27,32,16]{2,1,0:T(8,128)} %get-tuple-element.90) | data formatting | bytes 110592
  180.5 1.8 copy.28
  182.2 1.6 copy.29
  (3 shorter events, 0.1 us)
Async XLA Ops:
  0.6 71.7 %copy-start.1 = (bf16[27,32,16]{1,2,0:T(8,128)(2,1)S(1)}, bf16[27,32,16]{1,2,0:T(8,128)(2,1)}, u32[]{:S(2)}) copy-start(bf16[27,32,16]{1,2,0:T(8,128)(2,1)} %param.14) | copy-start | bytes 82948
  48.5 68.4 %copy-start = (bf16[27,16,32]{2,1,0:T(8,128)(2,1)S(1)}, bf16[27,16,32]{2,1,0:T(8,128)(2,1)}, u32[]{:S(2)}) copy-start(bf16[27,16,32]{2,1,0:T(8,128)(2,1)} %param.10) | copy-start | bytes 82948

commit v2 on v1

v2 whole, which is shorter than its diff:
```python
import functools
import math

import jax
import jax.numpy as jnp
from jax import lax
from jax.experimental import pallas as pl
from jax.experimental.pallas import tpu as pltpu
from jax.sharding import PartitionSpec as P

BF = jnp.bfloat16
F32 = jnp.float32
MESH = pl.DeviceIdType.MESH
LANES = 128


def dot(left, right):
    return jnp.dot(left, right, preferred_element_type=F32)


def dot_nt(left, right):
    return lax.dot_general(left, right, (((1,), (1,)), ((), ())), preferred_element_type=F32)


def dot_tn(left, right):
    return lax.dot_general(left, right, (((0,), (0,)), ((), ())), preferred_element_type=F32)


def sigmoid(values):
    return 0.5 * jnp.tanh(0.5 * values) + 0.5


def slope(values, sig):
    return sig * (1.0 + values * (1.0 - sig))


def lane_of(rows):
    return lax.broadcasted_iota(jnp.int32, (rows, LANES), 1)


def turn(tile, by):
    if isinstance(by, int):
        by = by % LANES
        return tile if by == 0 else pltpu.roll(tile, by, 1)
    return pltpu.roll(tile, lax.rem(by + 4 * LANES, LANES), 1)


def tap_rows(pair):
    return jnp.concatenate([turn(pair, 1), pair, turn(pair, -1)], axis=0)


def between(lower, upper):
    lane = lane_of(lower.shape[0])
    return jnp.where(lane < 64, turn(lower, 64), turn(upper, 64))


def store_taps(ref, x, pairs):
    stacks = [tap_rows(pair) for pair in pairs]
    for n, stack in enumerate(stacks):
        ref[x, 2 * n] = stack.astype(BF)
        if n + 1 < len(stacks):
            ref[x, 2 * n + 1] = between(stack, stacks[n + 1]).astype(BF)


def three(ref, x, y):
    block = ref[x, pl.ds(y, 3)]
    return block.reshape(3 * block.shape[1], LANES)


def conv(weight, ref, planes, starts):
    outs = weight.shape[0] // 3
    parts = []
    for x in range(planes + 2):
        tiles = [three(ref, x, y) for y in starts]
        block = tiles[0] if len(tiles) == 1 else jnp.concatenate(tiles, axis=1)
        parts.append(dot(weight, block))
        if x >= 2:
            yield (
                x - 2,
                parts[x - 2][:outs] + parts[x - 1][outs : 2 * outs] + parts[x][2 * outs :],
            )


def pool_matrix():
    row = lax.broadcasted_iota(jnp.int32, (8 * LANES, LANES), 0)
    col = lax.broadcasted_iota(jnp.int32, (8 * LANES, LANES), 1)
    hit = (row // 256 == col // 32) & (row % 64 // 2 == col % 32)
    return jnp.where(hit, 1.0, 0.0).astype(BF)


def pool_tile(ref, sums, x, half):
    cells = jnp.concatenate([ref[2 * x + a, 4 * half + q] for q in range(4) for a in range(2)], axis=1)
    return dot(cells, sums)


def grow_matrix():
    row = lax.broadcasted_iota(jnp.int32, (LANES, 2 * LANES), 0)
    col = lax.broadcasted_iota(jnp.int32, (LANES, 2 * LANES), 1)
    hit = (row // 64 == col // LANES) & (row % 64 - 8 == col % 64 // 2)
    return jnp.where(hit, 1.0, 0.0).astype(BF)


def coarse_sum_matrix(tiles):
    row = lax.broadcasted_iota(jnp.int32, (8, tiles * LANES), 0)
    cell = lax.broadcasted_iota(jnp.int32, (8, tiles * LANES), 1) % 64 - 8
    return (cell >= 0) & (cell < 32) & ((cell + 4) // 4 == row + 1)


def coarse_grow_matrix(cells, gz):
    row = lax.broadcasted_iota(jnp.int32, (cells, LANES), 0)
    cell = lax.broadcasted_iota(jnp.int32, (cells, LANES), 1) % 64 - 8
    mid = cell + gz * 32
    hit = (cell >= -3) & (cell < 35) & (mid >= 0) & (row == (mid + 4) // 4 - 1)
    return jnp.where(hit, 1.0, 0.0).astype(BF)


def plane_rows(block):
    rows = jnp.swapaxes(block, 0, 1)
    return [jnp.concatenate([rows[2 * t], rows[2 * t + 1]], axis=1) for t in range(8)]


def place_weight(ref, weight):
    for y2 in range(2):
        ref[y2] = jnp.zeros((LANES, 256), BF)
        ref[y2, pl.ds(32 * y2, 32)] = weight


def store_coarse_taps(ref, at, cells):
    count = cells.shape[0]
    row = lax.broadcasted_iota(jnp.int32, cells.shape, 0)
    before = jnp.where(row > 0, pltpu.roll(cells, 1, 0), 0.0)
    after = jnp.where(row < count - 1, pltpu.roll(cells, count - 1, 0), 0.0)
    ref[at + (slice(None), pl.ds(0, 256))] = before.astype(BF)
    ref[at + (slice(None), pl.ds(256, 256))] = cells.astype(BF)
    ref[at + (slice(None), pl.ds(512, 256))] = after.astype(BF)


def zero_rim(ref, rim):
    planes, rows = ref.shape[:2]

    def clear(x, _):
        for y in list(range(rim)) + list(range(rows - rim, rows)):
            ref[x, y] = jnp.zeros(ref.shape[2:], ref.dtype)
        return 0

    lax.fori_loop(0, planes, clear, 0)

    def clear_plane(y, _):
        for x in list(range(rim)) + list(range(planes - rim, planes)):
            ref[x, y] = jnp.zeros(ref.shape[2:], ref.dtype)
        return 0

    lax.fori_loop(0, rows, clear_plane, 0)


def clamp(at, count):
    return jnp.minimum(jnp.maximum(at, 0), count - 1)


def near_cells(sizes):
    nx, ny, _ = sizes
    gx, gy = lax.axis_index("gx"), lax.axis_index("gy")
    found = []
    for dx in range(3):
        for dy in range(4):
            x, y = gx - 1 + dx, gy + (dy + 1) // 2 - 1
            there = (x >= 0) & (x < nx) & (y >= 0) & (y < ny)
            keep = jnp.where(there, 1.0, 0.0)
            found.append((dx, dy, clamp(x, nx), clamp(y, ny), (dy + 1) % 2, keep))
    return found


def nothing():
    pass


def halo_round(sizes, hx, ht, refs, work, meanwhile):
    a_ref, e_ref, p_ref, er_ref, el_ref, send_sem, recv_sem = refs
    me = [lax.axis_index(name) for name in ("gx", "gy", "gz")]
    planes, tiles = a_ref.shape[:2]

    def there(at, step):
        if step == 0:
            return None
        return at[0] > 0 if step < 0 else at[0] < at[1] - 1

    def valid(steps):
        found = None
        for axis, step in enumerate(steps):
            test = there((me[axis], sizes[axis]), step)
            if test is not None:
                found = test if found is None else found & test
        return found

    def part(step, halo, count):
        if step == 0:
            return pl.ds(0, count), pl.ds(halo, count)
        if step > 0:
            return pl.ds(count - halo, halo), pl.ds(0, halo)
        return pl.ds(0, halo), pl.ds(count + halo, halo)

    steps_all = [
        (dx, dy, dz)
        for dz in (-1, 1, 0)
        for dx in (-1, 0, 1)
        for dy in (-1, 0, 1)
        if (dx, dy, dz) != (0, 0, 0)
    ]

    def copy_of(k, steps):
        dx, dy, dz = steps
        if dz == 0:
            fx, tx = part(dx, hx, planes)
            fy, ty = part(dy, ht, tiles)
            src, dst = a_ref.at[fx, fy], p_ref.at[tx, ty]
        elif dz > 0:
            src, dst = e_ref.at[1], el_ref.at[1 - dx, 1 - dy]
        else:
            src, dst = e_ref.at[0], er_ref.at[1 - dx, 1 - dy]
        return pltpu.make_async_remote_copy(
            src_ref=src,
            dst_ref=dst,
            send_sem=send_sem.at[k],
            recv_sem=recv_sem.at[k],
            device_id=(me[0] + dx, me[1] + dy, me[2] + dz),
            device_id_type=MESH,
        )

    barrier = pltpu.get_barrier_semaphore()
    total = 1
    for axis in range(3):
        low = jnp.where(me[axis] > 0, 1, 0)
        high = jnp.where(me[axis] < sizes[axis] - 1, 1, 0)
        total = total * (1 + low + high)
    for steps in steps_all:

        @pl.when(valid(steps))
        def _():
            pl.semaphore_signal(
                barrier,
                inc=1,
                device_id=tuple(me[axis] + steps[axis] for axis in range(3)),
                device_id_type=MESH,
            )

    work()
    pl.semaphore_wait(barrier, total - 1)

    for k, steps in enumerate(steps_all):

        @pl.when(valid(steps))
        def _():
            copy_of(k, steps).start()

    p_ref[pl.ds(hx, planes), pl.ds(ht, tiles)] = a_ref[...]
    for k, steps in enumerate(steps_all):
        back = tuple(-step for step in steps)
        dx, dy, dz = steps

        @pl.when(jnp.logical_not(valid(back)))
        def _():
            if dz == 0:
                _, tx = part(dx, hx, planes)
                _, ty = part(dy, ht, tiles)
                into = p_ref.at[tx, ty]
            elif dz > 0:
                into = el_ref.at[1 - dx, 1 - dy]
            else:
                into = er_ref.at[1 - dx, 1 - dy]
            into[...] = jnp.zeros(into.shape, into.dtype)

    meanwhile()
    for k, steps in enumerate(steps_all):
        back = tuple(-step for step in steps)

        @pl.when(valid(back))
        def _():
            copy_of(k, steps).wait_recv()

    for k, steps in enumerate(steps_all):

        @pl.when(valid(steps))
        def _():
            copy_of(k, steps).wait_send()


def plane_peers(nx, nz):
    return [(ox, oz) for ox in range(nx) for oz in range(nz) if (ox, oz) != (0, 0)]


def greet(peers, work):
    barrier = pltpu.get_barrier_semaphore()
    for peer in peers:
        pl.semaphore_signal(barrier, inc=1, device_id=peer, device_id_type=MESH)
    work()
    pl.semaphore_wait(barrier, len(peers))


def gather_round(sizes, refs, work, first_wait, second_wait):
    g_ref, all_ref, stage, send_a, recv_a, send_b, recv_b = refs
    nx, ny, nz = sizes
    gx, gy, gz = [lax.axis_index(name) for name in ("gx", "gy", "gz")]
    plane = plane_peers(nx, nz)
    greet(
        [(lax.rem(gx + ox, nx), gy, lax.rem(gz + oz, nz)) for ox, oz in plane]
        + [(gx, lax.rem(gy + oy, ny), gz) for oy in range(1, ny)],
        work,
    )

    def first(k, x, z, peer):
        return pltpu.make_async_remote_copy(
            src_ref=g_ref,
            dst_ref=stage.at[x, pl.ds(pl.multiple_of(z * 8, 8), 8)],
            send_sem=send_a.at[k],
            recv_sem=recv_a.at[k],
            device_id=peer,
            device_id_type=MESH,
        )

    def second(oy, y):
        return pltpu.make_async_remote_copy(
            src_ref=all_ref.at[gy],
            dst_ref=all_ref.at[y],
            send_sem=send_b.at[oy],
            recv_sem=recv_b.at[oy],
            device_id=(gx, lax.rem(gy + oy, ny), gz),
            device_id_type=MESH,
        )

    for k, (ox, oz) in enumerate(plane):
        first(k, gx, gz, (lax.rem(gx + ox, nx), gy, lax.rem(gz + oz, nz))).start()
    stage[gx, pl.ds(pl.multiple_of(gz * 8, 8), 8)] = g_ref[...]
    first_wait()
    for k, (ox, oz) in enumerate(plane):
        peer = (lax.rem(gx + ox, nx), gy, lax.rem(gz + oz, nz))
        first(k, lax.rem(gx + nx - ox, nx), lax.rem(gz + nz - oz, nz), peer).wait_recv()
    all_ref[gy] = stage[...].astype(BF)
    for oy in range(1, ny):
        second(oy, gy).start()
    second_wait()
    for k, (ox, oz) in enumerate(plane):
        first(k, gx, gz, (lax.rem(gx + ox, nx), gy, lax.rem(gz + oz, nz))).wait_send()
    for oy in range(1, ny):
        second(oy, lax.rem(gy + ny - oy, ny)).wait_recv()
    for oy in range(1, ny):
        second(oy, gy).wait_send()


def reduce_round(sizes, refs, work, waits):
    pay_ref, out_ref, ra, rb, send_a, recv_a, send_b, recv_b, send_c, recv_c = refs
    nx, ny, nz = sizes
    gx, gy, gz = [lax.axis_index(name) for name in ("gx", "gy", "gz")]
    mine = gx * nz + gz
    plane = plane_peers(nx, nz)
    greet(
        [(lax.rem(gx + ox, nx), gy, lax.rem(gz + oz, nz)) for ox, oz in plane]
        + [(gx, lax.rem(gy + oy, ny), gz) for oy in range(1, ny)],
        work,
    )

    def ahead(ox, oz):
        return lax.rem(gx + ox, nx), lax.rem(gz + oz, nz)

    def behind(ox, oz):
        return lax.rem(gx + nx - ox, nx), lax.rem(gz + nz - oz, nz)

    def scatter(k, ox, oz, slot):
        x, z = ahead(ox, oz)
        return pltpu.make_async_remote_copy(
            src_ref=pay_ref.at[x * nz + z],
            dst_ref=ra.at[slot],
            send_sem=send_a.at[k],
            recv_sem=recv_a.at[k],
            device_id=(x, gy, z),
            device_id_type=MESH,
        )

    def across(oy, slot):
        return pltpu.make_async_remote_copy(
            src_ref=rb.at[gy],
            dst_ref=rb.at[slot],
            send_sem=send_b.at[oy],
            recv_sem=recv_b.at[oy],
            device_id=(gx, lax.rem(gy + oy, ny), gz),
            device_id_type=MESH,
        )

    def spread(k, ox, oz, slot):
        x, z = ahead(ox, oz)
        return pltpu.make_async_remote_copy(
            src_ref=out_ref.at[mine],
            dst_ref=out_ref.at[slot],
            send_sem=send_c.at[k],
            recv_sem=recv_c.at[k],
            device_id=(x, gy, z),
            device_id_type=MESH,
        )

    for k, (ox, oz) in enumerate(plane):
        scatter(k, ox, oz, mine).start()
    ra[mine] = pay_ref[mine]
    waits[0]()
    for k, (ox, oz) in enumerate(plane):
        x, z = behind(ox, oz)
        scatter(k, ox, oz, x * nz + z).wait_recv()
    rb[gy] = jnp.sum(ra[...], axis=0)
    for oy in range(1, ny):
        across(oy, gy).start()
    waits[1]()
    for k, (ox, oz) in enumerate(plane):
        scatter(k, ox, oz, mine).wait_send()
    for oy in range(1, ny):
        across(oy, lax.rem(gy + ny - oy, ny)).wait_recv()
    out_ref[mine] = jnp.sum(rb[...], axis=0)
    for k, (ox, oz) in enumerate(plane):
        spread(k, ox, oz, mine).start()
    waits[2]()
    for oy in range(1, ny):
        across(oy, gy).wait_send()
    for k, (ox, oz) in enumerate(plane):
        x, z = behind(ox, oz)
        spread(k, ox, oz, x * nz + z).wait_recv()
    for k, (ox, oz) in enumerate(plane):
        spread(k, ox, oz, mine).wait_send()


def fold(ref, weight):
    ins, outs = weight.shape[1:]
    for i in range(3):
        block = weight[9 * i : 9 * i + 9].astype(F32).reshape(9 * ins, outs)
        ref[pl.ds(i * outs, outs)] = block.T.astype(BF)


def fold_back(ref, weight):
    outs, ins = weight.shape[1:]
    for i in range(3):
        parts = [weight[26 - 9 * i - jk].astype(F32).T for jk in range(9)]
        ref[pl.ds(i * outs, outs)] = jnp.concatenate(parts, axis=0).T.astype(BF)


def arrange_kernel(
    sizes,
    vol_ref,
    cot_ref,
    wf_ref,
    wd_ref,
    wu_ref,
    wp_ref,
    p_ref,
    er_ref,
    el_ref,
    ct_ref,
    pg_ref,
    wf_out,
    wd_out,
    wu_out,
    wdt_out,
    wut_out,
    wp_out,
    v_ref,
    e_ref,
    send,
    recv,
):
    def work():
        spot = lane_of(16) % 64

        def plane(x, edges):
            low, high = edges
            for t, tile in enumerate(plane_rows(vol_ref[:, x])):
                v_ref[x, t] = tile
                wide = tile.astype(F32)
                at = t * 8 + x
                low = jnp.where(spot == at, turn(wide, at), low)
                high = jnp.where(spot == at, turn(wide, at - 63), high)
            return low, high

        zero = jnp.zeros((16, LANES), F32)
        low, high = lax.fori_loop(0, 8, plane, (zero, zero))
        e_ref[0] = low.astype(BF)
        e_ref[1] = high.astype(BF)

    def meanwhile():
        def plane(x, _):
            for t, tile in enumerate(plane_rows(cot_ref[:, x])):
                ct_ref[x, t] = tile
            return 0

        lax.fori_loop(0, 8, plane, 0)
        sums = pool_matrix()

        for x in range(4):
            for half in range(2):
                pg_ref[x, half] = pool_tile(ct_ref, sums, x, half).astype(BF)

        fold(wf_out, wf_ref[...])
        fold(wd_out, wd_ref[...])
        fold(wu_out, wu_ref[...])
        fold_back(wdt_out, wd_ref[...])
        fold_back(wut_out, wu_ref[...])
        wp_out[...] = wp_ref[...].astype(F32).T.astype(BF)

    halo_round(sizes, 1, 1, (v_ref, e_ref, p_ref, er_ref, el_ref, send, recv), work, meanwhile)


def fine_kernel(
    sizes,
    p_ref,
    er_ref,
    el_ref,
    pg_ref,
    wf_ref,
    pre_ref,
    act_ref,
    v3_ref,
    p2_ref,
    er2_ref,
    el2_ref,
    mg_ref,
    e_ref,
    send,
    recv,
):
    def work():
        spot = lane_of(16) % 64

        def rows(x, _):
            dx, sx = (x + 7) // 8, lax.rem(x + 7, 8)
            stacks = []
            for t in range(10):
                dy, sy = (t + 7) // 8, (t + 7) % 8
                at = sy * 8 + sx
                tile = p_ref[x, t].astype(F32)
                left = turn(el_ref[dx, dy].astype(F32), -at)
                right = turn(er_ref[dx, dy].astype(F32), 63 - at)
                before = jnp.where(spot == 0, left, turn(tile, 1))
                after = jnp.where(spot == 63, right, turn(tile, -1))
                stacks.append(jnp.concatenate([before, tile, after], axis=0))
            for t in range(9):
                if t > 0:
                    v3_ref[x, 2 * t - 1] = stacks[t].astype(BF)
                v3_ref[x, 2 * t] = between(stacks[t], stacks[t + 1]).astype(BF)
            return 0

        lax.fori_loop(0, 10, rows, 0)
        weight = wf_ref[...]

        def convs(g, _):
            for x, pre in conv(weight, v3_ref, 8, (4 * g, 4 * g + 2)):
                act = (pre * sigmoid(pre)).astype(BF)
                for b in range(2):
                    pre_ref[x, 2 * g + b] = pre[:, b * LANES : (b + 1) * LANES]
                    act_ref[x, 2 * g + b] = act[:, b * LANES : (b + 1) * LANES]
            return 0

        lax.fori_loop(0, 4, convs, 0)

        sums = pool_matrix()
        lane = lane_of(32)
        low = jnp.zeros((32, LANES), F32)
        high = low
        for x in range(4):
            for half in range(2):
                pooled = (pool_tile(act_ref, sums, x, half) * 0.125).astype(BF)
                tile = jnp.concatenate([pooled, pg_ref[x, half]], axis=0)
                mg_ref[x, half] = tile
                wide = tile.astype(F32)
                for q in range(4):
                    at = (q % 2) * 64 + (x * 4 + 2 * half + q // 2) * 4
                    here = (lane >= at) & (lane < at + 4)
                    low = jnp.where(here, turn(wide, at - 32 * q), low)
                    high = jnp.where(here, turn(wide, at - 32 * q - 28), high)
        e_ref[0] = low.astype(BF)
        e_ref[1] = high.astype(BF)

    halo_round(sizes, 4, 1, (mg_ref, e_ref, p2_ref, er2_ref, el2_ref, send, recv), work, nothing)


def mid_kernel(
    sizes,
    p_ref,
    er_ref,
    el_ref,
    wd_ref,
    am_ref,
    dsm_ref,
    pm3n_ref,
    pgr_ref,
    pcg_ref,
    pm3,
    pgf,
    dsf,
    pc,
    stage,
    send_a,
    recv_a,
    send_b,
    recv_b,
):
    gx, gy, gz = [lax.axis_index(name) for name in ("gx", "gy", "gz")]
    nx, ny, nz = sizes

    def work():
        lane = lane_of(32)
        spot = lane % 64

        def rows(x, _):
            dx, sx = x // 4, lax.rem(x, 4)
            pairs = []
            for a in range(8):
                dy, sy = (a + 2) // 4, (a + 2) % 4
                tile = p_ref[x, a // 2].astype(F32)
                q = 2 * (a % 2)
                base = jnp.where(lane < 64, turn(tile, 8 - 32 * q), turn(tile, 40 - 32 * q))
                at = (sx * 4 + sy) * 4
                right = turn(er_ref[dx, dy].astype(F32), 40 - at)
                left = turn(el_ref[dx, dy].astype(F32), 4 - at)
                row = jnp.where(spot < 44, right, 0.0)
                row = jnp.where(spot < 40, base, row)
                row = jnp.where(spot < 8, left, row)
                row = jnp.where(spot < 4, 0.0, row)
                pgf[x, a] = row[16:].astype(BF)
                pairs.append(row[:16])
            store_taps(pm3, x, pairs)
            pm3[x, 15] = jnp.zeros((48, LANES), BF)
            pm3[x, 16] = jnp.zeros((48, LANES), BF)
            return 0

        lax.fori_loop(0, 12, rows, 0)
        weight = wd_ref[...]
        cell = spot - 8
        mid = cell + gz * 32
        inside = (cell >= -3) & (cell < 35) & (mid >= 0) & (mid < 32 * nz)
        second = lane // 64

        def convs(g, _):
            for x, both in conv(weight, pm3, 10, (4 * g, 4 * g + 2)):
                at_x = gx * 4 + x - 3
                for b in range(2):
                    pre = both[:, b * LANES : (b + 1) * LANES]
                    at_y = gy * 8 + 4 * g + 2 * b - 3 + second
                    keep = inside & (at_y >= 0) & (at_y < 8 * ny)
                    keep = keep & (at_x >= 0) & (at_x < 4 * nx)
                    sig = sigmoid(pre)
                    am_ref[x, 2 * g + b] = jnp.where(keep, pre * sig, 0.0).astype(BF)
                    dsf[x, 2 * g + b] = jnp.where(keep, slope(pre, sig), 0.0).astype(BF)
            return 0

        lax.fori_loop(0, 4, convs, 0)
        halves = [
            jnp.concatenate([am_ref[3 + a, 1 + 2 * h + m] for a in range(4) for m in range(3)], axis=1)
            for h in range(2)
        ]
        cells = jnp.concatenate(halves + [jnp.zeros((64, 12 * LANES), BF)], axis=0)
        col = lax.broadcasted_iota(jnp.int32, (8, 12 * LANES), 1)
        third, upper = col // LANES % 3, col // 64 % 2
        hit = coarse_sum_matrix(12) & ((third == 1) | ((third == 0) == (upper == 1)))
        pooled = dot_nt(jnp.where(hit, 1.0, 0.0).astype(BF), cells) * (1.0 / 64.0)
        pc[...] = pooled.astype(BF).astype(F32)

    def first_wait():
        dsm_ref[...] = dsf[2:8, 1:6]
        pm3n_ref[...] = pm3[3:9, 3:12]
        pgr_ref[...] = pgf[2:10, 1:7]

    gather_round(
        sizes, (pc, pcg_ref, stage, send_a, recv_a, send_b, recv_b), work, first_wait, nothing
    )


def up_kernel(
    sizes,
    scale,
    pcg_ref,
    am_ref,
    act_ref,
    pgr_ref,
    wl_ref,
    wc_ref,
    wp_ref,
    wu_ref,
    wut_ref,
    dec_ref,
    gj_ref,
    gwu_ref,
    gcg_ref,
    dsc_ref,
    actc_ref,
    alc_ref,
    wide_lift,
    al3,
    acc,
    cos,
    j3,
    guo,
    gu3,
    su,
    plane,
    gc,
    stage,
    send_a,
    recv_a,
    send_b,
    recv_b,
):
    nx, ny, nz = sizes
    gy, gz = lax.axis_index("gy"), lax.axis_index("gz")
    cells = 8 * nz

    def lift(o, _):
        y = lax.rem(gy + o + 4 * ny - 2, ny)
        for x in range(nx):
            for y2 in range(2):
                pre = dot(pcg_ref[y, x], wide_lift[y2])
                act = (pre * sigmoid(pre)).astype(BF)
                alc_ref[x, y, y2] = act
                store_coarse_taps(al3, (x + 1, 2 * y + y2 + 1), act.astype(F32))
        return 0

    def coarse(o, _):
        y = lax.rem(gy + o + ny - 1, ny)
        for i in range(3):
            for j in range(3):
                block = al3[pl.ds(i, nx), pl.ds(2 * y + j, 2)].reshape(nx * 2 * cells, 768)
                part = dot(block, wc_ref[3 * i + j])
                if i + j == 0:
                    acc[...] = part
                else:
                    acc[...] += part
        pre = acc[...]
        sig = sigmoid(pre)
        act = (pre * sig).astype(BF).reshape(nx, 2, cells, 256)
        grad = slope(pre, sig).astype(BF).reshape(nx, 2, cells, 256)
        for x in range(nx):
            actc_ref[x, y] = act[x]
            dsc_ref[x, y] = grad[x]
        return 0

    def work():
        place_weight(wide_lift, wl_ref[...])
        zero_rim(al3, 1)
        lax.fori_loop(0, 5, lift, 0)
        lax.fori_loop(0, 3, coarse, 0)

        spread = coarse_grow_matrix(cells, gz)
        for dx, dy, x, y, y2, keep in near_cells(sizes):
            out = dot_nt(wp_ref[...], actc_ref[x, y, y2]).astype(BF)
            cos[dx, dy] = dot(out, spread) * keep

        first = lane_of(32) < 64

        def join(x, _):
            pairs = []
            for m in range(7):
                add = jnp.where(
                    first, cos[(x + 1) // 4, (2 * m + 1) // 4], cos[(x + 1) // 4, (2 * m + 2) // 4]
                )
                row = am_ref[x, m].astype(F32) + add
                pairs.append(row.astype(BF).astype(F32))
            store_taps(j3, x, pairs)
            return 0

        lax.fori_loop(0, 10, join, 0)

        cell = lane_of(16) % 64 - 8
        near = (cell >= -2) & (cell < 34)
        weight = wu_ref[...]

        def up(g, _):
            for x, both in conv(weight, j3, 8, (4 * g, 4 * g + 2)):
                for b in range(2):
                    pre = both[:, b * LANES : (b + 1) * LANES]
                    sig = sigmoid(pre)
                    su[x, 2 * g + b] = (pre * sig).astype(BF)
                    pooled = pgr_ref[x, 2 * g + b].astype(F32) * scale
                    guo[x, 2 * g + b] = jnp.where(near, pooled * slope(pre, sig), 0.0).astype(BF)
            return 0

        lax.fori_loop(0, 3, up, 0)

        def stack(x, _):
            store_taps(gu3, x, [guo[x, m].astype(F32) for m in range(6)])
            return 0

        lax.fori_loop(0, 8, stack, 0)

        weight_t = wut_ref[...]
        for starts in ((0, 2), (4, 6), (8,)):
            for x, both in conv(weight_t, gu3, 6, starts):
                for b, y in enumerate(starts):
                    gj_ref[x, y // 2] = both[:, b * LANES : (b + 1) * LANES]

        totals = []
        for h in range(2):
            total = None
            for a in range(4):
                lower, middle, upper = [gj_ref[1 + a, 2 * h + m] for m in range(3)]
                row = middle + jnp.where(first, upper, lower)
                total = row if total is None else total + row
            totals.append(total)
        total = jnp.concatenate(totals + [jnp.zeros((64, LANES), F32)], axis=0)
        head = total.astype(BF)
        tail = (total - head.astype(F32)).astype(BF)
        sums = jnp.where(coarse_sum_matrix(1), 1.0, 0.0).astype(BF)
        gc[...] = (dot_nt(sums, head) + dot_nt(sums, tail)).astype(BF).astype(F32)

    def first_wait():
        cell = lane_of(16) % 64 - 8
        own = (cell >= 0) & (cell < 32)
        gwu_ref[...] = jnp.zeros(gwu_ref.shape, F32)
        grads = [
            jnp.concatenate(
                [jnp.where(own, guo[x + 2, m + 1].astype(F32), 0.0) for m in range(4)], axis=1
            ).astype(BF)
            for x in range(4)
        ]
        none = jnp.zeros((16, 4 * LANES), BF)
        for x in range(6):
            left = [grads[x - i] if 0 <= x - i < 4 else none for i in range(3)]
            right = [three(j3, x + 2, 2 * m + 2) for m in range(4)]
            gwu_ref[:, pl.ds(0, 288)] += dot_nt(
                jnp.concatenate(left, axis=0), jnp.concatenate(right, axis=1)
            )

        grow = grow_matrix()

        def decode(x, _):
            rows = jnp.concatenate([su[x + 2, m + 1] for m in range(4)], axis=0)
            grown = dot(rows, grow)
            for a in range(2):
                for t in range(8):
                    add = grown[16 * (t // 2) : 16 * (t // 2) + 16, (t % 2) * LANES :][:, :LANES]
                    tile = act_ref[2 * x + a, t].astype(F32) + add
                    plane[2 * t] = tile.astype(BF)
                    plane[2 * t + 1] = turn(tile, 64).astype(BF)
                dec_ref[:, 2 * x + a] = jnp.swapaxes(plane[...], 0, 1)[:, :, :64]
            return 0

        lax.fori_loop(0, 4, decode, 0)

    def second_wait():
        lax.fori_loop(5, max(ny, 5), lift, 0)
        lax.fori_loop(3, max(ny, 3), coarse, 0)

    gather_round(
        sizes, (gc, gcg_ref, stage, send_a, recv_a, send_b, recv_b), work, first_wait, second_wait
    )


def back_kernel(
    sizes,
    scale,
    gcg_ref,
    pcg_ref,
    dsc_ref,
    actc_ref,
    alc_ref,
    gj_ref,
    dsm_ref,
    pm3n_ref,
    ct_ref,
    pre_ref,
    v3_ref,
    gwu_ref,
    wl_ref,
    wc_ref,
    wp_ref,
    wdt_ref,
    red_ref,
    gwc_ref,
    gwp_ref,
    wide_lift,
    wide_proj,
    gp3,
    acc,
    gps,
    gm3,
    gpm,
    gf,
    accf,
    accd,
    sums,
    cells_t,
    pay,
    ra,
    rb,
    send_a,
    recv_a,
    send_b,
    recv_b,
    send_c,
    recv_c,
):
    nx, ny, nz = sizes
    gx, gy, gz = [lax.axis_index(name) for name in ("gx", "gy", "gz")]
    cells = 8 * nz
    count = nx * ny * 2 * cells

    def coarse(o, _):
        y = lax.rem(gy + o + ny - 1, ny)
        for x in range(nx):
            for y2 in range(2):
                grad = dot(gcg_ref[y, x], wide_proj[y2]) * dsc_ref[x, y, y2].astype(F32)
                grad = grad.astype(BF).astype(F32)
                store_coarse_taps(gp3, (x + 2, 2 * y + y2 + 2), grad)
        return 0

    def work():
        place_weight(wide_lift, wl_ref[...])
        place_weight(wide_proj, wp_ref[...])
        zero_rim(gp3, 2)
        lax.fori_loop(0, 3, coarse, 0)
        acc[...] = jnp.zeros(acc.shape, F32)

        def coarse_back(i, _):
            for j in range(3):
                block = gp3[pl.ds(gx + i, 3), pl.ds(2 * gy + j, 4)].reshape(12 * cells, 768)
                for k in range(3):
                    weight = wc_ref[8 - 3 * i - j, pl.ds(256 * (2 - k), 256)]
                    acc[...] += dot_nt(block[:, 256 * k : 256 * (k + 1)], weight)
            return 0

        lax.fori_loop(0, 3, coarse_back, 0)

        spread = coarse_grow_matrix(cells, gz)
        own = lax.broadcasted_iota(jnp.int32, (cells, 256), 0) // 8 == gz
        for at, (dx, dy, x, y, y2, keep) in enumerate(near_cells(sizes)):
            pre = dot(pcg_ref[y, x], wide_lift[y2])
            grad = (acc[pl.ds(at * cells, cells)] * slope(pre, sigmoid(pre))).astype(BF)
            out = dot_nt(wl_ref[...], grad).astype(BF)
            gps[dx, dy] = dot(out, spread) * (keep * (1.0 / 64.0))
            if dx == 1 and dy in (1, 2):
                masked = jnp.where(own, grad.astype(F32), 0.0).astype(BF)
                sums[y2] = dot_tn(pcg_ref[y, x], masked)
        lifts = sums[0, :32] + sums[1, 32:64]
        for b in range(2):
            pay_rows(432 + 32 * b, lifts[:, b * LANES : (b + 1) * LANES])

        first = lane_of(32) < 64

        def join(x, _):
            pairs = []
            for n in range(5):
                add = jnp.where(
                    first,
                    gps[(x + 3) // 4, (2 * n + 3) // 4],
                    gps[(x + 3) // 4, (2 * n + 4) // 4],
                )
                row = (gj_ref[x, n] + add) * dsm_ref[x, n].astype(F32)
                pairs.append(row.astype(BF).astype(F32))
            store_taps(gm3, x, pairs)
            return 0

        lax.fori_loop(0, 6, join, 0)

        weight_t = wdt_ref[...]
        for starts in ((0, 2), (4, 6)):
            for x, both in conv(weight_t, gm3, 4, starts):
                for b, y in enumerate(starts):
                    tile = both[:, b * LANES : (b + 1) * LANES].astype(BF)
                    gpm[x, pl.ds(8 * y, 16)] = tile

        grow = grow_matrix()
        for x in (0, 1, 10, 11):
            gf[x] = jnp.zeros(gf.shape[1:], BF)

        def fine(x, _):
            grown = dot(gpm[x], grow) * 0.125
            for a in range(2):
                for t in range(8):
                    add = grown[16 * (t // 2) : 16 * (t // 2) + 16, (t % 2) * LANES :][:, :LANES]
                    pre = pre_ref[2 * x + a, t]
                    grad = ct_ref[2 * x + a, t].astype(F32) * scale + add
                    grad = (grad * slope(pre, sigmoid(pre))).astype(BF)
                    gf[2 * x + a + 2, :, pl.ds(t * LANES, LANES)] = grad
            return 0

        lax.fori_loop(0, 4, fine, 0)

        accd[...] = jnp.zeros(accd.shape, F32)
        spot = lane_of(32) % 64
        inner = (spot >= 8) & (spot < 40)
        grads = [
            jnp.concatenate(
                [
                    jnp.where(inner, gm3[x + 1, 2 * m + 1, pl.ds(32, 32)].astype(F32), 0.0)
                    for m in range(4)
                ],
                axis=1,
            ).astype(BF)
            for x in range(4)
        ]
        none = jnp.zeros((32, 4 * LANES), BF)
        for x in range(6):
            left = [grads[x - i] if 0 <= x - i < 4 else none for i in range(3)]
            right = [three(pm3n_ref, x, 2 * m) for m in range(4)]
            accd[:, pl.ds(0, 144)] += dot_nt(
                jnp.concatenate(left, axis=0), jnp.concatenate(right, axis=1)
            )

        accf[...] = jnp.zeros(accf.shape, F32)

        def taps_fine(x, _):
            left = jnp.concatenate([gf[x + 2 - i] for i in range(3)], axis=0)
            right = jnp.concatenate([three(v3_ref, x, 2 * t) for t in range(8)], axis=1)
            accf[:, pl.ds(0, 144)] += dot_nt(left, right)
            return 0

        lax.fori_loop(0, 10, taps_fine, 0)

        for b in range(2):
            pay_rows(48 * b, accf[:, b * LANES : (b + 1) * LANES])
        for b in range(3):
            pay_rows(96 + 48 * b, gwu_ref[:, b * LANES : (b + 1) * LANES])
        for b in range(2):
            pay_rows(240 + 96 * b, accd[:, b * LANES : (b + 1) * LANES])
        pay_rows(496, jnp.zeros((16, LANES), F32))

    def pay_rows(start, block):
        per = pay.shape[1]
        done = 0
        while done < block.shape[0]:
            part, at = divmod(start + done, per)
            size = min(per - at, block.shape[0] - done)
            pay[part, pl.ds(at, size)] = block[done : done + size]
            done += size

    def coarse_taps(t, _):
        i, j = t // 3, lax.rem(t, 3)
        block = gp3[pl.ds(3 - i, nx), pl.ds(3 - j, 2 * ny)].reshape(count, 768)
        out = dot(cells_t[...], block)
        for k in range(3):
            gwc_ref[3 * t + k] = out[:, 256 * (2 - k) : 256 * (3 - k)].astype(BF)
        return 0

    def wait_a():
        lax.fori_loop(3, max(ny, 3), coarse, 0)
        cells_t[...] = alc_ref[...].reshape(count, 256).T
        lax.fori_loop(0, 2, coarse_taps, 0)

    def wait_b():
        lax.fori_loop(2, 5, coarse_taps, 0)

    def wait_c():
        lax.fori_loop(5, 9, coarse_taps, 0)
        sums[...] = jnp.zeros(sums.shape, F32)

        def proj_grad(x, _):
            for y2 in range(2):
                grads = gcg_ref[:, x].reshape(ny * cells, LANES)
                sums[y2] += dot_tn(grads, actc_ref[x, :, y2].reshape(ny * cells, 256))
            return 0

        lax.fori_loop(0, nx, proj_grad, 0)
        gwp_ref[...] = sums[0, :32] + sums[1, 32:64]

    reduce_round(
        sizes,
        (pay, red_ref, ra, rb, send_a, recv_a, send_b, recv_b, send_c, recv_c),
        work,
        (wait_a, wait_b, wait_c),
    )


def last_kernel(gwc_ref, red_ref, gwp_ref, wc_out, wf_out, wd_out, wl_out, wp_out, wu_out):
    @pl.when(pl.program_id(0) == 0)
    def _():
        def columns(start, blocks, rows):
            return jnp.concatenate(
                [red_ref[pl.ds(start + rows * b, rows)] for b in range(blocks)], axis=1
            )

        for out, start, blocks in ((wf_out, 0, 2), (wu_out, 96, 3), (wd_out, 240, 2)):
            ins, outs = out.shape[1:]
            table = columns(start, blocks, 3 * outs)
            for i in range(3):
                part = table[i * outs : (i + 1) * outs, : 9 * ins]
                out[pl.ds(9 * i, 9)] = part.T.reshape(9, ins, outs)
        wl_out[...] = columns(432, 2, 32)
        wp_out[...] = gwp_ref[...].T

    wc_out[...] = gwc_ref[...].astype(F32)


VMEM = pl.BlockSpec(memory_space=pltpu.VMEM)


def call(kernel, outs, args, scratch, collective):
    return pl.pallas_call(
        kernel,
        out_shape=[jax.ShapeDtypeStruct(shape, kind) for shape, kind in outs],
        in_specs=[VMEM] * len(args),
        out_specs=[VMEM] * len(outs),
        scratch_shapes=scratch,
        compiler_params=pltpu.CompilerParams(
            vmem_limit_bytes=56 * 1024 * 1024, collective_id=collective, has_side_effects=True
        ),
    )(*args)


def dma(*counts):
    return [pltpu.SemaphoreType.DMA((count,)) for count in counts]


def bf(*shape):
    return pltpu.VMEM(shape, BF)


def f32(*shape):
    return pltpu.VMEM(shape, F32)


def halo_shapes(planes, tiles, chans):
    return [
        ((planes, tiles, chans, LANES), BF),
        ((3, 3, chans, LANES), BF),
        ((3, 3, chans, LANES), BF),
    ]


def shards(sizes, volume, w_fine, w_down, w_lift, w_coarse, w_proj, w_up, cotangent):
    nx, ny, nz = sizes
    scale = 1.0 / math.sqrt(8 * nx * 16 * ny * 64 * nz)
    cells = 8 * nz
    wc = w_coarse.reshape(9, 768, 256)

    *halo, ct, pg, wf, wd, wu, wdt, wut, wp = call(
        functools.partial(arrange_kernel, sizes),
        halo_shapes(10, 10, 16)
        + [
            ((8, 8, 16, LANES), BF),
            ((4, 2, 16, LANES), BF),
            ((48, 144), BF),
            ((96, 144), BF),
            ((48, 288), BF),
            ((48, 288), BF),
            ((96, 144), BF),
            ((32, 256), BF),
        ],
        [volume, cotangent, w_fine, w_down, w_up, w_proj],
        [bf(8, 8, 16, LANES), bf(2, 16, LANES)] + dma(26, 26),
        1,
    )
    pre, act, v3, *halo = call(
        functools.partial(fine_kernel, sizes),
        [((8, 8, 16, LANES), F32), ((8, 8, 16, LANES), BF), ((10, 17, 48, LANES), BF)]
        + halo_shapes(12, 4, 32),
        [*halo, pg, wf],
        [bf(4, 2, 32, LANES), bf(2, 32, LANES)] + dma(26, 26),
        2,
    )
    gather_scratch = [f32(8, LANES), f32(nx, cells, LANES)] + dma(nx * nz, nx * nz, ny, ny)
    am, dsm, pm3n, pgr, pcg = call(
        functools.partial(mid_kernel, sizes),
        [
            ((10, 8, 32, LANES), BF),
            ((6, 5, 32, LANES), BF),
            ((6, 9, 48, LANES), BF),
            ((8, 6, 16, LANES), BF),
            ((ny, nx, cells, LANES), BF),
        ],
        [*halo, wd],
        [bf(12, 17, 48, LANES), bf(12, 8, 16, LANES), bf(10, 8, 32, LANES)] + gather_scratch,
        3,
    )
    grid = (nx, ny, 2, cells, 256)
    dec, gj, gwu, gcg, dsc, actc, alc = call(
        functools.partial(up_kernel, sizes, scale),
        [
            ((16, 8, 16, 64), BF),
            ((6, 5, 32, LANES), F32),
            ((48, 3 * LANES), F32),
            ((ny, nx, cells, LANES), BF),
            (grid, BF),
            (grid, BF),
            (grid, BF),
        ],
        [pcg, am, act, pgr, w_lift, wc, wp, wu, wut],
        [
            bf(2, LANES, 256),
            bf(nx + 2, 2 * ny + 2, cells, 768),
            f32(nx * 2 * cells, 256),
            f32(3, 4, 32, LANES),
            bf(10, 13, 96, LANES),
            bf(8, 6, 16, LANES),
            bf(8, 11, 48, LANES),
            bf(8, 6, 16, LANES),
            bf(16, 16, LANES),
        ]
        + gather_scratch,
        4,
    )
    parts = nx * nz
    rows = 512 // parts
    red, gwc, gwp = call(
        functools.partial(back_kernel, sizes, scale),
        [((parts, rows, LANES), F32), ((27, 256, 256), BF), ((32, 256), F32)],
        [gcg, pcg, dsc, actc, alc, gj, dsm, pm3n, ct, pre, v3, gwu, w_lift, wc, wp, wdt],
        [
            bf(2, LANES, 256),
            bf(2, LANES, 256),
            bf(nx + 4, 2 * ny + 4, cells, 768),
            f32(12 * cells, 256),
            f32(3, 4, 32, LANES),
            bf(6, 9, 96, LANES),
            bf(4, 64, LANES),
            bf(12, 16, 8 * LANES),
            f32(48, 2 * LANES),
            f32(96, 2 * LANES),
            f32(2, LANES, 256),
            bf(256, nx * ny * 2 * cells),
            f32(parts, rows, LANES),
            f32(parts, rows, LANES),
            f32(ny, rows, LANES),
        ]
        + dma(parts, parts, ny, ny, parts, parts),
        5,
    )
    shapes = [(27, 256, 256), (27, 16, 16), (27, 16, 32), (32, 256), (256, 32), (27, 32, 16)]

    def whole(shape):
        return pl.BlockSpec(shape, lambda t: (0,) * len(shape))

    block = pl.BlockSpec((3, 256, 256), lambda t: (t, 0, 0))
    gwc, gwf, gwd, gwl, gwp, gwu = pl.pallas_call(
        last_kernel,
        grid=(9,),
        out_shape=[jax.ShapeDtypeStruct(shape, F32) for shape in shapes],
        in_specs=[block, whole((512, LANES)), whole((32, 256))],
        out_specs=[block] + [whole(shape) for shape in shapes[1:]],
        compiler_params=pltpu.CompilerParams(dimension_semantics=("arbitrary",)),
    )(gwc, red.reshape(512, LANES), gwp)
    return dec, gwf, gwd, gwl, gwc, gwp, gwu


def solution(mesh):
    sizes = tuple(mesh.shape[name] for name in ("gx", "gy", "gz"))
    block = P(None, "gx", "gy", "gz")
    return jax.shard_map(
        functools.partial(shards, sizes),
        mesh=mesh,
        in_specs=(block, P(), P(), P(), P(), P(), P(), block),
        out_specs=(block, P(), P(), P(), P(), P(), P()),
        check_vma=False,
    )
```

time: 184 us -> 128 us (0.70)
  Pallas kernels: 171 us -> 116 us
    pallas_call x10 -> x5, Pallas kernels: 152 us -> 108 us  [call(): pl.pallas_call(kernel, out_shape=[jax.ShapeDtypeStruct(shape, kind) for s...]
    pallas_call x1, Pallas kernels: 19.2 us -> 8.23 us  [shards(): pl.pallas_call(last_kernel, grid=(9,), out_shape=[jax.ShapeDtypeStruct(sh...]
    unnamed x7 -> x9, local copies, waits for them, and re-layouts: 5.23 us -> 10.9 us
    reshape x5 -> x0, local copies, waits for them, and re-layouts: 4.63 us -> none  [the longest x1 1.59 us: shards(): wd = jnp.transpose(w_down, (2, 0, 1)).reshape(32, 432)]
    transpose x4 -> x0, local copies, waits for them, and re-layouts: 2.01 us -> none  [the longest x1 1.03 us: shards(): wf = jnp.transpose(w_fine, (2, 0, 1)).reshape(16, 432)]
where the time goes in v2:
time: 128 us; the launch traced here: 127 us
  Pallas kernels  116 us (91%)
  local copies, waits for them, and re-layouts  10.9 us (9%)
    pallas_call x5, Pallas kernels, call(): pl.pallas_call(kernel, out_shape=[jax.ShapeDtypeStruct(shape, kind) for s...  108 us
    unnamed x9, local copies, waits for them, and re-layouts  10.9 us
    pallas_call x1, Pallas kernels, shards(): pl.pallas_call(last_kernel, grid=(9,), out_shape=[jax.ShapeDtypeStruct(sh...  8.23 us

profile of v2, /device:TPU:1, one launch (start us, length us, event | category | flops | bytes accessed | tf_op | source)
XLA Modules:
  0.0 127.4 jit_solution(7046948063639097138)
XLA Ops:
  0.6 1.5 %copy.17.wp_ref = bf16[256,32]{1,0:T(8,128)(2,1)} copy(bf16[256,32]{0,1:T(8,128)(2,1)} %param.13) | data formatting | bytes 32768 | tf_op args[5]
  2.1 1.7 %copy.15.wf_ref = bf16[27,16,16]{2,1,0:T(8,128)(2,1)} copy(bf16[27,16,16]{0,2,1:T(8,128)(2,1)} %param.9) | data formatting | bytes 27648 | tf_op args[1]
  3.8 1.7 %copy.16.wu_ref = bf16[27,32,16]{2,1,0:T(8,128)(2,1)} copy(bf16[27,32,16]{1,2,0:T(8,128)(2,1)} %param.14) | data formatting | bytes 55296 | tf_op args[6]
  5.5 12.2 %shard_map.135 = (bf16[10,10,16,128]{3,2,1,0:T(8,128)(2,1)}, bf16[3,3,16,128]{3,2,1,0:T(8,128)(2,1)}, bf16[3,3,16,128]{3,2,1,0:T(8,128)(2,1)}, bf16[8,8,16,128]{...) custom-call(bf16[16,8,16,64]{3,2,1,0:T(8,128)(2,1)} %vol_ref.1, ...), custom_call_target="tpu_custom_call" | custom-call | tf_op jit(solution)/shard_map/pallas_call | solution.py:1089
  17.7 11.5 %shard_map.136 = (f32[8,8,16,128]{3,2,1,0:T(8,128)}, bf16[8,8,16,128]{3,2,1,0:T(8,128)(2,1)}, bf16[10,17,48,128]{3,2,1,0:T(8,128)(2,1)}, bf16[12,4,32,128]{3,2,1...) custom-call(bf16[10,10,16,128]{3,2,1,0:T(8,128)(2,1)} %get-tuple-element.45.p_ref, ...), custom_call_target="tpu_custom_call" | custom-call | tf_op jit(solution)/shard_map/pallas_call | solution.py:1089
  29.1 23.1 %shard_map.137 = (bf16[10,8,32,128]{3,2,1,0:T(8,128)(2,1)}, bf16[6,5,32,128]{3,2,1,0:T(8,128)(2,1)}, bf16[6,9,48,128]{3,2,1,0:T(8,128)(2,1)}, bf16[8,6,16,128]{3,2,1,0:T(8,128)(2,1)}, bf16[8,4,32,128]{3,2,1,0:T(8,128)(2,1)}) custom-call(bf16[12,4,32,128]{3,2,1,0:T(8,128)(2,1)} %get-tuple-element.50.p_ref, bf16[3,3,32,128]{3,2,1,0:T(8,128)(2,1)} %get-tuple-element.51.er_ref, ...), custom_call_target="tpu_custom_call" | custom-call | tf_op jit(solution)/shard_map/pallas_call | solution.py:1089
  52.2 27.1 %shard_map.138 = (bf16[16,8,16,64]{3,2,1,0:T(8,128)(2,1)}, f32[6,5,32,128]{3,2,1,0:T(8,128)}, f32[48,384]{1,0:T(8,128)}, bf16[8,4,32,128]{3,2,1,0:T(8,128)(2,1)}...) custom-call(bf16[8,4,32,128]{3,2,1,0:T(8,128)(2,1)} %get-tuple-elemen, ...), custom_call_target="tpu_custom_call" | custom-call | tf_op jit(solution)/shard_map/pallas_call | solution.py:1089
  79.3 33.8 %shard_map.139 = (f32[16,32,128]{2,1,0:T(8,128)}, bf16[27,256,256]{2,1,0:T(8,128)(2,1)}, f32[32,256]{1,0:T(8,128)}) custom-call(bf16[8,4,32,128]{3,2,1,0:T(8,128)(2,1)} %get-tuple-element.62.gcg_ref, bf16[8,4,32,128]{3,2,1,0:T(8,128)(2,1)} %get-tuple-element.54.pcg_ref, bf16[4,8,2,32,256]{4,3,2,1,0:T(8,128)(2,1)} %get-tuple-element.63.dsc_ref, ...), custom_call_target="tpu_custom_call" | custom-call | tf_op jit(solution)/shard_map/pallas_call | solution.py:1089
  113.1 0.0 copy-start
  113.1 8.2 %shard_map.140 = (f32[27,256,256]{2,1,0:T(8,128)}, f32[27,16,16]{2,1,0:T(8,128)}, f32[27,16,32]{2,1,0:T(8,128)}, f32[32,256]{1,0:T(8,128)}, f32[256,32]{1,0:T(8,128)}, /*index=5*/f32[27,32,16]{2,1,0:T(8,128)}) custom-call(bf16[27,256,256]{2,1,0:T(8,128)(2,1)} %get-tuple-element.74.gwc_ref, f32[512,128]{1,0:T(8,128)} %bitcast.4, ...), custom_call_target="tpu_custom_call" | custom-call | tf_op jit(solution)/shard_map/pallas_call | solution.py:1225
  121.4 1.8 %copy.18 = f32[27,16,16]{0,2,1:T(8,128)} copy(f32[27,16,16]{2,1,0:T(8,128)} %get-tuple-element.84) | data formatting | bytes 55296
  123.1 1.6 %copy.19 = f32[256,32]{0,1:T(8,128)} copy(f32[256,32]{1,0:T(8,128)} %get-tuple-element.88) | data formatting | bytes 65536
  124.7 1.9 %copy.20 = f32[27,32,16]{1,2,0:T(8,128)} copy(f32[27,32,16]{2,1,0:T(8,128)} %get-tuple-element.89) | data formatting | bytes 110592
  126.6 0.0 copy-done
  126.6 0.8 copy.22
Async XLA Ops:
  113.1 13.5 %copy-start = (bf16[16,8,16,64]{3,2,1,0:T(8,128)(2,1)S(1)}, bf16[16,8,16,64]{3,2,1,0:T(8,128)(2,1)}, u32[]{:S(2)}) copy-start(bf16[16,8,16,64]{3,2,1,0:T(8,128)(2,1)} %get-tuple-element.97) | copy-start | bytes 786436

commit v3 on v0

v3 whole, which is shorter than its diff:
```python
import functools
import math
import types

import jax
import jax.numpy as jnp
from jax import lax
from jax.experimental import pallas as pl
from jax.experimental.pallas import tpu as pltpu
from jax.sharding import PartitionSpec as P

BF = jnp.bfloat16
F32 = jnp.float32
MESH = pl.DeviceIdType.MESH
LANES = 128


def dot(left, right):
    return jnp.dot(left, right, preferred_element_type=F32)


def dot_nt(left, right):
    return lax.dot_general(left, right, (((1,), (1,)), ((), ())), preferred_element_type=F32)


def dot_tn(left, right):
    return lax.dot_general(left, right, (((0,), (0,)), ((), ())), preferred_element_type=F32)


def sigmoid(values):
    return 0.5 * jnp.tanh(0.5 * values) + 0.5


def slope(values, sig):
    return sig * (1.0 + values * (1.0 - sig))


def lane_of(rows):
    return lax.broadcasted_iota(jnp.int32, (rows, LANES), 1)


def turn(tile, by):
    if isinstance(by, int):
        by = by % LANES
        return tile if by == 0 else pltpu.roll(tile, by, 1)
    return pltpu.roll(tile, lax.rem(by + 4 * LANES, LANES), 1)


def tap_rows(pair):
    return jnp.concatenate([turn(pair, 1), pair, turn(pair, -1)], axis=0)


def between(lower, upper):
    lane = lane_of(lower.shape[0])
    return jnp.where(lane < 64, turn(lower, 64), turn(upper, 64))


def store_taps(ref, x, pairs):
    stacks = [tap_rows(pair) for pair in pairs]
    for n, stack in enumerate(stacks):
        ref[x, 2 * n] = stack.astype(BF)
        if n + 1 < len(stacks):
            ref[x, 2 * n + 1] = between(stack, stacks[n + 1]).astype(BF)


def three(ref, x, y):
    block = ref[x, pl.ds(y, 3)]
    return block.reshape(3 * block.shape[1], LANES)


def conv(weight, ref, planes, starts):
    outs = weight.shape[0] // 3
    parts = []
    for x in range(planes + 2):
        tiles = [three(ref, x, y) for y in starts]
        block = tiles[0] if len(tiles) == 1 else jnp.concatenate(tiles, axis=1)
        parts.append(dot(weight, block))
        if x >= 2:
            yield (
                x - 2,
                parts[x - 2][:outs] + parts[x - 1][outs : 2 * outs] + parts[x][2 * outs :],
            )


def pool_matrix():
    row = lax.broadcasted_iota(jnp.int32, (8 * LANES, LANES), 0)
    col = lax.broadcasted_iota(jnp.int32, (8 * LANES, LANES), 1)
    hit = (row // 256 == col // 32) & (row % 64 // 2 == col % 32)
    return jnp.where(hit, 1.0, 0.0).astype(BF)


def pool_tile(ref, sums, x, half):
    cells = jnp.concatenate([ref[2 * x + a, 4 * half + q] for q in range(4) for a in range(2)], axis=1)
    return dot(cells, sums)


def grow_matrix():
    row = lax.broadcasted_iota(jnp.int32, (LANES, 2 * LANES), 0)
    col = lax.broadcasted_iota(jnp.int32, (LANES, 2 * LANES), 1)
    hit = (row // 64 == col // LANES) & (row % 64 - 8 == col % 64 // 2)
    return jnp.where(hit, 1.0, 0.0).astype(BF)


def coarse_sum_matrix(tiles):
    row = lax.broadcasted_iota(jnp.int32, (8, tiles * LANES), 0)
    cell = lax.broadcasted_iota(jnp.int32, (8, tiles * LANES), 1) % 64 - 8
    return (cell >= 0) & (cell < 32) & ((cell + 4) // 4 == row + 1)


def coarse_grow_matrix(cells, gz):
    row = lax.broadcasted_iota(jnp.int32, (cells, LANES), 0)
    cell = lax.broadcasted_iota(jnp.int32, (cells, LANES), 1) % 64 - 8
    mid = cell + gz * 32
    hit = (cell >= -3) & (cell < 35) & (mid >= 0) & (row == (mid + 4) // 4 - 1)
    return jnp.where(hit, 1.0, 0.0).astype(BF)


def plane_rows(block):
    rows = jnp.swapaxes(block, 0, 1)
    return [jnp.concatenate([rows[2 * t], rows[2 * t + 1]], axis=1) for t in range(8)]


def place_weight(ref, weight):
    for y2 in range(2):
        ref[y2] = jnp.zeros((LANES, 256), BF)
        ref[y2, pl.ds(32 * y2, 32)] = weight


def store_coarse_taps(ref, at, cells):
    count = cells.shape[0]
    row = lax.broadcasted_iota(jnp.int32, cells.shape, 0)
    before = jnp.where(row > 0, pltpu.roll(cells, 1, 0), 0.0)
    after = jnp.where(row < count - 1, pltpu.roll(cells, count - 1, 0), 0.0)
    ref[at + (slice(None), pl.ds(0, 256))] = before.astype(BF)
    ref[at + (slice(None), pl.ds(256, 256))] = cells.astype(BF)
    ref[at + (slice(None), pl.ds(512, 256))] = after.astype(BF)


def zero_rim(ref, rim):
    planes, rows = ref.shape[:2]

    def clear(x, _):
        for y in list(range(rim)) + list(range(rows - rim, rows)):
            ref[x, y] = jnp.zeros(ref.shape[2:], ref.dtype)
        return 0

    lax.fori_loop(0, planes, clear, 0)

    def clear_plane(y, _):
        for x in list(range(rim)) + list(range(planes - rim, planes)):
            ref[x, y] = jnp.zeros(ref.shape[2:], ref.dtype)
        return 0

    lax.fori_loop(0, rows, clear_plane, 0)


def clamp(at, count):
    return jnp.minimum(jnp.maximum(at, 0), count - 1)


def near_cells(sizes):
    nx, ny, _ = sizes
    gx, gy = lax.axis_index("gx"), lax.axis_index("gy")
    found = []
    for dx in range(3):
        for dy in range(4):
            x, y = gx - 1 + dx, gy + (dy + 1) // 2 - 1
            there = (x >= 0) & (x < nx) & (y >= 0) & (y < ny)
            keep = jnp.where(there, 1.0, 0.0)
            found.append((dx, dy, clamp(x, nx), clamp(y, ny), (dy + 1) % 2, keep))
    return found


def nothing():
    pass


NEIGHBOURS = [
    (dx, dy, dz)
    for dz in (-1, 1, 0)
    for dx in (-1, 0, 1)
    for dy in (-1, 0, 1)
    if (dx, dy, dz) != (0, 0, 0)
]


def position():
    return [lax.axis_index(name) for name in ("gx", "gy", "gz")]


def valid(sizes, steps):
    found = None
    for at, size, step in zip(position(), sizes, steps):
        if step != 0:
            test = at > 0 if step < 0 else at < size - 1
            found = test if found is None else found & test
    return found


def plane_peers(nx, nz):
    return [(ox, oz) for ox in range(nx) for oz in range(nz) if (ox, oz) != (0, 0)]


def greet(sizes, work):
    nx, ny, nz = sizes
    me = gx, gy, gz = position()
    barrier = pltpu.get_barrier_semaphore()
    peers = [(lax.rem(gx + ox, nx), gy, lax.rem(gz + oz, nz)) for ox, oz in plane_peers(nx, nz)]
    peers += [(gx, lax.rem(gy + oy, ny), gz) for oy in range(1, ny)]
    for peer in peers:
        pl.semaphore_signal(barrier, inc=1, device_id=peer, device_id_type=MESH)
    total = 1
    for axis in range(3):
        low = jnp.where(me[axis] > 0, 1, 0)
        high = jnp.where(me[axis] < sizes[axis] - 1, 1, 0)
        total = total * (1 + low + high)
    for steps in NEIGHBOURS:

        @pl.when(valid(sizes, steps))
        def _():
            pl.semaphore_signal(
                barrier,
                inc=1,
                device_id=tuple(me[axis] + steps[axis] for axis in range(3)),
                device_id_type=MESH,
            )

    work()
    pl.semaphore_wait(barrier, total - 1 + len(peers))


def halo_round(sizes, hx, ht, refs, meanwhile):
    a_ref, e_ref, p_ref, er_ref, el_ref, send_sem, recv_sem = refs
    me = [lax.axis_index(name) for name in ("gx", "gy", "gz")]
    planes, tiles = a_ref.shape[:2]

    def part(step, halo, count):
        if step == 0:
            return pl.ds(0, count), pl.ds(halo, count)
        if step > 0:
            return pl.ds(count - halo, halo), pl.ds(0, halo)
        return pl.ds(0, halo), pl.ds(count + halo, halo)

    def copy_of(k, steps):
        dx, dy, dz = steps
        if dz == 0:
            fx, tx = part(dx, hx, planes)
            fy, ty = part(dy, ht, tiles)
            src, dst = a_ref.at[fx, fy], p_ref.at[tx, ty]
        elif dz > 0:
            src, dst = e_ref.at[1], el_ref.at[1 - dx, 1 - dy]
        else:
            src, dst = e_ref.at[0], er_ref.at[1 - dx, 1 - dy]
        return pltpu.make_async_remote_copy(
            src_ref=src,
            dst_ref=dst,
            send_sem=send_sem.at[k],
            recv_sem=recv_sem.at[k],
            device_id=(me[0] + dx, me[1] + dy, me[2] + dz),
            device_id_type=MESH,
        )

    for k, steps in enumerate(NEIGHBOURS):

        @pl.when(valid(sizes, steps))
        def _():
            copy_of(k, steps).start()

    p_ref[pl.ds(hx, planes), pl.ds(ht, tiles)] = a_ref[...]
    for k, steps in enumerate(NEIGHBOURS):
        back = tuple(-step for step in steps)
        dx, dy, dz = steps

        @pl.when(jnp.logical_not(valid(sizes, back)))
        def _():
            if dz == 0:
                _, tx = part(dx, hx, planes)
                _, ty = part(dy, ht, tiles)
                into = p_ref.at[tx, ty]
            elif dz > 0:
                into = el_ref.at[1 - dx, 1 - dy]
            else:
                into = er_ref.at[1 - dx, 1 - dy]
            into[...] = jnp.zeros(into.shape, into.dtype)

    meanwhile()
    for k, steps in enumerate(NEIGHBOURS):
        back = tuple(-step for step in steps)

        @pl.when(valid(sizes, back))
        def _():
            copy_of(k, steps).wait_recv()

    for k, steps in enumerate(NEIGHBOURS):

        @pl.when(valid(sizes, steps))
        def _():
            copy_of(k, steps).wait_send()


def gather_round(sizes, refs, first_wait, second_wait):
    g_ref, all_ref, stage, send_a, recv_a, send_b, recv_b = refs
    nx, ny, nz = sizes
    gx, gy, gz = [lax.axis_index(name) for name in ("gx", "gy", "gz")]
    plane = plane_peers(nx, nz)

    def first(k, x, z, peer):
        return pltpu.make_async_remote_copy(
            src_ref=g_ref,
            dst_ref=stage.at[x, pl.ds(pl.multiple_of(z * 8, 8), 8)],
            send_sem=send_a.at[k],
            recv_sem=recv_a.at[k],
            device_id=peer,
            device_id_type=MESH,
        )

    def second(oy, y):
        return pltpu.make_async_remote_copy(
            src_ref=all_ref.at[gy],
            dst_ref=all_ref.at[y],
            send_sem=send_b.at[oy],
            recv_sem=recv_b.at[oy],
            device_id=(gx, lax.rem(gy + oy, ny), gz),
            device_id_type=MESH,
        )

    for k, (ox, oz) in enumerate(plane):
        first(k, gx, gz, (lax.rem(gx + ox, nx), gy, lax.rem(gz + oz, nz))).start()
    stage[gx, pl.ds(pl.multiple_of(gz * 8, 8), 8)] = g_ref[...]
    first_wait()
    for k, (ox, oz) in enumerate(plane):
        peer = (lax.rem(gx + ox, nx), gy, lax.rem(gz + oz, nz))
        first(k, lax.rem(gx + nx - ox, nx), lax.rem(gz + nz - oz, nz), peer).wait_recv()
    all_ref[gy] = stage[...].astype(BF)
    for oy in range(1, ny):
        second(oy, gy).start()
    second_wait()
    for k, (ox, oz) in enumerate(plane):
        first(k, gx, gz, (lax.rem(gx + ox, nx), gy, lax.rem(gz + oz, nz))).wait_send()
    for oy in range(1, ny):
        second(oy, lax.rem(gy + ny - oy, ny)).wait_recv()
    for oy in range(1, ny):
        second(oy, gy).wait_send()


def reduce_round(sizes, refs, waits):
    pay_ref, out_ref, ra, rb, send_a, recv_a, send_b, recv_b, send_c, recv_c = refs
    nx, ny, nz = sizes
    gx, gy, gz = [lax.axis_index(name) for name in ("gx", "gy", "gz")]
    mine = gx * nz + gz
    plane = plane_peers(nx, nz)

    def ahead(ox, oz):
        return lax.rem(gx + ox, nx), lax.rem(gz + oz, nz)

    def behind(ox, oz):
        return lax.rem(gx + nx - ox, nx), lax.rem(gz + nz - oz, nz)

    def scatter(k, ox, oz, slot):
        x, z = ahead(ox, oz)
        return pltpu.make_async_remote_copy(
            src_ref=pay_ref.at[x * nz + z],
            dst_ref=ra.at[slot],
            send_sem=send_a.at[k],
            recv_sem=recv_a.at[k],
            device_id=(x, gy, z),
            device_id_type=MESH,
        )

    def across(oy, slot):
        return pltpu.make_async_remote_copy(
            src_ref=rb.at[gy],
            dst_ref=rb.at[slot],
            send_sem=send_b.at[oy],
            recv_sem=recv_b.at[oy],
            device_id=(gx, lax.rem(gy + oy, ny), gz),
            device_id_type=MESH,
        )

    def spread(k, ox, oz, slot):
        x, z = ahead(ox, oz)
        return pltpu.make_async_remote_copy(
            src_ref=out_ref.at[mine],
            dst_ref=out_ref.at[slot],
            send_sem=send_c.at[k],
            recv_sem=recv_c.at[k],
            device_id=(x, gy, z),
            device_id_type=MESH,
        )

    for k, (ox, oz) in enumerate(plane):
        scatter(k, ox, oz, mine).start()
    ra[mine] = pay_ref[mine]
    waits[0]()
    for k, (ox, oz) in enumerate(plane):
        x, z = behind(ox, oz)
        scatter(k, ox, oz, x * nz + z).wait_recv()
    rb[gy] = jnp.sum(ra[...], axis=0)
    for oy in range(1, ny):
        across(oy, gy).start()
    waits[1]()
    for k, (ox, oz) in enumerate(plane):
        scatter(k, ox, oz, mine).wait_send()
    for oy in range(1, ny):
        across(oy, lax.rem(gy + ny - oy, ny)).wait_recv()
    out_ref[mine] = jnp.sum(rb[...], axis=0)
    for k, (ox, oz) in enumerate(plane):
        spread(k, ox, oz, mine).start()
    waits[2]()
    for oy in range(1, ny):
        across(oy, gy).wait_send()
    for k, (ox, oz) in enumerate(plane):
        x, z = behind(ox, oz)
        spread(k, ox, oz, x * nz + z).wait_recv()
    for k, (ox, oz) in enumerate(plane):
        spread(k, ox, oz, mine).wait_send()


def fold(ref, i, tiles):
    block = jnp.concatenate(tiles, axis=0)
    outs = block.shape[1]
    ref[pl.ds(i * outs, outs)] = block.T.astype(BF)


def prepare_weights(r):
    for c in range(16):
        r.wrows[pl.ds(c, 27, stride=16)] = r.wf_in[c].astype(F32).T
    for i in range(3):
        r.wf[pl.ds(16 * i, 16)] = r.wrows[pl.ds(144 * i, 144)].T.astype(BF)
        down = [r.wd_in[9 * i + jk].astype(F32) for jk in range(9)]
        up = [r.wu_in[9 * i + jk].astype(F32).T for jk in range(9)]
        down_back = [r.wd_in[26 - 9 * i - jk].astype(F32).T for jk in range(9)]
        up_back = [r.wu_in[26 - 9 * i - jk].astype(F32) for jk in range(9)]
        fold(r.wd, i, down)
        fold(r.wu, i, up)
        fold(r.wdt, i, down_back)
        fold(r.wut, i, up_back)


def arrange_volume(r):
    spot = lane_of(16) % 64

    def plane(x, edges):
        low, high = edges
        for t, tile in enumerate(plane_rows(r.vol[:, x])):
            r.v[x, t] = tile
            wide = tile.astype(F32)
            at = t * 8 + x
            low = jnp.where(spot == at, turn(wide, at), low)
            high = jnp.where(spot == at, turn(wide, at - 63), high)
        return low, high

    zero = jnp.zeros((16, LANES), F32)
    low, high = lax.fori_loop(0, 8, plane, (zero, zero))
    r.ve[0] = low.astype(BF)
    r.ve[1] = high.astype(BF)


def arrange_cotangent(r):
    def plane(x, _):
        for t, tile in enumerate(plane_rows(r.cot[:, x])):
            r.ct[x, t] = tile
        return 0

    lax.fori_loop(0, 8, plane, 0)
    sums = pool_matrix()
    r.sums[...] = sums
    for x in range(4):
        for half in range(2):
            r.pg[x, half] = pool_tile(r.ct, sums, x, half).astype(BF)


def fine_forward(r):
    spot = lane_of(16) % 64

    def rows(x, _):
        dx, sx = (x + 7) // 8, lax.rem(x + 7, 8)
        stacks = []
        for t in range(10):
            dy, sy = (t + 7) // 8, (t + 7) % 8
            at = sy * 8 + sx
            tile = r.vp[x, t].astype(F32)
            left = turn(r.vel[dx, dy].astype(F32), -at)
            right = turn(r.ver[dx, dy].astype(F32), 63 - at)
            before = jnp.where(spot == 0, left, turn(tile, 1))
            after = jnp.where(spot == 63, right, turn(tile, -1))
            stacks.append(jnp.concatenate([before, tile, after], axis=0))
        for t in range(9):
            if t > 0:
                r.v3[x, 2 * t - 1] = stacks[t].astype(BF)
            r.v3[x, 2 * t] = between(stacks[t], stacks[t + 1]).astype(BF)
        return 0

    lax.fori_loop(0, 10, rows, 0)
    weight = r.wf[...]

    def convs(g, _):
        for x, pre in conv(weight, r.v3, 8, (4 * g, 4 * g + 2)):
            act = (pre * sigmoid(pre)).astype(BF)
            for b in range(2):
                r.pre[x, 2 * g + b] = pre[:, b * LANES : (b + 1) * LANES]
                r.act[x, 2 * g + b] = act[:, b * LANES : (b + 1) * LANES]
        return 0

    lax.fori_loop(0, 4, convs, 0)

    sums = r.sums[...]
    lane = lane_of(32)
    low = jnp.zeros((32, LANES), F32)
    high = low
    for x in range(4):
        for half in range(2):
            pooled = (pool_tile(r.act, sums, x, half) * 0.125).astype(BF)
            tile = jnp.concatenate([pooled, r.pg[x, half]], axis=0)
            r.m[x, half] = tile
            wide = tile.astype(F32)
            for q in range(4):
                at = (q % 2) * 64 + (x * 4 + 2 * half + q // 2) * 4
                here = (lane >= at) & (lane < at + 4)
                low = jnp.where(here, turn(wide, at - 32 * q), low)
                high = jnp.where(here, turn(wide, at - 32 * q - 28), high)
    r.me[0] = low.astype(BF)
    r.me[1] = high.astype(BF)


def mid_forward(r, sizes):
    nx, ny, nz = sizes
    gx, gy, gz = position()
    lane = lane_of(32)
    spot = lane % 64

    def rows(x, _):
        dx, sx = x // 4, lax.rem(x, 4)
        pairs = []
        for a in range(8):
            dy, sy = (a + 2) // 4, (a + 2) % 4
            tile = r.mp[x, a // 2].astype(F32)
            q = 2 * (a % 2)
            base = jnp.where(lane < 64, turn(tile, 8 - 32 * q), turn(tile, 40 - 32 * q))
            at = (sx * 4 + sy) * 4
            right = turn(r.mer[dx, dy].astype(F32), 40 - at)
            left = turn(r.mel[dx, dy].astype(F32), 4 - at)
            row = jnp.where(spot < 44, right, 0.0)
            row = jnp.where(spot < 40, base, row)
            row = jnp.where(spot < 8, left, row)
            row = jnp.where(spot < 4, 0.0, row)
            r.pgp[x, a] = row[16:].astype(BF)
            pairs.append(row[:16])
        store_taps(r.pm3, x, pairs)
        r.pm3[x, 15] = jnp.zeros((48, LANES), BF)
        r.pm3[x, 16] = jnp.zeros((48, LANES), BF)
        return 0

    lax.fori_loop(0, 12, rows, 0)
    weight = r.wd[...]
    cell = spot - 8
    mid = cell + gz * 32
    inside = (cell >= -3) & (cell < 35) & (mid >= 0) & (mid < 32 * nz)
    second = lane // 64

    def convs(g, _):
        for x, both in conv(weight, r.pm3, 10, (4 * g, 4 * g + 2)):
            at_x = gx * 4 + x - 3
            for b in range(2):
                pre = both[:, b * LANES : (b + 1) * LANES]
                at_y = gy * 8 + 4 * g + 2 * b - 3 + second
                keep = inside & (at_y >= 0) & (at_y < 8 * ny)
                keep = keep & (at_x >= 0) & (at_x < 4 * nx)
                sig = sigmoid(pre)
                r.am[x, 2 * g + b] = jnp.where(keep, pre * sig, 0.0).astype(BF)
                r.dsm[x, 2 * g + b] = jnp.where(keep, slope(pre, sig), 0.0).astype(BF)
        return 0

    lax.fori_loop(0, 4, convs, 0)
    halves = [
        jnp.concatenate([r.am[3 + a, 1 + 2 * h + m] for a in range(4) for m in range(3)], axis=1)
        for h in range(2)
    ]
    cells = jnp.concatenate(halves + [jnp.zeros((64, 12 * LANES), BF)], axis=0)
    col = lax.broadcasted_iota(jnp.int32, (8, 12 * LANES), 1)
    third, upper = col // LANES % 3, col // 64 % 2
    hit = coarse_sum_matrix(12) & ((third == 1) | ((third == 0) == (upper == 1)))
    pooled = dot_nt(jnp.where(hit, 1.0, 0.0).astype(BF), cells) * (1.0 / 64.0)
    r.pc[...] = pooled.astype(BF).astype(F32)


def near_rows(sizes, count):
    ny = sizes[1]
    have = min(count, ny)
    start = lax.axis_index("gy") - count // 2
    return jnp.minimum(jnp.maximum(start, 0), ny - have), have


def lift_row(r, sizes, y):
    for x in range(sizes[0]):
        for y2 in range(2):
            pre = dot(r.pcg[y, x], r.wide_lift[y2])
            act = (pre * sigmoid(pre)).astype(BF)
            r.alc[x, y, y2] = act
            store_coarse_taps(r.al3, (x + 1, 2 * y + y2 + 1), act.astype(F32))


def coarse_forward(r, sizes, y, have):
    nx, cells = sizes[0], 8 * sizes[2]
    rows = nx * 2 * have * cells
    for i in range(3):
        for j in range(3):
            block = r.al3[pl.ds(i, nx), pl.ds(2 * y + j, 2 * have)].reshape(rows, 768)
            part = dot(block, r.wc[3 * i + j])
            if i + j == 0:
                r.acc[pl.ds(0, rows)] = part
            else:
                r.acc[pl.ds(0, rows)] += part
    per = 2 * have * cells
    for x in range(nx):
        pre = r.acc[pl.ds(x * per, per)]
        sig = sigmoid(pre)
        r.actc[x, pl.ds(y, have)] = (pre * sig).astype(BF).reshape(have, 2, cells, 256)
        r.dsc[x, pl.ds(y, have)] = slope(pre, sig).astype(BF).reshape(have, 2, cells, 256)


def up_forward(r, sizes, scale):
    cells = 8 * sizes[2]
    gz = lax.axis_index("gz")
    start, have = near_rows(sizes, 5)

    def lift(o, _):
        lift_row(r, sizes, start + o)
        return 0

    lax.fori_loop(0, have, lift, 0)
    coarse_forward(r, sizes, *near_rows(sizes, 3))

    spread = coarse_grow_matrix(cells, gz)
    for dx, dy, x, y, y2, keep in near_cells(sizes):
        out = dot_nt(r.wp[...], r.actc[x, y, y2]).astype(BF)
        r.cos[dx, dy] = dot(out, spread) * keep

    first = lane_of(32) < 64

    def join(x, _):
        pairs = []
        for m in range(7):
            lower = r.cos[(x + 1) // 4, (2 * m + 1) // 4]
            upper = r.cos[(x + 1) // 4, (2 * m + 2) // 4]
            row = r.am[x, m].astype(F32) + jnp.where(first, lower, upper)
            pairs.append(row.astype(BF).astype(F32))
        store_taps(r.j3, x, pairs)
        return 0

    lax.fori_loop(0, 10, join, 0)

    cell = lane_of(16) % 64 - 8
    near = (cell >= -2) & (cell < 34)
    weight = r.wu[...]

    def up(g, _):
        for x, both in conv(weight, r.j3, 8, (4 * g, 4 * g + 2)):
            for b in range(2):
                pre = both[:, b * LANES : (b + 1) * LANES]
                sig = sigmoid(pre)
                r.su[x, 2 * g + b] = (pre * sig).astype(BF)
                pooled = r.pgp[x + 2, 2 * g + b + 1].astype(F32) * scale
                grad = jnp.where(near, pooled * slope(pre, sig), 0.0)
                r.guo[x, 2 * g + b] = grad.astype(BF)
        return 0

    lax.fori_loop(0, 3, up, 0)

    def stack(x, _):
        store_taps(r.gu3, x, [r.guo[x, m].astype(F32) for m in range(6)])
        return 0

    lax.fori_loop(0, 8, stack, 0)

    weight_t = r.wut[...]
    for starts in ((0, 2), (4, 6), (8,)):
        for x, both in conv(weight_t, r.gu3, 6, starts):
            for b, y in enumerate(starts):
                r.gj[x, y // 2] = both[:, b * LANES : (b + 1) * LANES]

    totals = []
    for h in range(2):
        total = None
        for a in range(4):
            lower, middle, upper = [r.gj[1 + a, 2 * h + m] for m in range(3)]
            row = middle + jnp.where(first, upper, lower)
            total = row if total is None else total + row
        totals.append(total)
    total = jnp.concatenate(totals + [jnp.zeros((64, LANES), F32)], axis=0)
    head = total.astype(BF)
    tail = (total - head.astype(F32)).astype(BF)
    sums = jnp.where(coarse_sum_matrix(1), 1.0, 0.0).astype(BF)
    r.gc[...] = (dot_nt(sums, head) + dot_nt(sums, tail)).astype(BF).astype(F32)


def up_taps(r):
    cell = lane_of(16) % 64 - 8
    own = (cell >= 0) & (cell < 32)
    r.accu[...] = jnp.zeros(r.accu.shape, F32)
    grads = [
        jnp.concatenate(
            [jnp.where(own, r.guo[x + 2, m + 1].astype(F32), 0.0) for m in range(4)], axis=1
        ).astype(BF)
        for x in range(4)
    ]
    none = jnp.zeros((16, 4 * LANES), BF)
    for x in range(6):
        left = [grads[x - i] if 0 <= x - i < 4 else none for i in range(3)]
        right = [three(r.j3, x + 2, 2 * m + 2) for m in range(4)]
        r.accu[:, pl.ds(0, 288)] += dot_nt(
            jnp.concatenate(left, axis=0), jnp.concatenate(right, axis=1)
        )


def decode(r):
    grow = grow_matrix()

    def plane(x, _):
        rows = jnp.concatenate([r.su[x + 2, m + 1] for m in range(4)], axis=0)
        grown = dot(rows, grow)
        for a in range(2):
            for t in range(8):
                add = grown[16 * (t // 2) : 16 * (t // 2) + 16, (t % 2) * LANES :][:, :LANES]
                tile = r.act[2 * x + a, t].astype(F32) + add
                r.plane[2 * t] = tile.astype(BF)
                r.plane[2 * t + 1] = turn(tile, 64).astype(BF)
            r.dec[:, 2 * x + a] = jnp.swapaxes(r.plane[...], 0, 1)[:, :, :64]
        return 0

    lax.fori_loop(0, 4, plane, 0)


def coarse_grad_row(r, sizes, y):
    for x in range(sizes[0]):
        for y2 in range(2):
            grad = dot(r.gcg[y, x], r.wide_proj[y2]) * r.dsc[x, y, y2].astype(F32)
            grad = grad.astype(BF).astype(F32)
            store_coarse_taps(r.gp3, (x + 2, 2 * y + y2 + 2), grad)


def pay_rows(r, start, block):
    per = r.pay.shape[1]
    done = 0
    while done < block.shape[0]:
        part, at = divmod(start + done, per)
        size = min(per - at, block.shape[0] - done)
        r.pay[part, pl.ds(at, size)] = block[done : done + size]
        done += size


def backward(r, sizes, scale):
    cells = 8 * sizes[2]
    gx, gy, gz = position()
    start, have = near_rows(sizes, 3)

    def coarse(o, _):
        coarse_grad_row(r, sizes, start + o)
        return 0

    lax.fori_loop(0, have, coarse, 0)
    rows = 12 * cells
    for i in range(3):
        for j in range(3):
            block = r.gp3[pl.ds(gx + i, 3), pl.ds(2 * gy + j, 4)].reshape(rows, 768)
            part = dot(block, r.wct[3 * i + j])
            if i + j == 0:
                r.acc[pl.ds(0, rows)] = part
            else:
                r.acc[pl.ds(0, rows)] += part

    spread = coarse_grow_matrix(cells, gz)
    own = lax.broadcasted_iota(jnp.int32, (cells, 256), 0) // 8 == gz
    for at, (dx, dy, x, y, y2, keep) in enumerate(near_cells(sizes)):
        pre = dot(r.pcg[y, x], r.wide_lift[y2])
        grad = (r.acc[pl.ds(at * cells, cells)] * slope(pre, sigmoid(pre))).astype(BF)
        out = dot_nt(r.wl[...], grad).astype(BF)
        r.cos[dx, dy] = dot(out, spread) * (keep * (1.0 / 64.0))
        if dx == 1 and dy in (1, 2):
            masked = jnp.where(own, grad.astype(F32), 0.0).astype(BF)
            r.pairs[y2] = dot_tn(r.pcg[y, x], masked)
    lifts = r.pairs[0, :32] + r.pairs[1, 32:64]
    for b in range(2):
        pay_rows(r, 432 + 32 * b, lifts[:, b * LANES : (b + 1) * LANES])

    first = lane_of(32) < 64

    def join(x, _):
        pairs = []
        for n in range(5):
            lower = r.cos[(x + 3) // 4, (2 * n + 3) // 4]
            upper = r.cos[(x + 3) // 4, (2 * n + 4) // 4]
            row = r.gj[x, n] + jnp.where(first, lower, upper)
            row = row * r.dsm[x + 2, n + 1].astype(F32)
            pairs.append(row.astype(BF).astype(F32))
        store_taps(r.gm3, x, pairs)
        return 0

    lax.fori_loop(0, 6, join, 0)

    weight_t = r.wdt[...]
    for starts in ((0, 2), (4, 6)):
        for x, both in conv(weight_t, r.gm3, 4, starts):
            for b, y in enumerate(starts):
                r.gpm[x, pl.ds(8 * y, 16)] = both[:, b * LANES : (b + 1) * LANES].astype(BF)

    grow = grow_matrix()
    for x in (0, 1, 10, 11):
        r.gf[x] = jnp.zeros(r.gf.shape[1:], BF)

    def fine(x, _):
        grown = dot(r.gpm[x], grow) * 0.125
        for a in range(2):
            for t in range(8):
                add = grown[16 * (t // 2) : 16 * (t // 2) + 16, (t % 2) * LANES :][:, :LANES]
                pre = r.pre[2 * x + a, t]
                grad = r.ct[2 * x + a, t].astype(F32) * scale + add
                grad = (grad * slope(pre, sigmoid(pre))).astype(BF)
                r.gf[2 * x + a + 2, :, pl.ds(t * LANES, LANES)] = grad
        return 0

    lax.fori_loop(0, 4, fine, 0)

    r.accd[...] = jnp.zeros(r.accd.shape, F32)
    spot = lane_of(32) % 64
    inner = (spot >= 8) & (spot < 40)
    grads = [
        jnp.concatenate(
            [
                jnp.where(inner, r.gm3[x + 1, 2 * m + 1, pl.ds(32, 32)].astype(F32), 0.0)
                for m in range(4)
            ],
            axis=1,
        ).astype(BF)
        for x in range(4)
    ]
    none = jnp.zeros((32, 4 * LANES), BF)
    for x in range(6):
        left = [grads[x - i] if 0 <= x - i < 4 else none for i in range(3)]
        right = [three(r.pm3, x + 3, 2 * m + 3) for m in range(4)]
        r.accd[:, pl.ds(0, 144)] += dot_nt(
            jnp.concatenate(left, axis=0), jnp.concatenate(right, axis=1)
        )

    r.accf[...] = jnp.zeros(r.accf.shape, F32)

    def taps_fine(x, _):
        left = jnp.concatenate([r.gf[x + 2 - i] for i in range(3)], axis=0)
        right = jnp.concatenate([three(r.v3, x, 2 * t) for t in range(8)], axis=1)
        r.accf[:, pl.ds(0, 144)] += dot_nt(left, right)
        return 0

    lax.fori_loop(0, 10, taps_fine, 0)

    for b in range(2):
        pay_rows(r, 48 * b, r.accf[:, b * LANES : (b + 1) * LANES])
    for b in range(3):
        pay_rows(r, 96 + 48 * b, r.accu[:, b * LANES : (b + 1) * LANES])
    for b in range(2):
        pay_rows(r, 240 + 96 * b, r.accd[:, b * LANES : (b + 1) * LANES])
    pay_rows(r, 496, jnp.zeros((16, LANES), F32))


def coarse_taps(r, sizes, first, last):
    nx, ny, nz = sizes
    count = nx * ny * 16 * nz

    def taps(t, _):
        i, j = t // 3, lax.rem(t, 3)
        block = r.gp3[pl.ds(3 - i, nx), pl.ds(3 - j, 2 * ny)].reshape(count, 768)
        out = dot(r.cells_t[...], block)
        for k in range(3):
            r.gwc[3 * t + k] = out[:, 256 * (2 - k) : 256 * (3 - k)].astype(BF)
        return 0

    lax.fori_loop(first, last, taps, 0)


def proj_grad(r, sizes):
    nx, ny, nz = sizes
    cells = 8 * nz
    r.pairs[...] = jnp.zeros(r.pairs.shape, F32)

    def plane(x, _):
        for y2 in range(2):
            grads = r.gcg[:, x].reshape(ny * cells, LANES)
            r.pairs[y2] += dot_tn(grads, r.actc[x, :, y2].reshape(ny * cells, 256))
        return 0

    lax.fori_loop(0, nx, plane, 0)
    r.gwp[...] = r.pairs[0, :32] + r.pairs[1, 32:64]


def step_kernel(sizes, scale, names, *refs):
    nx, ny, nz = sizes
    count = nx * ny * 16 * nz
    r = types.SimpleNamespace(**dict(zip(names, refs, strict=True)))
    fetch = pltpu.make_async_copy(r.wc_in, r.wc, r.fetched)
    fetch.start()
    greet(sizes, lambda: arrange_volume(r))

    def first_wait():
        prepare_weights(r)
        arrange_cotangent(r)
        place_weight(r.wide_lift, r.wl[...])
        place_weight(r.wide_proj, r.wp[...])

    halo_round(sizes, 1, 1, (r.v, r.ve, r.vp, r.ver, r.vel, r.vsend, r.vrecv), first_wait)
    fine_forward(r)

    def second_wait():
        zero_rim(r.al3, 1)
        zero_rim(r.gp3, 2)
        fetch.wait()

        def turn_weights(t, _):
            for k in range(3):
                block = r.wc[8 - t, pl.ds(256 * (2 - k), 256)]
                r.wct[t, pl.ds(256 * k, 256)] = block.T
            return 0

        lax.fori_loop(0, 9, turn_weights, 0)

    halo_round(sizes, 4, 1, (r.m, r.me, r.mp, r.mer, r.mel, r.msend, r.mrecv), second_wait)
    mid_forward(r, sizes)
    sems = (r.ga_send, r.ga_recv, r.gb_send, r.gb_recv)
    gather_round(sizes, (r.pc, r.pcg, r.pstage) + sems, nothing, nothing)
    up_forward(r, sizes, scale)

    def third_wait():
        up_taps(r)
        decode(r)

    def fourth_wait():
        start, have = near_rows(sizes, 5)

        def lift(o, _):
            lift_row(r, sizes, lax.rem(start + o, ny))
            return 0

        lax.fori_loop(have, ny, lift, 0)
        start_c, have_c = near_rows(sizes, 3)

        def coarse(o, _):
            coarse_forward(r, sizes, lax.rem(start_c + o, ny), 1)
            return 0

        lax.fori_loop(have_c, ny, coarse, 0)

    sems = (r.ha_send, r.ha_recv, r.hb_send, r.hb_recv)
    gather_round(sizes, (r.gc, r.gcg, r.gstage) + sems, third_wait, fourth_wait)
    backward(r, sizes, scale)

    def store(part, first, last):
        taps = pl.ds(3 * first, 3 * (last - first))
        return pltpu.make_async_copy(r.gwc.at[taps], r.gwc_out.at[taps], r.stored.at[part])

    ends = (0, 2, 5, 9)

    def taps_wait(part):
        def wait():
            if part == 0:
                start, have = near_rows(sizes, 3)

                def coarse(o, _):
                    coarse_grad_row(r, sizes, lax.rem(start + o, ny))
                    return 0

                lax.fori_loop(have, ny, coarse, 0)
                r.cells_t[...] = r.alc[...].reshape(count, 256).T
            coarse_taps(r, sizes, ends[part], ends[part + 1])
            store(part, ends[part], ends[part + 1]).start()
            if part == 2:
                proj_grad(r, sizes)

        return wait

    sems = (r.ra_send, r.ra_recv, r.rb_send, r.rb_recv, r.rc_send, r.rc_recv)
    reduce_round(sizes, (r.pay, r.red, r.ra, r.rb) + sems, [taps_wait(part) for part in range(3)])
    for part in range(3):
        store(part, ends[part], ends[part + 1]).wait()


def last_kernel(gwc_ref, red_ref, gwp_ref, wc_out, wf_out, wd_out, wl_out, wp_out, wu_out, rows):
    step = pl.program_id(0)

    def columns(start, blocks, count):
        return jnp.concatenate(
            [red_ref[pl.ds(start + count * b, count)] for b in range(blocks)], axis=1
        )

    @pl.when(step == 0)
    def _():
        table = columns(0, 2, 48)
        for i in range(3):
            rows[pl.ds(144 * i, 144)] = table[16 * i : 16 * i + 16, :144].T
        for c in range(16):
            wf_out[c] = rows[pl.ds(c, 27, stride=16)].T

    @pl.when(step == 1)
    def _():
        table = columns(96, 3, 48)
        for i in range(3):
            for jk in range(9):
                tile = table[16 * i : 16 * i + 16, 32 * jk : 32 * jk + 32]
                wu_out[9 * i + jk] = tile

    @pl.when(step == 2)
    def _():
        table = columns(240, 2, 96)
        for i in range(3):
            part = table[32 * i : 32 * i + 32, :144]
            wd_out[pl.ds(9 * i, 9)] = part.T.reshape(9, 16, 32)

    @pl.when(step == 3)
    def _():
        wl_out[...] = columns(432, 2, 32)
        wp_out[...] = gwp_ref[...]

    wc_out[...] = gwc_ref[...].astype(F32)


VMEM = pl.BlockSpec(memory_space=pltpu.VMEM)
HBM = pl.BlockSpec(memory_space=pl.ANY)


def shards(sizes, volume, w_fine, w_down, w_lift, w_coarse, w_proj, w_up, cotangent):
    nx, ny, nz = sizes
    scale = 1.0 / math.sqrt(8 * nx * 16 * ny * 64 * nz)
    cells = 8 * nz
    parts = nx * nz
    per = 512 // parts
    grid = (nx, ny, 2, cells, 256)
    gathered = (ny, nx, cells, LANES)
    ins = {
        "vol": volume,
        "cot": cotangent,
        "wf_in": jnp.transpose(w_fine, (1, 2, 0)),
        "wd_in": w_down,
        "wu_in": jnp.transpose(w_up, (0, 2, 1)),
        "wl": w_lift,
        "wp": jnp.transpose(w_proj),
        "wc_in": w_coarse.reshape(9, 768, 256),
    }
    outs = {
        "dec": ((16, 8, 16, 64), BF),
        "red": ((parts, per, LANES), F32),
        "gwp": ((32, 256), F32),
        "gwc_out": ((27, 256, 256), BF),
    }
    narrow = {
        "v": (8, 8, 16, LANES),
        "ve": (2, 16, LANES),
        "vp": (10, 10, 16, LANES),
        "ver": (3, 3, 16, LANES),
        "vel": (3, 3, 16, LANES),
        "ct": (8, 8, 16, LANES),
        "sums": (8 * LANES, LANES),
        "pg": (4, 2, 16, LANES),
        "wf": (48, 144),
        "wd": (96, 144),
        "wu": (48, 288),
        "wdt": (48, 288),
        "wut": (96, 144),
        "v3": (10, 17, 48, LANES),
        "act": (8, 8, 16, LANES),
        "m": (4, 2, 32, LANES),
        "me": (2, 32, LANES),
        "mp": (12, 4, 32, LANES),
        "mer": (3, 3, 32, LANES),
        "mel": (3, 3, 32, LANES),
        "pm3": (12, 17, 48, LANES),
        "pgp": (12, 8, 16, LANES),
        "am": (10, 8, 32, LANES),
        "dsm": (10, 8, 32, LANES),
        "pcg": gathered,
        "gcg": gathered,
        "wc": (9, 768, 256),
        "wct": (9, 768, 256),
        "wide_lift": (2, LANES, 256),
        "wide_proj": (2, LANES, 256),
        "al3": (nx + 2, 2 * ny + 2, cells, 768),
        "gp3": (nx + 4, 2 * ny + 4, cells, 768),
        "alc": grid,
        "actc": grid,
        "dsc": grid,
        "j3": (10, 13, 96, LANES),
        "guo": (8, 6, 16, LANES),
        "gu3": (8, 11, 48, LANES),
        "su": (8, 6, 16, LANES),
        "plane": (16, 16, LANES),
        "gm3": (6, 9, 96, LANES),
        "gpm": (4, 64, LANES),
        "gf": (12, 16, 8 * LANES),
        "cells_t": (256, nx * ny * 2 * cells),
        "gwc": (27, 256, 256),
    }
    wide = {
        "wrows": (432, 16),
        "pre": (8, 8, 16, LANES),
        "pc": (8, LANES),
        "pstage": (nx, cells, LANES),
        "acc": (max(nx * 2 * min(3, ny), 12) * cells, 256),
        "cos": (3, 4, 32, LANES),
        "gj": (6, 5, 32, LANES),
        "gc": (8, LANES),
        "gstage": (nx, cells, LANES),
        "accu": (48, 3 * LANES),
        "accf": (48, 2 * LANES),
        "accd": (96, 2 * LANES),
        "pairs": (2, LANES, 256),
        "pay": (parts, per, LANES),
        "ra": (parts, per, LANES),
        "rb": (ny, per, LANES),
    }
    sems = {
        "vsend": 26,
        "vrecv": 26,
        "msend": 26,
        "mrecv": 26,
        "ga_send": parts,
        "ga_recv": parts,
        "gb_send": ny,
        "gb_recv": ny,
        "ha_send": parts,
        "ha_recv": parts,
        "hb_send": ny,
        "hb_recv": ny,
        "ra_send": parts,
        "ra_recv": parts,
        "rb_send": ny,
        "rb_recv": ny,
        "rc_send": parts,
        "rc_recv": parts,
        "stored": 3,
    }
    names = list(ins) + list(outs) + list(narrow) + list(wide) + list(sems) + ["fetched"]
    dec, red, gwp, gwc = pl.pallas_call(
        functools.partial(step_kernel, sizes, scale, names),
        out_shape=[jax.ShapeDtypeStruct(shape, kind) for shape, kind in outs.values()],
        in_specs=[VMEM] * (len(ins) - 1) + [HBM],
        out_specs=[VMEM] * (len(outs) - 1) + [HBM],
        scratch_shapes=[pltpu.VMEM(shape, BF) for shape in narrow.values()]
        + [pltpu.VMEM(shape, F32) for shape in wide.values()]
        + [pltpu.SemaphoreType.DMA((size,)) for size in sems.values()]
        + [pltpu.SemaphoreType.DMA],
        compiler_params=pltpu.CompilerParams(
            vmem_limit_bytes=62 * 1024 * 1024, collective_id=1, has_side_effects=True
        ),
    )(*ins.values())
    shapes = [(27, 256, 256), (16, 16, 27), (27, 16, 32), (32, 256), (32, 256), (27, 16, 32)]

    def whole(shape):
        return pl.BlockSpec(shape, lambda t: (0,) * len(shape))

    block = pl.BlockSpec((3, 256, 256), lambda t: (t, 0, 0))
    gwc, gwf, gwd, gwl, gwp, gwu = pl.pallas_call(
        last_kernel,
        grid=(9,),
        out_shape=[jax.ShapeDtypeStruct(shape, F32) for shape in shapes],
        in_specs=[block, whole((512, LANES)), whole((32, 256))],
        out_specs=[block] + [whole(shape) for shape in shapes[1:]],
        scratch_shapes=[pltpu.VMEM((432, 16), F32)],
        compiler_params=pltpu.CompilerParams(dimension_semantics=("arbitrary",)),
    )(gwc, red.reshape(512, LANES), gwp)
    gwf = jnp.transpose(gwf, (2, 0, 1))
    gwu = jnp.transpose(gwu, (0, 2, 1))
    return dec, gwf, gwd, gwl, gwc, jnp.transpose(gwp), gwu


def solution(mesh):
    sizes = tuple(mesh.shape[name] for name in ("gx", "gy", "gz"))
    block = P(None, "gx", "gy", "gz")
    return jax.shard_map(
        functools.partial(shards, sizes),
        mesh=mesh,
        in_specs=(block, P(), P(), P(), P(), P(), P(), block),
        out_specs=(block, P(), P(), P(), P(), P(), P()),
        check_vma=False,
    )
```

time: 693 us -> 103 us (0.15); the launches traced: 684 us -> 102 us
  waiting for transfers between devices: 322 us -> 0 us
  starting transfers between devices: 123 us -> 0 us
  Pallas kernels: 0 us -> 101 us
  local copies, waits for them, and re-layouts: 80.3 us -> 0.8 us
  blocking collectives: 56.6 us -> 0 us
  matrix products: 56.4 us -> 0 us
  other arithmetic: 28.5 us -> 0 us
  between operations: 17.7 us -> 0.65 us
    psum x2 -> x0, waiting for transfers between devices: 276 us -> none  [the longest x1 147 us: shards(): lax.psum((grad_w_fine, grad_w_down, grad_w_up, grad_w_lift, grad_w_proj),...]
    ppermute x38 -> x0, starting transfers between devices: 123 us -> none  [the longest x19 90.5 us: padded_2(): lax.ppermute(tail, axis, [(i, (i + 1) % count) for i in range(ends)])]
    pallas_call x0 -> x2, Pallas kernels: none -> 101 us  [the longest x1 92.7 us: shards(): pl.pallas_call(functools.partial(step_kernel, sizes, scale, names), out_s...]
    all_gather x2 -> x0, blocking collectives: 56.6 us -> none  [column_border(): column = lax.all_gather(values, 'gy', axis=1, tiled=True)]
    dot_general x105 -> x0, matrix products: 56.4 us -> none  [the longest x45 26.1 us: apply_taps(): jnp.einsum('kcxyz,kco->oxyz', stacked, tap_weights, preferred_element_typ...]
    ppermute x38 -> x0, waiting for transfers between devices: 45.6 us -> none  [the longest x19 43.2 us: padded_2(): lax.ppermute(head, axis, [((i + 1) % count, i) for i in range(ends)])]
    unnamed x382 -> x3, local copies, waits for them, and re-layouts: 41 us -> 0.8 us
    reduce_sum x5 -> x0, other arithmetic: 10.3 us -> none  [pool_sum(): return jnp.sum(shaped, axis=(2, 4, 6))]
  transfers between devices with their start and end apart: 40 -> 0, of which waited for: 18 -> 0; matrix products, arithmetic and copies ran while one was open for 8% -> 0% of each run, Pallas kernels for 0% -> 0%
where the time goes in v3:
time: 103 us; the launch traced here: 102 us
  Pallas kernels  101 us (98%)
    pallas_call x1, Pallas kernels, shards(): pl.pallas_call(functools.partial(step_kernel, sizes, scale, names), out_s...  92.7 us
    pallas_call x1, Pallas kernels, shards(): pl.pallas_call(last_kernel, grid=(9,), out_shape=[jax.ShapeDtypeStruct(sh...  8.2 us

profile of v3, /device:TPU:1, one launch (start us, length us, event | category | flops | bytes accessed | tf_op | source)
XLA Modules:
  0.0 102.3 jit_solution(8862686320289540041)
XLA Ops:
  0.6 92.7 %shard_map.135 = (bf16[16,8,16,64]{3,2,1,0:T(8,128)(2,1)}, f32[16,32,128]{2,1,0:T(8,128)}, f32[32,256]{1,0:T(8,128)}, bf16[27,256,256]{2,1,0:T(8,128)(2,1)}) custom-call(bf16[16,8,16,64]{3,2,1,0:T(8,128)(2,1)} %refs_0_.1, bf16[16,8,16,64]{3,2,1,0:T(8,128)(2,1)} %refs_1_.1, bf16[16,16,27]{2,1,0:T(8,128)(2,1)} %bitcast.11, bf16[27,16,32]{2,1,0:T(8,128)(2,1)} %refs_3_.1, ...), custom_call_target="tpu_custom_call" | custom-call | tf_op jit(solution)/shard_map/pallas_call | solution.py:1138
  93.3 0.0 copy-start
  93.3 8.2 %shard_map.136 = (f32[27,256,256]{2,1,0:T(8,128)}, f32[16,16,27]{2,1,0:T(8,128)}, f32[27,16,32]{2,1,0:T(8,128)}, f32[32,256]{1,0:T(8,128)}, f32[32,256]{1,0:T(8,128)}, /*index=5*/f32[27,16,32]{2,1,0:T(8,128)}) custom-call(bf16[27,256,256]{2,1,0:T(8,128)(2,1)} %get-tuple-element.18.gwc_ref, f32[512,128]{1,0:T(8,128)} %bitcast.9, ...), custom_call_target="tpu_custom_call" | custom-call | tf_op jit(solution)/shard_map/pallas_call | solution.py:1157
  101.5 0.0 copy-done
  101.5 0.8 copy.16
Async XLA Ops:
  93.3 8.2 %copy-start = (bf16[16,8,16,64]{3,2,1,0:T(8,128)(2,1)S(1)}, bf16[16,8,16,64]{3,2,1,0:T(8,128)(2,1)}, u32[]{:S(2)}) copy-start(bf16[16,8,16,64]{3,2,1,0:T(8,128)(2,1)} %get-tuple-element.34) | copy-start | bytes 786436

commit v4 on v3

--- a/solution.py
+++ b/solution.py
@@ -89,9 +89,13 @@
     return jnp.where(hit, 1.0, 0.0).astype(BF)
 
 
-def pool_tile(ref, sums, x, half):
-    cells = jnp.concatenate([ref[2 * x + a, 4 * half + q] for q in range(4) for a in range(2)], axis=1)
-    return dot(cells, sums)
+def pool_tiles(ref, sums):
+    cells = [
+        jnp.concatenate([ref[2 * x + a, 4 * half + q] for q in range(4) for a in range(2)], axis=1)
+        for x in range(4)
+        for half in range(2)
+    ]
+    return dot(jnp.concatenate(cells, axis=0), sums)
 
 
 def grow_matrix():
@@ -465,9 +469,7 @@
     lax.fori_loop(0, 8, plane, 0)
     sums = pool_matrix()
     r.sums[...] = sums
-    for x in range(4):
-        for half in range(2):
-            r.pg[x, half] = pool_tile(r.ct, sums, x, half).astype(BF)
+    r.pg[...] = pool_tiles(r.ct, sums).astype(BF).reshape(4, 2, 16, LANES)
 
 
 def fine_forward(r):
@@ -508,10 +510,10 @@
     lane = lane_of(32)
     low = jnp.zeros((32, LANES), F32)
     high = low
+    pooled = (pool_tiles(r.act, sums) * 0.125).astype(BF).reshape(4, 2, 16, LANES)
     for x in range(4):
         for half in range(2):
-            pooled = (pool_tile(r.act, sums, x, half) * 0.125).astype(BF)
-            tile = jnp.concatenate([pooled, r.pg[x, half]], axis=0)
+            tile = jnp.concatenate([pooled[x, half], r.pg[x, half]], axis=0)
             r.m[x, half] = tile
             wide = tile.astype(F32)
             for q in range(4):
@@ -844,13 +846,16 @@
 
     r.accf[...] = jnp.zeros(r.accf.shape, F32)
 
-    def taps_fine(x, _):
-        left = jnp.concatenate([r.gf[x + 2 - i] for i in range(3)], axis=0)
-        right = jnp.concatenate([three(r.v3, x, 2 * t) for t in range(8)], axis=1)
-        r.accf[:, pl.ds(0, 144)] += dot_nt(left, right)
-        return 0
-
-    lax.fori_loop(0, 10, taps_fine, 0)
+    def taps_fine(n, _):
+        planes = (2 * n, 2 * n + 1)
+        left = [jnp.concatenate([r.gf[x + 2 - i] for x in planes], axis=1) for i in range(3)]
+        right = [three(r.v3, x, 2 * t) for x in planes for t in range(8)]
+        r.accf[:, pl.ds(0, 144)] += dot_nt(
+            jnp.concatenate(left, axis=0), jnp.concatenate(right, axis=1)
+        )
+        return 0
+
+    lax.fori_loop(0, 5, taps_fine, 0)
 
     for b in range(2):
         pay_rows(r, 48 * b, r.accf[:, b * LANES : (b + 1) * LANES])
@@ -861,19 +866,14 @@
     pay_rows(r, 496, jnp.zeros((16, LANES), F32))
 
 
-def coarse_taps(r, sizes, first, last):
+def coarse_taps(r, sizes, t):
     nx, ny, nz = sizes
     count = nx * ny * 16 * nz
-
-    def taps(t, _):
-        i, j = t // 3, lax.rem(t, 3)
-        block = r.gp3[pl.ds(3 - i, nx), pl.ds(3 - j, 2 * ny)].reshape(count, 768)
-        out = dot(r.cells_t[...], block)
-        for k in range(3):
-            r.gwc[3 * t + k] = out[:, 256 * (2 - k) : 256 * (3 - k)].astype(BF)
-        return 0
-
-    lax.fori_loop(first, last, taps, 0)
+    i, j = t // 3, lax.rem(t, 3)
+    block = r.gp3[pl.ds(3 - i, nx), pl.ds(3 - j, 2 * ny)].reshape(count, 768)
+    out = dot(r.cells_t[...], block)
+    for k in range(3):
+        r.gwc[3 * t + k] = out[:, 256 * (2 - k) : 256 * (3 - k)].astype(BF)
 
 
 def proj_grad(r, sizes):
@@ -895,12 +895,29 @@
     nx, ny, nz = sizes
     count = nx * ny * 16 * nz
     r = types.SimpleNamespace(**dict(zip(names, refs, strict=True)))
-    fetch = pltpu.make_async_copy(r.wc_in, r.wc, r.fetched)
-    fetch.start()
-    greet(sizes, lambda: arrange_volume(r))
+    gx, gy, gz = position()
+    pair = nz % 2 == 0
+    mine = lax.rem(gz, 2) if pair else 0
+    other = (gx, gy, gz + 1 - 2 * mine) if pair else None
+
+    fetch = [
+        pltpu.make_async_copy(source, target, r.fetched.at[n])
+        for n, (source, target) in enumerate(
+            ((r.vol_in, r.vol), (r.cot_in, r.cot), (r.wc_in, r.wc))
+        )
+    ]
+    for copy in fetch:
+        copy.start()
+
+    def arrange():
+        fetch[0].wait()
+        arrange_volume(r)
+
+    greet(sizes, arrange)
 
     def first_wait():
         prepare_weights(r)
+        fetch[1].wait()
         arrange_cotangent(r)
         place_weight(r.wide_lift, r.wl[...])
         place_weight(r.wide_proj, r.wp[...])
@@ -911,7 +928,7 @@
     def second_wait():
         zero_rim(r.al3, 1)
         zero_rim(r.gp3, 2)
-        fetch.wait()
+        fetch[2].wait()
 
         def turn_weights(t, _):
             for k in range(3):
@@ -927,9 +944,35 @@
     gather_round(sizes, (r.pc, r.pcg, r.pstage) + sems, nothing, nothing)
     up_forward(r, sizes, scale)
 
+    decoded = pltpu.make_async_copy(r.dec, r.dec_out, r.fetched.at[3])
+
     def third_wait():
         up_taps(r)
         decode(r)
+        decoded.start()
+
+    far_start, far_first = near_rows(sizes, 3)
+
+    def far_row(n, whose):
+        step = 2 if pair else 1
+        return lax.rem(far_start + far_first + step * n + whose, ny)
+
+    def far_count(whose):
+        return (ny - far_first + 1 - whose) // 2 if pair else ny - far_first
+
+    def far_copies(n, whose):
+        y = far_row(n, whose)
+        return [
+            pltpu.make_async_remote_copy(
+                src_ref=ref.at[:, pl.ds(y, 1)],
+                dst_ref=ref.at[:, pl.ds(y, 1)],
+                send_sem=r.far_send.at[part, n],
+                recv_sem=r.far_recv.at[part, n],
+                device_id=other,
+                device_id_type=MESH,
+            )
+            for part, ref in enumerate((r.actc, r.dsc))
+        ]
 
     def fourth_wait():
         start, have = near_rows(sizes, 5)
@@ -939,85 +982,156 @@
             return 0
 
         lax.fori_loop(have, ny, lift, 0)
-        start_c, have_c = near_rows(sizes, 3)
-
-        def coarse(o, _):
-            coarse_forward(r, sizes, lax.rem(start_c + o, ny), 1)
+
+        def coarse(n, _):
+            coarse_forward(r, sizes, far_row(n, mine), 1)
+            if pair:
+                for copy in far_copies(n, mine):
+                    copy.start()
             return 0
 
-        lax.fori_loop(have_c, ny, coarse, 0)
+        lax.fori_loop(0, far_count(mine), coarse, 0)
 
     sems = (r.ha_send, r.ha_recv, r.hb_send, r.hb_recv)
     gather_round(sizes, (r.gc, r.gcg, r.gstage) + sems, third_wait, fourth_wait)
     backward(r, sizes, scale)
 
-    def store(part, first, last):
-        taps = pl.ds(3 * first, 3 * (last - first))
-        return pltpu.make_async_copy(r.gwc.at[taps], r.gwc_out.at[taps], r.stored.at[part])
-
-    ends = (0, 2, 5, 9)
-
-    def taps_wait(part):
-        def wait():
-            if part == 0:
-                start, have = near_rows(sizes, 3)
-
-                def coarse(o, _):
-                    coarse_grad_row(r, sizes, lax.rem(start + o, ny))
-                    return 0
-
-                lax.fori_loop(have, ny, coarse, 0)
-                r.cells_t[...] = r.alc[...].reshape(count, 256).T
-            coarse_taps(r, sizes, ends[part], ends[part + 1])
-            store(part, ends[part], ends[part + 1]).start()
-            if part == 2:
-                proj_grad(r, sizes)
-
-        return wait
+    half = 5 if pair else 9
+
+    def taps_count(whose):
+        return half - whose
+
+    def keep_taps(n):
+        taps = pl.ds(3 * (n + half * mine), 3)
+        return pltpu.make_async_copy(r.gwc.at[taps], r.gwc_out.at[taps], r.kept.at[n])
+
+    def send_taps(n, whose):
+        taps = pl.ds(3 * (n + half * whose), 3)
+        return pltpu.make_async_remote_copy(
+            src_ref=r.gwc.at[taps],
+            dst_ref=r.gwc_out.at[taps],
+            send_sem=r.tap_send.at[n],
+            recv_sem=r.tap_recv.at[n],
+            device_id=other,
+            device_id_type=MESH,
+        )
+
+    def do_taps(first, last):
+        def taps(n, _):
+            coarse_taps(r, sizes, n + half * mine)
+            keep_taps(n).start()
+            if pair:
+                send_taps(n, mine).start()
+            return 0
+
+        lax.fori_loop(first, last, taps, 0)
+
+    def wait_a():
+        if pair:
+
+            def arrived(n, _):
+                for copy in far_copies(n, 1 - mine):
+                    copy.wait_recv()
+                return 0
+
+            lax.fori_loop(0, far_count(1 - mine), arrived, 0)
+        start, have = near_rows(sizes, 3)
+
+        def coarse(o, _):
+            coarse_grad_row(r, sizes, lax.rem(start + o, ny))
+            return 0
+
+        lax.fori_loop(have, ny, coarse, 0)
+        r.cells_t[...] = r.alc[...].reshape(count, 256).T
+        do_taps(0, 1)
+
+    def wait_b():
+        do_taps(1, 3)
+
+    def wait_c():
+        do_taps(3, taps_count(mine))
+        proj_grad(r, sizes)
 
     sems = (r.ra_send, r.ra_recv, r.rb_send, r.rb_recv, r.rc_send, r.rc_recv)
-    reduce_round(sizes, (r.pay, r.red, r.ra, r.rb) + sems, [taps_wait(part) for part in range(3)])
-    for part in range(3):
-        store(part, ends[part], ends[part + 1]).wait()
-
-
-def last_kernel(gwc_ref, red_ref, gwp_ref, wc_out, wf_out, wd_out, wl_out, wp_out, wu_out, rows):
-    step = pl.program_id(0)
+    reduce_round(sizes, (r.pay, r.red, r.ra, r.rb) + sems, (wait_a, wait_b, wait_c))
+
+    def finish(n, _):
+        keep_taps(n).wait()
+        if pair:
+            send_taps(n, mine).wait_send()
+        return 0
+
+    lax.fori_loop(0, taps_count(mine), finish, 0)
+    decoded.wait()
+    if pair:
+
+        def sent(n, _):
+            for copy in far_copies(n, mine):
+                copy.wait_send()
+            return 0
+
+        def landed(n, _):
+            send_taps(n, 1 - mine).wait_recv()
+            return 0
+
+        lax.fori_loop(0, far_count(mine), sent, 0)
+        lax.fori_loop(0, taps_count(1 - mine), landed, 0)
+
+
+def last_kernel(
+    gwc_in,
+    red_ref,
+    gwp_ref,
+    wc_out,
+    wf_out,
+    wd_out,
+    wl_out,
+    wp_out,
+    wu_out,
+    rows,
+    narrow,
+    wide,
+    load_sem,
+    store_sem,
+):
+    blocks = [pl.ds(3 * n, 3) for n in range(9)]
+    loads = [
+        pltpu.make_async_copy(gwc_in.at[block], narrow.at[block], load_sem.at[n])
+        for n, block in enumerate(blocks)
+    ]
+    stores = [
+        pltpu.make_async_copy(wide.at[block], wc_out.at[block], store_sem.at[n])
+        for n, block in enumerate(blocks)
+    ]
+    for load in loads:
+        load.start()
+    for n, block in enumerate(blocks):
+        loads[n].wait()
+        wide[block] = narrow[block].astype(F32)
+        stores[n].start()
 
     def columns(start, blocks, count):
         return jnp.concatenate(
             [red_ref[pl.ds(start + count * b, count)] for b in range(blocks)], axis=1
         )
 
-    @pl.when(step == 0)
-    def _():
-        table = columns(0, 2, 48)
-        for i in range(3):
-            rows[pl.ds(144 * i, 144)] = table[16 * i : 16 * i + 16, :144].T
-        for c in range(16):
-            wf_out[c] = rows[pl.ds(c, 27, stride=16)].T
-
-    @pl.when(step == 1)
-    def _():
-        table = columns(96, 3, 48)
-        for i in range(3):
-            for jk in range(9):
-                tile = table[16 * i : 16 * i + 16, 32 * jk : 32 * jk + 32]
-                wu_out[9 * i + jk] = tile
-
-    @pl.when(step == 2)
-    def _():
-        table = columns(240, 2, 96)
-        for i in range(3):
-            part = table[32 * i : 32 * i + 32, :144]
-            wd_out[pl.ds(9 * i, 9)] = part.T.reshape(9, 16, 32)
-
-    @pl.when(step == 3)
-    def _():
-        wl_out[...] = columns(432, 2, 32)
-        wp_out[...] = gwp_ref[...]
-
-    wc_out[...] = gwc_ref[...].astype(F32)
+    table = columns(0, 2, 48)
+    for i in range(3):
+        rows[pl.ds(144 * i, 144)] = table[16 * i : 16 * i + 16, :144].T
+    for c in range(16):
+        wf_out[c] = rows[pl.ds(c, 27, stride=16)].T
+    table = columns(96, 3, 48)
+    for i in range(3):
+        for jk in range(9):
+            wu_out[9 * i + jk] = table[16 * i : 16 * i + 16, 32 * jk : 32 * jk + 32]
+    table = columns(240, 2, 96)
+    for i in range(3):
+        part = table[32 * i : 32 * i + 32, :144]
+        wd_out[pl.ds(9 * i, 9)] = part.T.reshape(9, 16, 32)
+    wl_out[...] = columns(432, 2, 32)
+    wp_out[...] = gwp_ref[...]
+    for store in stores:
+        store.wait()
 
 
 VMEM = pl.BlockSpec(memory_space=pltpu.VMEM)
@@ -1033,22 +1147,25 @@
     grid = (nx, ny, 2, cells, 256)
     gathered = (ny, nx, cells, LANES)
     ins = {
-        "vol": volume,
-        "cot": cotangent,
         "wf_in": jnp.transpose(w_fine, (1, 2, 0)),
         "wd_in": w_down,
         "wu_in": jnp.transpose(w_up, (0, 2, 1)),
         "wl": w_lift,
         "wp": jnp.transpose(w_proj),
+        "vol_in": volume,
+        "cot_in": cotangent,
         "wc_in": w_coarse.reshape(9, 768, 256),
     }
     outs = {
-        "dec": ((16, 8, 16, 64), BF),
         "red": ((parts, per, LANES), F32),
         "gwp": ((32, 256), F32),
+        "dec_out": ((16, 8, 16, 64), BF),
         "gwc_out": ((27, 256, 256), BF),
     }
     narrow = {
+        "vol": (16, 8, 16, 64),
+        "cot": (16, 8, 16, 64),
+        "dec": (16, 8, 16, 64),
         "v": (8, 8, 16, LANES),
         "ve": (2, 16, LANES),
         "vp": (10, 10, 16, LANES),
@@ -1132,36 +1249,41 @@
         "rb_recv": ny,
         "rc_send": parts,
         "rc_recv": parts,
-        "stored": 3,
+        "kept": 9,
+        "tap_send": 9,
+        "tap_recv": 9,
+        "fetched": 4,
     }
-    names = list(ins) + list(outs) + list(narrow) + list(wide) + list(sems) + ["fetched"]
-    dec, red, gwp, gwc = pl.pallas_call(
+    far = {"far_send": (2, ny), "far_recv": (2, ny)}
+    names = list(ins) + list(outs) + list(narrow) + list(wide) + list(sems) + list(far)
+    red, gwp, dec, gwc = pl.pallas_call(
         functools.partial(step_kernel, sizes, scale, names),
         out_shape=[jax.ShapeDtypeStruct(shape, kind) for shape, kind in outs.values()],
-        in_specs=[VMEM] * (len(ins) - 1) + [HBM],
-        out_specs=[VMEM] * (len(outs) - 1) + [HBM],
+        in_specs=[VMEM] * (len(ins) - 3) + [HBM] * 3,
+        out_specs=[VMEM] * 2 + [HBM] * 2,
         scratch_shapes=[pltpu.VMEM(shape, BF) for shape in narrow.values()]
         + [pltpu.VMEM(shape, F32) for shape in wide.values()]
         + [pltpu.SemaphoreType.DMA((size,)) for size in sems.values()]
-        + [pltpu.SemaphoreType.DMA],
+        + [pltpu.SemaphoreType.DMA(shape) for shape in far.values()],
         compiler_params=pltpu.CompilerParams(
             vmem_limit_bytes=62 * 1024 * 1024, collective_id=1, has_side_effects=True
         ),
     )(*ins.values())
     shapes = [(27, 256, 256), (16, 16, 27), (27, 16, 32), (32, 256), (32, 256), (27, 16, 32)]
 
-    def whole(shape):
-        return pl.BlockSpec(shape, lambda t: (0,) * len(shape))
-
-    block = pl.BlockSpec((3, 256, 256), lambda t: (t, 0, 0))
     gwc, gwf, gwd, gwl, gwp, gwu = pl.pallas_call(
         last_kernel,
-        grid=(9,),
         out_shape=[jax.ShapeDtypeStruct(shape, F32) for shape in shapes],
-        in_specs=[block, whole((512, LANES)), whole((32, 256))],
-        out_specs=[block] + [whole(shape) for shape in shapes[1:]],
-        scratch_shapes=[pltpu.VMEM((432, 16), F32)],
-        compiler_params=pltpu.CompilerParams(dimension_semantics=("arbitrary",)),
+        in_specs=[HBM, VMEM, VMEM],
+        out_specs=[HBM] + [VMEM] * 5,
+        scratch_shapes=[
+            pltpu.VMEM((432, 16), F32),
+            pltpu.VMEM((27, 256, 256), BF),
+            pltpu.VMEM((27, 256, 256), F32),
+            pltpu.SemaphoreType.DMA((9,)),
+            pltpu.SemaphoreType.DMA((9,)),
+        ],
+        compiler_params=pltpu.CompilerParams(vmem_limit_bytes=32 * 1024 * 1024),
     )(gwc, red.reshape(512, LANES), gwp)
     gwf = jnp.transpose(gwf, (2, 0, 1))
     gwu = jnp.transpose(gwu, (0, 2, 1))

time: 103 us -> 103 us (level)
  Pallas kernels: 101 us -> 97.2 us
  local copies, waits for them, and re-layouts: 0.8 us -> 4.5 us
    unnamed x3 -> x9, local copies, waits for them, and re-layouts: 0.8 us -> 4.5 us
    pallas_call x1, Pallas kernels: 8.2 us -> 5.61 us  [shards(): pl.pallas_call(last_kernel, out_shape=[jax.ShapeDtypeStruct(shape, F32) f...]
    pallas_call x1, Pallas kernels: 92.7 us -> 91.6 us  [shards(): pl.pallas_call(functools.partial(step_kernel, sizes, scale, names), out_s...]
where the time goes in v4:
time: 103 us; the launch traced here: 102 us
  Pallas kernels  97.2 us (94%)
  local copies, waits for them, and re-layouts  4.5 us (4%)
    pallas_call x1, Pallas kernels, shards(): pl.pallas_call(functools.partial(step_kernel, sizes, scale, names), out_s...  91.6 us
    pallas_call x1, Pallas kernels, shards(): pl.pallas_call(last_kernel, out_shape=[jax.ShapeDtypeStruct(shape, F32) f...  5.61 us
    unnamed x9, local copies, waits for them, and re-layouts  4.5 us

profile of v4, /device:TPU:1, one launch (start us, length us, event | category | flops | bytes accessed | tf_op | source)
XLA Modules:
  0.0 102.4 jit_solution(15403864774814996891)
XLA Ops:
  0.6 91.6 %shard_map.135 = (f32[16,32,128]{2,1,0:T(8,128)}, f32[32,256]{1,0:T(8,128)}, bf16[16,8,16,64]{3,2,1,0:T(8,128)(2,1)}, bf16[27,256,256]{2,1,0:T(8,128)(2,1)}) custom-call(bf16[16,16,27]{2,1,0:T(8,128)(2,1)} %bitcast.11, bf16[27,16,32]{2,1,0:T(8,128)(2,1)} %refs_1_.1, bf16[27,16,32]{2,1,0:T(8,128)(2,1)} %bitcast.10, bf16[32,256]{1,0:T(8,128)(2,1)} %refs_3_.1, ...), custom_call_target="tpu_custom_call" | custom-call | tf_op jit(solution)/shard_map/pallas_call | solution.py:1259
  92.3 0.0 copy-start
  92.3 2.0 %copy-done = bf16[27,256,256]{2,1,0:T(8,128)(2,1)S(1)} copy-done((bf16[27,256,256]{2,1,0:T(8,128)(2,1)S(1)}, bf16[27,256,256]{2,1,0:T(8,128)(2,1)}, u32[]{:S(2)}) %copy-start) | copy-done | bytes 3538968
  94.3 0.0 copy-start.1
  94.3 0.9 copy-done.1
  95.2 0.0 copy-start.2
  95.2 0.8 copy-done.2
  96.0 0.0 copy-start.3
  96.0 5.6 %shard_map.136 = (f32[27,256,256]{2,1,0:T(8,128)}, f32[16,16,27]{2,1,0:T(8,128)}, f32[27,16,32]{2,1,0:T(8,128)}, f32[32,256]{1,0:T(8,128)}, f32[32,256]{1,0:T(8,128)}, /*index=5*/f32[27,16,32]{2,1,0:T(8,128)}) custom-call(bf16[27,256,256]{2,1,0:T(8,128)(2,1)S(1)} %copy-done, f32[512,128]{1,0:T(8,128)S(1)} %bitcast.8, f32[32,256]{1,0:T(8,128)S(1)} %copy-done.2), custom_call_target="tpu_custom_call" | custom-call | tf_op jit(solution)/shard_map/pallas_call | solution.py:1274
  101.6 0.0 copy-done.3
  101.6 0.8 copy.16
Async XLA Ops:
  92.3 2.0 %copy-start = (bf16[27,256,256]{2,1,0:T(8,128)(2,1)S(1)}, bf16[27,256,256]{2,1,0:T(8,128)(2,1)}, u32[]{:S(2)}) copy-start(bf16[27,256,256]{2,1,0:T(8,128)(2,1)} %get-tuple-element.18.gwc_in) | copy-start | bytes 10616836
  94.3 0.9 copy-start.1
  95.2 0.8 copy-start.2
  96.0 5.6 %copy-start.3 = (bf16[16,8,16,64]{3,2,1,0:T(8,128)(2,1)S(1)}, bf16[16,8,16,64]{3,2,1,0:T(8,128)(2,1)}, u32[]{:S(2)}) copy-start(bf16[16,8,16,64]{3,2,1,0:T(8,128)(2,1)} %get-tuple-element.34) | copy-start | bytes 786436

commit v5 on v4

--- a/solution.py
+++ b/solution.py
@@ -58,9 +58,9 @@
 def store_taps(ref, x, pairs):
     stacks = [tap_rows(pair) for pair in pairs]
     for n, stack in enumerate(stacks):
-        ref[x, 2 * n] = stack.astype(BF)
+        ref[x, 2 * n] = stack
         if n + 1 < len(stacks):
-            ref[x, 2 * n + 1] = between(stack, stacks[n + 1]).astype(BF)
+            ref[x, 2 * n + 1] = between(stack, stacks[n + 1])
 
 
 def three(ref, x, y):
@@ -68,17 +68,17 @@
     return block.reshape(3 * block.shape[1], LANES)
 
 
-def conv(weight, ref, planes, starts):
+def conv(weight, ref, first, planes, starts):
     outs = weight.shape[0] // 3
     parts = []
-    for x in range(planes + 2):
-        tiles = [three(ref, x, y) for y in starts]
+    for n in range(planes + 2):
+        tiles = [three(ref, first + n, y) for y in starts]
         block = tiles[0] if len(tiles) == 1 else jnp.concatenate(tiles, axis=1)
         parts.append(dot(weight, block))
-        if x >= 2:
+        if n >= 2:
             yield (
-                x - 2,
-                parts[x - 2][:outs] + parts[x - 1][outs : 2 * outs] + parts[x][2 * outs :],
+                first + n - 2,
+                parts[n - 2][:outs] + parts[n - 1][outs : 2 * outs] + parts[n][2 * outs :],
             )
 
 
@@ -481,23 +481,23 @@
         for t in range(10):
             dy, sy = (t + 7) // 8, (t + 7) % 8
             at = sy * 8 + sx
-            tile = r.vp[x, t].astype(F32)
-            left = turn(r.vel[dx, dy].astype(F32), -at)
-            right = turn(r.ver[dx, dy].astype(F32), 63 - at)
+            tile = r.vp[x, t]
+            left = turn(r.vel[dx, dy], -at)
+            right = turn(r.ver[dx, dy], 63 - at)
             before = jnp.where(spot == 0, left, turn(tile, 1))
             after = jnp.where(spot == 63, right, turn(tile, -1))
             stacks.append(jnp.concatenate([before, tile, after], axis=0))
         for t in range(9):
             if t > 0:
-                r.v3[x, 2 * t - 1] = stacks[t].astype(BF)
-            r.v3[x, 2 * t] = between(stacks[t], stacks[t + 1]).astype(BF)
+                r.v3[x, 2 * t - 1] = stacks[t]
+            r.v3[x, 2 * t] = between(stacks[t], stacks[t + 1])
         return 0
 
     lax.fori_loop(0, 10, rows, 0)
     weight = r.wf[...]
 
     def convs(g, _):
-        for x, pre in conv(weight, r.v3, 8, (4 * g, 4 * g + 2)):
+        for x, pre in conv(weight, r.v3, 0, 8, (4 * g, 4 * g + 2)):
             act = (pre * sigmoid(pre)).astype(BF)
             for b in range(2):
                 r.pre[x, 2 * g + b] = pre[:, b * LANES : (b + 1) * LANES]
@@ -525,43 +525,48 @@
     r.me[1] = high.astype(BF)
 
 
-def mid_forward(r, sizes):
-    nx, ny, nz = sizes
-    gx, gy, gz = position()
+def mid_rows(r, first, last):
     lane = lane_of(32)
     spot = lane % 64
+    none = jnp.zeros((32, LANES), BF)
 
     def rows(x, _):
         dx, sx = x // 4, lax.rem(x, 4)
         pairs = []
         for a in range(8):
             dy, sy = (a + 2) // 4, (a + 2) % 4
-            tile = r.mp[x, a // 2].astype(F32)
+            tile = r.mp[x, a // 2]
             q = 2 * (a % 2)
             base = jnp.where(lane < 64, turn(tile, 8 - 32 * q), turn(tile, 40 - 32 * q))
             at = (sx * 4 + sy) * 4
-            right = turn(r.mer[dx, dy].astype(F32), 40 - at)
-            left = turn(r.mel[dx, dy].astype(F32), 4 - at)
-            row = jnp.where(spot < 44, right, 0.0)
+            right = turn(r.mer[dx, dy], 40 - at)
+            left = turn(r.mel[dx, dy], 4 - at)
+            row = jnp.where(spot < 44, right, none)
             row = jnp.where(spot < 40, base, row)
             row = jnp.where(spot < 8, left, row)
-            row = jnp.where(spot < 4, 0.0, row)
-            r.pgp[x, a] = row[16:].astype(BF)
+            row = jnp.where(spot < 4, none, row)
+            r.pgp[x, a] = row[16:]
             pairs.append(row[:16])
         store_taps(r.pm3, x, pairs)
         r.pm3[x, 15] = jnp.zeros((48, LANES), BF)
         r.pm3[x, 16] = jnp.zeros((48, LANES), BF)
         return 0
 
-    lax.fori_loop(0, 12, rows, 0)
+    lax.fori_loop(first, last, rows, 0)
+
+
+def mid_convs(r, sizes, first, planes, groups):
+    nx, ny, nz = sizes
+    gx, gy, gz = position()
+    lane = lane_of(32)
     weight = r.wd[...]
-    cell = spot - 8
+    cell = lane % 64 - 8
     mid = cell + gz * 32
     inside = (cell >= -3) & (cell < 35) & (mid >= 0) & (mid < 32 * nz)
     second = lane // 64
 
     def convs(g, _):
-        for x, both in conv(weight, r.pm3, 10, (4 * g, 4 * g + 2)):
+        for x, both in conv(weight, r.pm3, first, planes, (4 * g, 4 * g + 2)):
             at_x = gx * 4 + x - 3
             for b in range(2):
                 pre = both[:, b * LANES : (b + 1) * LANES]
@@ -573,7 +578,12 @@
                 r.dsm[x, 2 * g + b] = jnp.where(keep, slope(pre, sig), 0.0).astype(BF)
         return 0
 
-    lax.fori_loop(0, 4, convs, 0)
+    lax.fori_loop(*groups, convs, 0)
+
+
+def mid_own(r, sizes):
+    mid_rows(r, 3, 9)
+    mid_convs(r, sizes, 3, 4, (0, 3))
     halves = [
         jnp.concatenate([r.am[3 + a, 1 + 2 * h + m] for a in range(4) for m in range(3)], axis=1)
         for h in range(2)
@@ -584,6 +594,14 @@
     hit = coarse_sum_matrix(12) & ((third == 1) | ((third == 0) == (upper == 1)))
     pooled = dot_nt(jnp.where(hit, 1.0, 0.0).astype(BF), cells) * (1.0 / 64.0)
     r.pc[...] = pooled.astype(BF).astype(F32)
+
+
+def mid_halo(r, sizes):
+    mid_rows(r, 0, 3)
+    mid_rows(r, 9, 12)
+    mid_convs(r, sizes, 0, 3, (0, 4))
+    mid_convs(r, sizes, 7, 3, (0, 4))
+    mid_convs(r, sizes, 3, 4, (3, 4))
 
 
 def near_rows(sizes, count):
@@ -621,43 +639,29 @@
         r.dsc[x, pl.ds(y, have)] = slope(pre, sig).astype(BF).reshape(have, 2, cells, 256)
 
 
-def up_forward(r, sizes, scale):
-    cells = 8 * sizes[2]
-    gz = lax.axis_index("gz")
-    start, have = near_rows(sizes, 5)
-
-    def lift(o, _):
-        lift_row(r, sizes, start + o)
-        return 0
-
-    lax.fori_loop(0, have, lift, 0)
-    coarse_forward(r, sizes, *near_rows(sizes, 3))
-
-    spread = coarse_grow_matrix(cells, gz)
-    for dx, dy, x, y, y2, keep in near_cells(sizes):
-        out = dot_nt(r.wp[...], r.actc[x, y, y2]).astype(BF)
-        r.cos[dx, dy] = dot(out, spread) * keep
-
-    first = lane_of(32) < 64
+def join_planes(r, first, last):
+    lower_row = lane_of(32) < 64
 
     def join(x, _):
         pairs = []
         for m in range(7):
             lower = r.cos[(x + 1) // 4, (2 * m + 1) // 4]
             upper = r.cos[(x + 1) // 4, (2 * m + 2) // 4]
-            row = r.am[x, m].astype(F32) + jnp.where(first, lower, upper)
-            pairs.append(row.astype(BF).astype(F32))
+            row = r.am[x, m].astype(F32) + jnp.where(lower_row, lower, upper)
+            pairs.append(row.astype(BF))
         store_taps(r.j3, x, pairs)
         return 0
 
-    lax.fori_loop(0, 10, join, 0)
-
+    lax.fori_loop(first, last, join, 0)
+
+
+def up_planes(r, scale, first, planes):
     cell = lane_of(16) % 64 - 8
     near = (cell >= -2) & (cell < 34)
     weight = r.wu[...]
 
     def up(g, _):
-        for x, both in conv(weight, r.j3, 8, (4 * g, 4 * g + 2)):
+        for x, both in conv(weight, r.j3, first, planes, (4 * g, 4 * g + 2)):
             for b in range(2):
                 pre = both[:, b * LANES : (b + 1) * LANES]
                 sig = sigmoid(pre)
@@ -670,17 +674,51 @@
     lax.fori_loop(0, 3, up, 0)
 
     def stack(x, _):
-        store_taps(r.gu3, x, [r.guo[x, m].astype(F32) for m in range(6)])
-        return 0
-
-    lax.fori_loop(0, 8, stack, 0)
-
+        store_taps(r.gu3, x, [r.guo[x, m] for m in range(6)])
+        return 0
+
+    lax.fori_loop(first, first + planes, stack, 0)
+
+
+def up_back_planes(r, first, planes):
     weight_t = r.wut[...]
     for starts in ((0, 2), (4, 6), (8,)):
-        for x, both in conv(weight_t, r.gu3, 6, starts):
+        for x, both in conv(weight_t, r.gu3, first, planes, starts):
             for b, y in enumerate(starts):
                 r.gj[x, y // 2] = both[:, b * LANES : (b + 1) * LANES]
 
+
+def up_halo(r, scale):
+    join_planes(r, 0, 1)
+    join_planes(r, 9, 10)
+    for x in (0, 7):
+        up_planes(r, scale, x, 1)
+    for x in (0, 5):
+        up_back_planes(r, x, 1)
+
+
+def up_forward(r, sizes, scale):
+    cells = 8 * sizes[2]
+    gz = lax.axis_index("gz")
+    start, have = near_rows(sizes, 5)
+
+    def lift(o, _):
+        lift_row(r, sizes, start + o)
+        return 0
+
+    lax.fori_loop(0, have, lift, 0)
+    coarse_forward(r, sizes, *near_rows(sizes, 3))
+
+    spread = coarse_grow_matrix(cells, gz)
+    for dx, dy, x, y, y2, keep in near_cells(sizes):
+        out = dot_nt(r.wp[...], r.actc[x, y, y2]).astype(BF)
+        r.cos[dx, dy] = dot(out, spread) * keep
+
+    join_planes(r, 1, 9)
+    up_planes(r, scale, 1, 6)
+    up_back_planes(r, 1, 4)
+
+    first = lane_of(32) < 64
     totals = []
     for h in range(2):
         total = None
@@ -794,7 +832,7 @@
             upper = r.cos[(x + 3) // 4, (2 * n + 4) // 4]
             row = r.gj[x, n] + jnp.where(first, lower, upper)
             row = row * r.dsm[x + 2, n + 1].astype(F32)
-            pairs.append(row.astype(BF).astype(F32))
+            pairs.append(row.astype(BF))
         store_taps(r.gm3, x, pairs)
         return 0
 
@@ -802,7 +840,7 @@
 
     weight_t = r.wdt[...]
     for starts in ((0, 2), (4, 6)):
-        for x, both in conv(weight_t, r.gm3, 4, starts):
+        for x, both in conv(weight_t, r.gm3, 0, 4, starts):
             for b, y in enumerate(starts):
                 r.gpm[x, pl.ds(8 * y, 16)] = both[:, b * LANES : (b + 1) * LANES].astype(BF)
 
@@ -939,14 +977,15 @@
         lax.fori_loop(0, 9, turn_weights, 0)
 
     halo_round(sizes, 4, 1, (r.m, r.me, r.mp, r.mer, r.mel, r.msend, r.mrecv), second_wait)
-    mid_forward(r, sizes)
+    mid_own(r, sizes)
     sems = (r.ga_send, r.ga_recv, r.gb_send, r.gb_recv)
-    gather_round(sizes, (r.pc, r.pcg, r.pstage) + sems, nothing, nothing)
+    gather_round(sizes, (r.pc, r.pcg, r.pstage) + sems, lambda: mid_halo(r, sizes), nothing)
     up_forward(r, sizes, scale)
 
     decoded = pltpu.make_async_copy(r.dec, r.dec_out, r.fetched.at[3])
 
     def third_wait():
+        up_halo(r, scale)
         up_taps(r)
         decode(r)
         decoded.start()
@@ -1283,7 +1322,7 @@
             pltpu.SemaphoreType.DMA((9,)),
             pltpu.SemaphoreType.DMA((9,)),
         ],
-        compiler_params=pltpu.CompilerParams(vmem_limit_bytes=32 * 1024 * 1024),
+        compiler_params=pltpu.CompilerParams(vmem_limit_bytes=62 * 1024 * 1024),
     )(gwc, red.reshape(512, LANES), gwp)
     gwf = jnp.transpose(gwf, (2, 0, 1))
     gwu = jnp.transpose(gwu, (0, 2, 1))

time: 103 us -> 95.6 us (0.928)
  local copies, waits for them, and re-layouts: 4.5 us -> 0.8 us
  Pallas kernels: 97.2 us -> 94 us
    unnamed x9 -> x3, local copies, waits for them, and re-layouts: 4.5 us -> 0.8 us
    pallas_call x1, Pallas kernels: 91.6 us -> 88 us  [shards(): pl.pallas_call(functools.partial(step_kernel, sizes, scale, names), out_s...]
where the time goes in v5:
time: 95.6 us; the launch traced here: 95.4 us
  Pallas kernels  94 us (98%)
    pallas_call x1, Pallas kernels, shards(): pl.pallas_call(functools.partial(step_kernel, sizes, scale, names), out_s...  88 us
    pallas_call x1, Pallas kernels, shards(): pl.pallas_call(last_kernel, out_shape=[jax.ShapeDtypeStruct(shape, F32) f...  5.94 us

profile of v5, /device:TPU:1, one launch (start us, length us, event | category | flops | bytes accessed | tf_op | source)
XLA Modules:
  0.0 95.4 jit_solution(12376245303998815121)
XLA Ops:
  0.6 88.0 %shard_map.135 = (f32[16,32,128]{2,1,0:T(8,128)}, f32[32,256]{1,0:T(8,128)}, bf16[16,8,16,64]{3,2,1,0:T(8,128)(2,1)}, bf16[27,256,256]{2,1,0:T(8,128)(2,1)}) custom-call(bf16[16,16,27]{2,1,0:T(8,128)(2,1)} %bitcast.11, bf16[27,16,32]{2,1,0:T(8,128)(2,1)} %refs_1_.1, bf16[27,16,32]{2,1,0:T(8,128)(2,1)} %bitcast.10, bf16[32,256]{1,0:T(8,128)(2,1)} %refs_3_.1, ...), custom_call_target="tpu_custom_call" | custom-call | tf_op jit(solution)/shard_map/pallas_call | solution.py:1298
  88.7 0.0 copy-start
  88.7 5.9 %shard_map.136 = (f32[27,256,256]{2,1,0:T(8,128)}, f32[16,16,27]{2,1,0:T(8,128)}, f32[27,16,32]{2,1,0:T(8,128)}, f32[32,256]{1,0:T(8,128)}, f32[32,256]{1,0:T(8,128)}, /*index=5*/f32[27,16,32]{2,1,0:T(8,128)}) custom-call(bf16[27,256,256]{2,1,0:T(8,128)(2,1)} %get-tuple-element.18.gwc_in, f32[512,128]{1,0:T(8,128)} %bitcast.9, ...), custom_call_target="tpu_custom_call" | custom-call | tf_op jit(solution)/shard_map/pallas_call | solution.py:1313
  94.6 0.0 copy-done
  94.6 0.8 copy.16
Async XLA Ops:
  88.7 6.0 %copy-start = (bf16[16,8,16,64]{3,2,1,0:T(8,128)(2,1)S(1)}, bf16[16,8,16,64]{3,2,1,0:T(8,128)(2,1)}, u32[]{:S(2)}) copy-start(bf16[16,8,16,64]{3,2,1,0:T(8,128)(2,1)} %get-tuple-element.34) | copy-start | bytes 786436

commit v6 on v5

--- a/solution.py
+++ b/solution.py
@@ -339,12 +339,20 @@
     for oy in range(1, ny):
         second(oy, gy).start()
     second_wait()
-    for k, (ox, oz) in enumerate(plane):
-        first(k, gx, gz, (lax.rem(gx + ox, nx), gy, lax.rem(gz + oz, nz))).wait_send()
-    for oy in range(1, ny):
+    near = sorted({1, ny - 1}) if ny > 1 else []
+    for oy in near:
         second(oy, lax.rem(gy + ny - oy, ny)).wait_recv()
-    for oy in range(1, ny):
-        second(oy, gy).wait_send()
+
+    def rest():
+        for k, (ox, oz) in enumerate(plane):
+            first(k, gx, gz, (lax.rem(gx + ox, nx), gy, lax.rem(gz + oz, nz))).wait_send()
+        for oy in range(1, ny):
+            if oy not in near:
+                second(oy, lax.rem(gy + ny - oy, ny)).wait_recv()
+        for oy in range(1, ny):
+            second(oy, gy).wait_send()
+
+    return rest
 
 
 def reduce_round(sizes, refs, waits):
@@ -604,11 +612,9 @@
     mid_convs(r, sizes, 3, 4, (3, 4))
 
 
-def near_rows(sizes, count):
+def coarse_pair(sizes, o):
     ny = sizes[1]
-    have = min(count, ny)
-    start = lax.axis_index("gy") - count // 2
-    return jnp.minimum(jnp.maximum(start, 0), ny - have), have
+    return lax.rem(lax.axis_index("gy") + o + ny - 1, ny)
 
 
 def lift_row(r, sizes, y):
@@ -617,26 +623,30 @@
             pre = dot(r.pcg[y, x], r.wide_lift[y2])
             act = (pre * sigmoid(pre)).astype(BF)
             r.alc[x, y, y2] = act
-            store_coarse_taps(r.al3, (x + 1, 2 * y + y2 + 1), act.astype(F32))
-
-
-def coarse_forward(r, sizes, y, have):
-    nx, cells = sizes[0], 8 * sizes[2]
-    rows = nx * 2 * have * cells
+            store_coarse_taps(r.al3, (x + 2, 2 * y + y2 + 2), act.astype(F32))
+
+
+def coarse_conv(r, source, weight, x, planes, y, rows, cells):
+    count = planes * rows * cells
     for i in range(3):
         for j in range(3):
-            block = r.al3[pl.ds(i, nx), pl.ds(2 * y + j, 2 * have)].reshape(rows, 768)
-            part = dot(block, r.wc[3 * i + j])
+            block = source[pl.ds(x + i, planes), pl.ds(y + j, rows)].reshape(count, 768)
+            part = dot(block, weight[3 * i + j])
             if i + j == 0:
-                r.acc[pl.ds(0, rows)] = part
+                r.acc[pl.ds(0, count)] = part
             else:
-                r.acc[pl.ds(0, rows)] += part
-    per = 2 * have * cells
+                r.acc[pl.ds(0, count)] += part
+
+
+def coarse_forward(r, sizes, y):
+    nx, cells = sizes[0], 8 * sizes[2]
+    coarse_conv(r, r.al3, r.wc, 1, nx, 2 * y + 1, 2, cells)
+    per = 2 * cells
     for x in range(nx):
         pre = r.acc[pl.ds(x * per, per)]
         sig = sigmoid(pre)
-        r.actc[x, pl.ds(y, have)] = (pre * sig).astype(BF).reshape(have, 2, cells, 256)
-        r.dsc[x, pl.ds(y, have)] = slope(pre, sig).astype(BF).reshape(have, 2, cells, 256)
+        r.actc[x, y] = (pre * sig).astype(BF).reshape(2, cells, 256)
+        r.dsc[x, y] = slope(pre, sig).astype(BF).reshape(2, cells, 256)
 
 
 def join_planes(r, first, last):
@@ -699,19 +709,19 @@
 
 def up_forward(r, sizes, scale):
     cells = 8 * sizes[2]
-    gz = lax.axis_index("gz")
-    start, have = near_rows(sizes, 5)
+    gx, gy, gz = position()
 
     def lift(o, _):
-        lift_row(r, sizes, start + o)
-        return 0
-
-    lax.fori_loop(0, have, lift, 0)
-    coarse_forward(r, sizes, *near_rows(sizes, 3))
+        lift_row(r, sizes, coarse_pair(sizes, o))
+        return 0
+
+    lax.fori_loop(0, min(3, sizes[1]), lift, 0)
+    coarse_conv(r, r.al3, r.wc, gx, 3, 2 * gy, 4, cells)
 
     spread = coarse_grow_matrix(cells, gz)
-    for dx, dy, x, y, y2, keep in near_cells(sizes):
-        out = dot_nt(r.wp[...], r.actc[x, y, y2]).astype(BF)
+    for at, (dx, dy, _, _, _, keep) in enumerate(near_cells(sizes)):
+        pre = r.acc[pl.ds(at * cells, cells)]
+        out = dot_nt(r.wp[...], (pre * sigmoid(pre)).astype(BF)).astype(BF)
         r.cos[dx, dy] = dot(out, spread) * keep
 
     join_planes(r, 1, 9)
@@ -792,22 +802,13 @@
 def backward(r, sizes, scale):
     cells = 8 * sizes[2]
     gx, gy, gz = position()
-    start, have = near_rows(sizes, 3)
 
     def coarse(o, _):
-        coarse_grad_row(r, sizes, start + o)
-        return 0
-
-    lax.fori_loop(0, have, coarse, 0)
-    rows = 12 * cells
-    for i in range(3):
-        for j in range(3):
-            block = r.gp3[pl.ds(gx + i, 3), pl.ds(2 * gy + j, 4)].reshape(rows, 768)
-            part = dot(block, r.wct[3 * i + j])
-            if i + j == 0:
-                r.acc[pl.ds(0, rows)] = part
-            else:
-                r.acc[pl.ds(0, rows)] += part
+        coarse_grad_row(r, sizes, coarse_pair(sizes, o))
+        return 0
+
+    lax.fori_loop(0, min(3, sizes[1]), coarse, 0)
+    coarse_conv(r, r.gp3, r.wct, gx, 3, 2 * gy, 4, cells)
 
     spread = coarse_grow_matrix(cells, gz)
     own = lax.broadcasted_iota(jnp.int32, (cells, 256), 0) // 8 == gz
@@ -964,7 +965,7 @@
     fine_forward(r)
 
     def second_wait():
-        zero_rim(r.al3, 1)
+        zero_rim(r.al3, 2)
         zero_rim(r.gp3, 2)
         fetch[2].wait()
 
@@ -979,7 +980,9 @@
     halo_round(sizes, 4, 1, (r.m, r.me, r.mp, r.mer, r.mel, r.msend, r.mrecv), second_wait)
     mid_own(r, sizes)
     sems = (r.ga_send, r.ga_recv, r.gb_send, r.gb_recv)
-    gather_round(sizes, (r.pc, r.pcg, r.pstage) + sems, lambda: mid_halo(r, sizes), nothing)
+    pooled_rest = gather_round(
+        sizes, (r.pc, r.pcg, r.pstage) + sems, lambda: mid_halo(r, sizes), nothing
+    )
     up_forward(r, sizes, scale)
 
     decoded = pltpu.make_async_copy(r.dec, r.dec_out, r.fetched.at[3])
@@ -987,17 +990,14 @@
     def third_wait():
         up_halo(r, scale)
         up_taps(r)
-        decode(r)
-        decoded.start()
-
-    far_start, far_first = near_rows(sizes, 3)
+
+    near = min(3, ny)
 
     def far_row(n, whose):
-        step = 2 if pair else 1
-        return lax.rem(far_start + far_first + step * n + whose, ny)
-
-    def far_count(whose):
-        return (ny - far_first + 1 - whose) // 2 if pair else ny - far_first
+        return coarse_pair(sizes, 2 * n + whose if pair else n)
+
+    def far_count(whose, count=ny):
+        return (count + 1 - whose) // 2 if pair else count
 
     def far_copies(n, whose):
         y = far_row(n, whose)
@@ -1014,16 +1014,16 @@
         ]
 
     def fourth_wait():
-        start, have = near_rows(sizes, 5)
+        pooled_rest()
 
         def lift(o, _):
-            lift_row(r, sizes, lax.rem(start + o, ny))
+            lift_row(r, sizes, coarse_pair(sizes, o))
             return 0
 
-        lax.fori_loop(have, ny, lift, 0)
+        lax.fori_loop(near, ny, lift, 0)
 
         def coarse(n, _):
-            coarse_forward(r, sizes, far_row(n, mine), 1)
+            coarse_forward(r, sizes, far_row(n, mine))
             if pair:
                 for copy in far_copies(n, mine):
                     copy.start()
@@ -1031,8 +1031,15 @@
 
         lax.fori_loop(0, far_count(mine), coarse, 0)
 
+    def arrived(n, _):
+        for copy in far_copies(n, 1 - mine):
+            copy.wait_recv()
+        return 0
+
     sems = (r.ha_send, r.ha_recv, r.hb_send, r.hb_recv)
-    gather_round(sizes, (r.gc, r.gcg, r.gstage) + sems, third_wait, fourth_wait)
+    grads_rest = gather_round(sizes, (r.gc, r.gcg, r.gstage) + sems, third_wait, fourth_wait)
+    if pair:
+        lax.fori_loop(0, far_count(1 - mine, near), arrived, 0)
     backward(r, sizes, scale)
 
     half = 5 if pair else 9
@@ -1066,25 +1073,21 @@
         lax.fori_loop(first, last, taps, 0)
 
     def wait_a():
+        grads_rest()
         if pair:
-
-            def arrived(n, _):
-                for copy in far_copies(n, 1 - mine):
-                    copy.wait_recv()
-                return 0
-
-            lax.fori_loop(0, far_count(1 - mine), arrived, 0)
-        start, have = near_rows(sizes, 3)
+            lax.fori_loop(far_count(1 - mine, near), far_count(1 - mine), arrived, 0)
 
         def coarse(o, _):
-            coarse_grad_row(r, sizes, lax.rem(start + o, ny))
+            coarse_grad_row(r, sizes, coarse_pair(sizes, o))
             return 0
 
-        lax.fori_loop(have, ny, coarse, 0)
+        lax.fori_loop(near, ny, coarse, 0)
         r.cells_t[...] = r.alc[...].reshape(count, 256).T
         do_taps(0, 1)
 
     def wait_b():
+        decode(r)
+        decoded.start()
         do_taps(1, 3)
 
     def wait_c():
@@ -1119,8 +1122,8 @@
 
 def last_kernel(
     gwc_in,
-    red_ref,
-    gwp_ref,
+    red_in,
+    gwp_in,
     wc_out,
     wf_out,
     wd_out,
@@ -1130,6 +1133,7 @@
     rows,
     narrow,
     wide,
+    red_ref,
     load_sem,
     store_sem,
 ):
@@ -1142,12 +1146,17 @@
         pltpu.make_async_copy(wide.at[block], wc_out.at[block], store_sem.at[n])
         for n, block in enumerate(blocks)
     ]
+    loads.append(pltpu.make_async_copy(red_in, red_ref, load_sem.at[9]))
+    loads.append(pltpu.make_async_copy(gwp_in, wp_out, load_sem.at[10]))
     for load in loads:
         load.start()
     for n, block in enumerate(blocks):
         loads[n].wait()
         wide[block] = narrow[block].astype(F32)
         stores[n].start()
+
+    loads[9].wait()
+    loads[10].wait()
 
     def columns(start, blocks, count):
         return jnp.concatenate(
@@ -1168,7 +1177,6 @@
         part = table[32 * i : 32 * i + 32, :144]
         wd_out[pl.ds(9 * i, 9)] = part.T.reshape(9, 16, 32)
     wl_out[...] = columns(432, 2, 32)
-    wp_out[...] = gwp_ref[...]
     for store in stores:
         store.wait()
 
@@ -1235,7 +1243,7 @@
         "wct": (9, 768, 256),
         "wide_lift": (2, LANES, 256),
         "wide_proj": (2, LANES, 256),
-        "al3": (nx + 2, 2 * ny + 2, cells, 768),
+        "al3": (nx + 4, 2 * ny + 4, cells, 768),
         "gp3": (nx + 4, 2 * ny + 4, cells, 768),
         "alc": grid,
         "actc": grid,
@@ -1256,7 +1264,7 @@
         "pre": (8, 8, 16, LANES),
         "pc": (8, LANES),
         "pstage": (nx, cells, LANES),
-        "acc": (max(nx * 2 * min(3, ny), 12) * cells, 256),
+        "acc": (max(nx * 2, 12) * cells, 256),
         "cos": (3, 4, 32, LANES),
         "gj": (6, 5, 32, LANES),
         "gc": (8, LANES),
@@ -1313,13 +1321,14 @@
     gwc, gwf, gwd, gwl, gwp, gwu = pl.pallas_call(
         last_kernel,
         out_shape=[jax.ShapeDtypeStruct(shape, F32) for shape in shapes],
-        in_specs=[HBM, VMEM, VMEM],
+        in_specs=[HBM] * 3,
         out_specs=[HBM] + [VMEM] * 5,
         scratch_shapes=[
             pltpu.VMEM((432, 16), F32),
             pltpu.VMEM((27, 256, 256), BF),
             pltpu.VMEM((27, 256, 256), F32),
-            pltpu.SemaphoreType.DMA((9,)),
+            pltpu.VMEM((512, LANES), F32),
+            pltpu.SemaphoreType.DMA((11,)),
             pltpu.SemaphoreType.DMA((9,)),
         ],
         compiler_params=pltpu.CompilerParams(vmem_limit_bytes=62 * 1024 * 1024),

time: 95.6 us -> 91.8 us (0.960)
  Pallas kernels: 94 us -> 90.2 us
    pallas_call x1, Pallas kernels: 88 us -> 85.2 us  [shards(): pl.pallas_call(functools.partial(step_kernel, sizes, scale, names), out_s...]
where the time goes in v6:
time: 91.8 us; the launch traced here: 91.6 us
  Pallas kernels  90.2 us (98%)
    pallas_call x1, Pallas kernels, shards(): pl.pallas_call(functools.partial(step_kernel, sizes, scale, names), out_s...  85.2 us
    pallas_call x1, Pallas kernels, shards(): pl.pallas_call(last_kernel, out_shape=[jax.ShapeDtypeStruct(shape, F32) f...  5.01 us

profile of v6, /device:TPU:1, one launch (start us, length us, event | category | flops | bytes accessed | tf_op | source)
XLA Modules:
  0.0 91.6 jit_solution(1345366411491801740)
XLA Ops:
  0.6 85.2 %shard_map.135 = (f32[16,32,128]{2,1,0:T(8,128)}, f32[32,256]{1,0:T(8,128)}, bf16[16,8,16,64]{3,2,1,0:T(8,128)(2,1)}, bf16[27,256,256]{2,1,0:T(8,128)(2,1)}) custom-call(bf16[16,16,27]{2,1,0:T(8,128)(2,1)} %bitcast.11, bf16[27,16,32]{2,1,0:T(8,128)(2,1)} %refs_1_.1, bf16[27,16,32]{2,1,0:T(8,128)(2,1)} %bitcast.10, bf16[32,256]{1,0:T(8,128)(2,1)} %refs_3_.1, ...), custom_call_target="tpu_custom_call" | custom-call | tf_op jit(solution)/shard_map/pallas_call | solution.py:1306
  85.8 0.0 copy-start
  85.8 5.0 %shard_map.136 = (f32[27,256,256]{2,1,0:T(8,128)}, f32[16,16,27]{2,1,0:T(8,128)}, f32[27,16,32]{2,1,0:T(8,128)}, f32[32,256]{1,0:T(8,128)}, f32[32,256]{1,0:T(8,128)}, /*index=5*/f32[27,16,32]{2,1,0:T(8,128)}) custom-call(bf16[27,256,256]{2,1,0:T(8,128)(2,1)} %get-tuple-element.18.gwc_in, f32[512,128]{1,0:T(8,128)} %bitcast.9, ...), custom_call_target="tpu_custom_call" | custom-call | tf_op jit(solution)/shard_map/pallas_call | solution.py:1321
  90.8 0.0 copy-done
  90.8 0.8 copy.16
Async XLA Ops:
  85.8 5.0 %copy-start = (bf16[16,8,16,64]{3,2,1,0:T(8,128)(2,1)S(1)}, bf16[16,8,16,64]{3,2,1,0:T(8,128)(2,1)}, u32[]{:S(2)}) copy-start(bf16[16,8,16,64]{3,2,1,0:T(8,128)(2,1)} %get-tuple-element.34) | copy-start | bytes 786436

commit v7 on v6

--- a/solution.py
+++ b/solution.py
@@ -173,10 +173,6 @@
             keep = jnp.where(there, 1.0, 0.0)
             found.append((dx, dy, clamp(x, nx), clamp(y, ny), (dy + 1) % 2, keep))
     return found
-
-
-def nothing():
-    pass
 
 
 NEIGHBOURS = [
@@ -439,14 +435,14 @@
         r.wrows[pl.ds(c, 27, stride=16)] = r.wf_in[c].astype(F32).T
     for i in range(3):
         r.wf[pl.ds(16 * i, 16)] = r.wrows[pl.ds(144 * i, 144)].T.astype(BF)
-        down = [r.wd_in[9 * i + jk].astype(F32) for jk in range(9)]
-        up = [r.wu_in[9 * i + jk].astype(F32).T for jk in range(9)]
-        down_back = [r.wd_in[26 - 9 * i - jk].astype(F32).T for jk in range(9)]
-        up_back = [r.wu_in[26 - 9 * i - jk].astype(F32) for jk in range(9)]
-        fold(r.wd, i, down)
-        fold(r.wu, i, up)
-        fold(r.wdt, i, down_back)
-        fold(r.wut, i, up_back)
+        fold(r.wd, i, [r.wd_in[9 * i + jk].astype(F32) for jk in range(9)])
+
+
+def prepare_later_weights(r):
+    for i in range(3):
+        fold(r.wu, i, [r.wu_in[9 * i + jk].astype(F32).T for jk in range(9)])
+        fold(r.wdt, i, [r.wd_in[26 - 9 * i - jk].astype(F32).T for jk in range(9)])
+        fold(r.wut, i, [r.wu_in[26 - 9 * i - jk].astype(F32) for jk in range(9)])
 
 
 def arrange_volume(r):
@@ -512,7 +508,8 @@
                 r.act[x, 2 * g + b] = act[:, b * LANES : (b + 1) * LANES]
         return 0
 
-    lax.fori_loop(0, 4, convs, 0)
+    for g in range(4):
+        convs(g, 0)
 
     sums = r.sums[...]
     lane = lane_of(32)
@@ -586,7 +583,8 @@
                 r.dsm[x, 2 * g + b] = jnp.where(keep, slope(pre, sig), 0.0).astype(BF)
         return 0
 
-    lax.fori_loop(*groups, convs, 0)
+    for g in range(*groups):
+        convs(g, 0)
 
 
 def mid_own(r, sizes):
@@ -681,7 +679,8 @@
                 r.guo[x, 2 * g + b] = grad.astype(BF)
         return 0
 
-    lax.fori_loop(0, 3, up, 0)
+    for g in range(3):
+        up(g, 0)
 
     def stack(x, _):
         store_taps(r.gu3, x, [r.guo[x, m] for m in range(6)])
@@ -894,7 +893,8 @@
         )
         return 0
 
-    lax.fori_loop(0, 5, taps_fine, 0)
+    for n in range(5):
+        taps_fine(n, 0)
 
     for b in range(2):
         pay_rows(r, 48 * b, r.accf[:, b * LANES : (b + 1) * LANES])
@@ -981,7 +981,10 @@
     mid_own(r, sizes)
     sems = (r.ga_send, r.ga_recv, r.gb_send, r.gb_recv)
     pooled_rest = gather_round(
-        sizes, (r.pc, r.pcg, r.pstage) + sems, lambda: mid_halo(r, sizes), nothing
+        sizes,
+        (r.pc, r.pcg, r.pstage) + sems,
+        lambda: mid_halo(r, sizes),
+        lambda: prepare_later_weights(r),
     )
     up_forward(r, sizes, scale)
 
@@ -992,6 +995,7 @@
         up_taps(r)
 
     near = min(3, ny)
+    soon = max(near, ny - 2)
 
     def far_row(n, whose):
         return coarse_pair(sizes, 2 * n + whose if pair else n)
@@ -1022,14 +1026,14 @@
 
         lax.fori_loop(near, ny, lift, 0)
 
-        def coarse(n, _):
-            coarse_forward(r, sizes, far_row(n, mine))
-            if pair:
-                for copy in far_copies(n, mine):
-                    copy.start()
-            return 0
-
-        lax.fori_loop(0, far_count(mine), coarse, 0)
+        lax.fori_loop(0, far_count(mine, soon), coarse_share, 0)
+
+    def coarse_share(n, _):
+        coarse_forward(r, sizes, far_row(n, mine))
+        if pair:
+            for copy in far_copies(n, mine):
+                copy.start()
+        return 0
 
     def arrived(n, _):
         for copy in far_copies(n, 1 - mine):
@@ -1072,26 +1076,31 @@
 
         lax.fori_loop(first, last, taps, 0)
 
-    def wait_a():
-        grads_rest()
+    def coarse_grads(first, last):
         if pair:
-            lax.fori_loop(far_count(1 - mine, near), far_count(1 - mine), arrived, 0)
+            lax.fori_loop(far_count(1 - mine, first), far_count(1 - mine, last), arrived, 0)
 
         def coarse(o, _):
             coarse_grad_row(r, sizes, coarse_pair(sizes, o))
             return 0
 
-        lax.fori_loop(near, ny, coarse, 0)
+        lax.fori_loop(first, last, coarse, 0)
+
+    def wait_a():
+        lax.fori_loop(far_count(mine, soon), far_count(mine), coarse_share, 0)
+        grads_rest()
+        coarse_grads(near, soon)
         r.cells_t[...] = r.alc[...].reshape(count, 256).T
+        coarse_grads(soon, ny)
         do_taps(0, 1)
 
     def wait_b():
+        do_taps(1, 4)
+
+    def wait_c():
+        do_taps(4, taps_count(mine))
         decode(r)
         decoded.start()
-        do_taps(1, 3)
-
-    def wait_c():
-        do_taps(3, taps_count(mine))
         proj_grad(r, sizes)
 
     sems = (r.ra_send, r.ra_recv, r.rb_send, r.rb_recv, r.rc_send, r.rc_recv)

time: 91.8 us -> 91.4 us (level)
  no operation moved by 1% of the time
where the time goes in v7:
time: 91.4 us; the launch traced here: 91.3 us
  Pallas kernels  89.8 us (98%)
    pallas_call x1, Pallas kernels, shards(): pl.pallas_call(functools.partial(step_kernel, sizes, scale, names), out_s...  84.8 us
    pallas_call x1, Pallas kernels, shards(): pl.pallas_call(last_kernel, out_shape=[jax.ShapeDtypeStruct(shape, F32) f...  5.01 us

profile of v7, /device:TPU:1, one launch (start us, length us, event | category | flops | bytes accessed | tf_op | source)
XLA Modules:
  0.0 91.3 jit_solution(10846503648102145446)
XLA Ops:
  0.6 84.8 %shard_map.135 = (f32[16,32,128]{2,1,0:T(8,128)}, f32[32,256]{1,0:T(8,128)}, bf16[16,8,16,64]{3,2,1,0:T(8,128)(2,1)}, bf16[27,256,256]{2,1,0:T(8,128)(2,1)}) custom-call(bf16[16,16,27]{2,1,0:T(8,128)(2,1)} %bitcast.11, bf16[27,16,32]{2,1,0:T(8,128)(2,1)} %refs_1_.1, bf16[27,16,32]{2,1,0:T(8,128)(2,1)} %bitcast.10, bf16[32,256]{1,0:T(8,128)(2,1)} %refs_3_.1, ...), custom_call_target="tpu_custom_call" | custom-call | tf_op jit(solution)/shard_map/pallas_call | solution.py:1315
  85.4 0.0 copy-start
  85.5 5.0 %shard_map.136 = (f32[27,256,256]{2,1,0:T(8,128)}, f32[16,16,27]{2,1,0:T(8,128)}, f32[27,16,32]{2,1,0:T(8,128)}, f32[32,256]{1,0:T(8,128)}, f32[32,256]{1,0:T(8,128)}, /*index=5*/f32[27,16,32]{2,1,0:T(8,128)}) custom-call(bf16[27,256,256]{2,1,0:T(8,128)(2,1)} %get-tuple-element.18.gwc_in, f32[512,128]{1,0:T(8,128)} %bitcast.9, ...), custom_call_target="tpu_custom_call" | custom-call | tf_op jit(solution)/shard_map/pallas_call | solution.py:1330
  90.5 0.0 copy-done
  90.5 0.8 copy.16
Async XLA Ops:
  85.4 5.0 %copy-start = (bf16[16,8,16,64]{3,2,1,0:T(8,128)(2,1)S(1)}, bf16[16,8,16,64]{3,2,1,0:T(8,128)(2,1)}, u32[]{:S(2)}) copy-start(bf16[16,8,16,64]{3,2,1,0:T(8,128)(2,1)} %get-tuple-element.34) | copy-start | bytes 786436
